TPU v7x, 512 devices: a whole 4x8x8 slice. The times are simulated.
512 devices in a mesh: dp: 16 (over y_lo, z), mp: 32 (over y_hi, x, core).
Axes of the slice: x: 4, y: 8 (y_hi: 4, y_lo: 2; y = y_hi * 2 + y_lo), z: 8, core: 2. Of those that a mesh axis runs over, the one named last changes fastest.
Arguments:
- inputs: bfloat16 [5120, 3072], P('dp'), may hold values from -64 to 64
- ln_gain: float32 [3072], replicated, may hold values from 0.5 to 2
- w_qkv: bfloat16 [3072, 12288], P('dp', 'mp'), may hold values from -0.109375 to 0.109375
- q_gain: float32 [128], replicated, may hold values from 0.5 to 2
- k_gain: float32 [128], replicated, may hold values from 0.5 to 2
- cotangent: bfloat16 [5120, 4096], P('dp', 'mp'), may hold values from -6 to 6
Outputs:
- grad_input: bfloat16 [5120, 3072], P('dp')
- grad_w_qkv: float32 [3072, 12288], P('dp', 'mp')
All inputs are finite; a program needn't handle non-finite values.
Results may differ from a plain program's by a relative error of at most 0.033.
Values may be sent and summed in bfloat16 or wider, within the bound.
No kernel may reach another device: no remote copies, remote signals or barrier semaphores. Data moves between devices by JAX's collectives and lax.ppermute only.
A program may use at most 64 MiB of HBM per device.

v0:
```python
import math

import jax
import jax.numpy as jnp
from jax import lax
from jax.sharding import PartitionSpec as P

EPSILON = 1e-06


def normalize(values):
    centred = values - jnp.mean(values, axis=-1, keepdims=True)
    inverse = lax.rsqrt(jnp.mean(centred * centred, axis=-1, keepdims=True) + EPSILON)
    return (centred * inverse, inverse)


def norm_backward(grad_unit, unit_vals, inverse):
    first_mean = jnp.mean(grad_unit, axis=-1, keepdims=True)
    second_mean = jnp.mean(grad_unit * unit_vals, axis=-1, keepdims=True)
    return inverse * (grad_unit - first_mean - unit_vals * second_mean)


def contract(left_op, right_op, left_dim, right_dim):
    return lax.dot_general(
        left_op,
        right_op,
        (((left_dim,), (right_dim,)), ((), ())),
        preferred_element_type=jnp.float32,
    )


def head_grads(qkv_head, cot_head, q_gain, k_gain):
    head_width = cot_head.shape[1]
    factor = 1.0 / math.sqrt(head_width)
    q_unit, q_inverse = normalize(qkv_head[:, :head_width].astype(jnp.float32))
    k_unit, k_inverse = normalize(qkv_head[:, head_width : 2 * head_width].astype(jnp.float32))
    values = qkv_head[:, 2 * head_width :]
    q_normed = (q_unit * q_gain).astype(jnp.bfloat16)
    k_normed = (k_unit * k_gain).astype(jnp.bfloat16)
    scores = contract(q_normed, k_normed, 1, 1) * factor
    exp_scores = jnp.exp(scores)
    attn_weights = exp_scores / jnp.sum(exp_scores, axis=-1, keepdims=True)
    grad_attn = contract(cot_head, values, 1, 1)
    centre = jnp.sum(attn_weights * grad_attn, axis=-1, keepdims=True)
    grad_scores = (attn_weights * (grad_attn - centre)).astype(jnp.bfloat16)
    grad_values = contract(attn_weights.astype(jnp.bfloat16), cot_head, 0, 0)
    grad_query = norm_backward(
        contract(grad_scores, k_normed, 1, 0) * factor * q_gain, q_unit, q_inverse
    )
    grad_key = norm_backward(
        contract(grad_scores, q_normed, 0, 0) * factor * k_gain, k_unit, k_inverse
    )
    return jnp.concatenate([grad_query, grad_key, grad_values], axis=1).astype(jnp.bfloat16)


def per_device(inputs, ln_gain, w_qkv, q_gain, k_gain, cotangent):
    x_unit, x_inverse = normalize(inputs.astype(jnp.float32))
    normed = (x_unit * ln_gain).astype(jnp.bfloat16)
    weights = lax.all_gather(w_qkv, "dp", axis=0, tiled=True)
    qkv_local = jnp.dot(normed, weights, preferred_element_type=jnp.float32).astype(jnp.bfloat16)
    grad_qkv = head_grads(qkv_local, cotangent, q_gain, k_gain)
    head_term = contract(grad_qkv, weights, 1, 1)
    grad_normed = lax.psum(head_term.astype(jnp.bfloat16), "mp").astype(jnp.float32)
    grad_input = norm_backward(grad_normed * ln_gain, x_unit, x_inverse).astype(jnp.bfloat16)
    grad_w_qkv = lax.psum_scatter(
        contract(normed, grad_qkv, 0, 0).astype(jnp.bfloat16), "dp", scatter_dimension=0, tiled=True
    ).astype(jnp.float32)
    return (grad_input, grad_w_qkv)


def solution(mesh):
    placed = (P("dp", None), P(), P("dp", "mp"), P(), P(), P("dp", "mp"))
    return jax.shard_map(
        per_device,
        mesh=mesh,
        in_specs=placed,
        out_specs=(P("dp", None), P("dp", "mp")),
        check_vma=False,
    )
```

profile of v0, /device:TPU:6, one launch (start us, length us, event | category | flops | bytes accessed | tf_op | source)
XLA Modules:
  0.0 479.5 jit_solution(2127800866732190663)
XLA Ops:
  7.2 0.0 copy-start
  7.2 0.0 copy-start.1
  7.2 0.0 copy-start.3
  7.2 0.0 all-gather.2.cloned.1.call-start
  7.2 0.7 all-gather.2.cloned.1.call-update
  7.9 0.0 all-reduce.2.cloned.1.call-start
  8.0 1.9 convert_reduce_fusion
  9.9 0.7 broadcast_multiply_fusion.10
  10.5 0.7 broadcast_multiply_fusion.9
  11.2 0.0 copy-done.1
  11.2 0.7 fusion.10
  11.9 0.0 copy-start.5
  11.9 0.0 copy-start.6
  11.9 78.2 %all-gather.2.cloned.1.call-done = bf16[3072,384]{1,0:T(8,128)(2,1)} async-done(((bf16[192,384]{1,0:T(8,128)(2,1)}), bf16[3072,384]{1,0:T(8,128)(2,1)}) %all-gather.2.cloned.1.call-update) | async-done | bytes 2359312 | tf_op jit(solution)/shard_map/all_gather | solution.py:59
  90.1 0.0 copy-done.3
  90.1 2.9 convolution_convert_fusion.2
  93.0 0.1 convert_reduce_fusion.1
  93.2 0.3 fusion.29
  93.5 0.0 copy-done.5
  93.5 0.0 copy-done.6
  93.5 0.4 fusion.45
  93.9 0.0 copy-done
  93.9 0.2 convolution_convert_fusion.3
  94.2 0.0 copy-start.4
  94.2 0.2 multiply_reduce_fusion
  94.4 0.1 multiply_convert_fusion
  94.5 0.3 convolution_multiply_fusion.1
  94.8 0.8 fusion.31
  95.7 0.4 fusion.34
  96.1 0.0 copy-done.4
  96.1 2.5 convolution_convert_fusion.1
  98.6 0.0 all-reduce.2.cloned.1.call-update
  98.7 0.0 reduce-scatter.2.cloned.1.call-start
  98.7 3.3 convolution_convert_fusion
  102.0 0.0 reduce-scatter.2.cloned.1.call-update
  102.0 276.7 %all-reduce.2.cloned.1.call-done = bf16[320,3072]{1,0:T(8,128)(2,1)} async-done(((bf16[320,3072]{1,0:T(8,128)(2,1)}), bf16[320,3072]{1,0:T(8,128)(2,1)}) %all-reduce.2.cloned.1.call-update) | async-done | bytes 1966096 | tf_op jit(solution)/shard_map/psum | solution.py:63
  378.8 0.0 copy-start.2
  378.8 2.8 fusion.11
  381.6 0.0 copy-done.2
  381.6 3.0 fusion.9
  384.7 86.7 %reduce-scatter.2.cloned.1.call-done = bf16[192,384]{1,0:T(8,128)(2,1)} async-done(((bf16[3072,384]{1,0:T(8,128)(2,1)}), bf16[192,384]{1,0:T(8,128)(2,1)}) %reduce-scatter.2.cloned.1.call-update) | async-done | bytes 147472 | tf_op jit(solution)/shard_map/reduce_scatter | solution.py:65
  471.4 1.6 convert_element_type.56
  (11 shorter events, 0.0 us)
Async XLA Ops:
  7.2 86.8 %copy-start = (bf16[320,128]{1,0:T(8,128)(2,1)S(1)}, bf16[320,128]{1,0:T(8,128)(2,1)}, u32[]{:S(2)}) copy-start(bf16[320,128]{1,0:T(8,128)(2,1)} %param.11) | copy-start | bytes 245764
  7.2 4.0 copy-start.1
  7.2 82.9 %copy-start.3 = (f32[3072]{0:T(1024)S(1)}, f32[3072]{0:T(1024)}, u32[]{:S(2)}) copy-start(f32[3072]{0:T(1024)} %param.7) | copy-start | bytes 36868
  7.2 82.9 %all-gather.2.cloned.1.call-start = ((), (), s32[]{:S(2)}) async-start(), calls=%async_computation.1 | async-start | bytes 2506752 | tf_op jit(solution)/shard_map/all_gather | solution.py:59
  7.9 370.8 %all-reduce.2.cloned.1.call-start = ((), (), s32[]{:S(2)}) async-start(), calls=%async_computation.2 | async-start | bytes 3932160 | tf_op jit(solution)/shard_map/psum | solution.py:63
  11.9 81.6 %copy-start.5 = (f32[128]{0:T(128)S(1)}, f32[128]{0:T(128)}, u32[]{:S(2)}) copy-start(f32[128]{0:T(128)} %param.9) | copy-start | bytes 1540
  11.9 81.6 %copy-start.6 = (f32[128]{0:T(128)S(1)}, f32[128]{0:T(128)}, u32[]{:S(2)}) copy-start(f32[128]{0:T(128)} %param.10) | copy-start | bytes 1540
  94.2 2.0 copy-start.4
  98.7 372.7 %reduce-scatter.2.cloned.1.call-start = ((), (), s32[]{:S(2)}) async-start(), calls=%async_computation.3 | async-start | bytes 2506752 | tf_op jit(solution)/shard_map/reduce_scatter | solution.py:65
  378.8 2.8 copy-start.2
Sparse Core Ops, SparseCore 0:
  10.1 79.9 all-gather.1
  98.8 279.9 all-reduce.1
  381.9 89.4 reduce-scatter.1
where the time goes:
time: 480 us
  waiting for transfers between devices  442 us (92%)
  between operations  13.9 us (3%)
  other arithmetic  12.4 us (3%)
  matrix products  10.7 us (2%)
    psum x1, waiting for transfers between devices, per_device(): lax.psum(head_term.astype(jnp.bfloat16), 'mp').astype(jnp.float32)  277 us
    reduce_scatter x1, waiting for transfers between devices, per_device(): lax.psum_scatter(contract(normed, grad_qkv, 0, 0).astype(jnp.bfloat16), '...  86.7 us
    all_gather x1, waiting for transfers between devices, per_device(): weights = lax.all_gather(w_qkv, 'dp', axis=0, tiled=True)  78.2 us
  transfers between devices with their start and end apart: 3, of which 3 were waited for; matrix products, arithmetic and copies ran while one was open for 3% of the time, Pallas kernels for 0%

commit v1 on v0

--- a/solution.py
+++ b/solution.py
@@ -53,18 +53,87 @@
     return jnp.concatenate([grad_query, grad_key, grad_values], axis=1).astype(jnp.bfloat16)
 
 
+Y_LO, Z = 2, 8
+Y_HI, X, CORE = 4, 4, 2
+
+
+def partner_rows():
+    return [(y * Z + z, (1 - y) * Z + z) for y in range(Y_LO) for z in range(Z)]
+
+
+def z_groups():
+    return [[y * Z + z for z in range(Z)] for y in range(Y_LO)]
+
+
+def shifted(step_y, step_x, step_core):
+    pairs = []
+    for y in range(Y_HI):
+        for x in range(X):
+            for core in range(CORE):
+                source = (y * X + x) * CORE + core
+                target = ((y + step_y) % Y_HI * X + (x + step_x) % X) * CORE + (core + step_core) % CORE
+                pairs.append((source, target))
+    return pairs
+
+
+def take(values, at, rows):
+    return lax.dynamic_slice_in_dim(values, at * rows, rows, 0)
+
+
+def scatter_sum(values, at, parts, perm_of):
+    rows = values.shape[0] // parts
+    sent = [
+        lax.ppermute(take(values, (at + step) % parts, rows), "mp", perm_of(step))
+        for step in range(1, parts)
+    ]
+    total = take(values, at, rows).astype(jnp.float32)
+    for term in sent:
+        total = total + term.astype(jnp.float32)
+    return total
+
+
+def gather_rows(values, at, parts, perm_of):
+    rows = values.shape[0]
+    whole = jnp.zeros((parts * rows, values.shape[1]), values.dtype)
+    whole = lax.dynamic_update_slice_in_dim(whole, values, at * rows, 0)
+    for step in range(1, parts):
+        got = lax.ppermute(values, "mp", perm_of(step))
+        whole = lax.dynamic_update_slice_in_dim(whole, got, (at - step) % parts * rows, 0)
+    return whole
+
+
 def per_device(inputs, ln_gain, w_qkv, q_gain, k_gain, cotangent):
+    dp_at = lax.axis_index("dp")
+    mp_at = lax.axis_index("mp")
+    y_lo = dp_at // Z
+    core, x_at, y_hi = mp_at % CORE, mp_at // CORE % X, mp_at // (CORE * X)
     x_unit, x_inverse = normalize(inputs.astype(jnp.float32))
     normed = (x_unit * ln_gain).astype(jnp.bfloat16)
-    weights = lax.all_gather(w_qkv, "dp", axis=0, tiled=True)
+    other = lax.ppermute(w_qkv, "dp", partner_rows())
+    pair = jnp.where(y_lo == 0, jnp.stack([w_qkv, other]), jnp.stack([other, w_qkv]))
+    weights = lax.all_gather(pair, "dp", axis_index_groups=z_groups())
+    weights = jnp.transpose(weights, (1, 0, 2, 3)).reshape(inputs.shape[1], w_qkv.shape[1])
     qkv_local = jnp.dot(normed, weights, preferred_element_type=jnp.float32).astype(jnp.bfloat16)
     grad_qkv = head_grads(qkv_local, cotangent, q_gain, k_gain)
-    head_term = contract(grad_qkv, weights, 1, 1)
-    grad_normed = lax.psum(head_term.astype(jnp.bfloat16), "mp").astype(jnp.float32)
-    grad_input = norm_backward(grad_normed * ln_gain, x_unit, x_inverse).astype(jnp.bfloat16)
     grad_w_qkv = lax.psum_scatter(
         contract(normed, grad_qkv, 0, 0).astype(jnp.bfloat16), "dp", scatter_dimension=0, tiled=True
     ).astype(jnp.float32)
+    by_core = lambda step: shifted(0, 0, step)
+    by_x = lambda step: shifted(0, step, 0)
+    by_y = lambda step: shifted(step, 0, 0)
+    head_term = contract(grad_qkv, weights, 1, 1).astype(jnp.bfloat16)
+    part = scatter_sum(head_term, core, CORE, by_core).astype(jnp.bfloat16)
+    part = scatter_sum(part, x_at, X, by_x).astype(jnp.bfloat16)
+    grad_normed = scatter_sum(part, y_hi, Y_HI, by_y)
+    rows = grad_normed.shape[0]
+    first = ((core * X + x_at) * Y_HI + y_hi) * rows
+    own_unit, own_inverse = normalize(
+        lax.dynamic_slice_in_dim(inputs, first, rows, 0).astype(jnp.float32)
+    )
+    own = norm_backward(grad_normed * ln_gain, own_unit, own_inverse).astype(jnp.bfloat16)
+    own = gather_rows(own, y_hi, Y_HI, by_y)
+    own = gather_rows(own, x_at, X, by_x)
+    grad_input = gather_rows(own, core, CORE, by_core)
     return (grad_input, grad_w_qkv)
 
 

time: 480 us -> 191 us (0.40)
  the two profiles are of different devices: /device:TPU:6 before, /device:TPU:58 now
where the time goes in v1:
time: 191 us; the launch traced here: 190 us
  waiting for transfers between devices  96 us (50%)
  starting transfers between devices  49.3 us (26%)
  between operations  14.9 us (8%)
  other arithmetic  10.8 us (6%)
  matrix products  10.4 us (5%)
  local copies, waits for them, and re-layouts  8.81 us (5%)
    all_gather x1, waiting for transfers between devices, per_device(): weights = lax.all_gather(pair, 'dp', axis_index_groups=z_groups())  46.6 us
    ppermute x7, starting transfers between devices, scatter_sum(): lax.ppermute(take(values, (at + step) % parts, rows), 'mp', perm_of(step))  24.2 us
    ppermute x7, starting transfers between devices, gather_rows(): got = lax.ppermute(values, 'mp', perm_of(step))  21.6 us
    ppermute x7, waiting for transfers between devices, scatter_sum(): lax.ppermute(take(values, (at + step) % parts, rows), 'mp', perm_of(step))  18.3 us
    ppermute x7, waiting for transfers between devices, gather_rows(): got = lax.ppermute(values, 'mp', perm_of(step))  18.1 us
    reduce_scatter x1, waiting for transfers between devices, per_device(): lax.psum_scatter(contract(normed, grad_qkv, 0, 0).astype(jnp.bfloat16), '...  8.6 us
    dot_general x7, matrix products, contract(): lax.dot_general(left_op, right_op, (((left_dim,), (right_dim,)), ((), ())...  7.52 us
    ppermute x1, waiting for transfers between devices, per_device(): other = lax.ppermute(w_qkv, 'dp', partner_rows())  4.41 us
  transfers between devices with their start and end apart: 17, of which 13 were waited for; matrix products, arithmetic and copies ran while one was open for 8% of the time, Pallas kernels for 0%

profile of v1, /device:TPU:58, one launch (start us, length us, event | category | flops | bytes accessed | tf_op | source)
XLA Modules:
  0.0 190.2 jit_solution(3001139408432722359)
XLA Ops:
  7.2 0.0 all-gather.2.cloned.1.call-start
  7.3 3.4 %collective-permute-start = (bf16[192,384]{1,0:T(8,128)(2,1)}, bf16[192,384]{1,0:T(8,128)(2,1)S(1)}, u32[]{:S(2)}, u32[]{:S(2)}) collective-permute-start(bf16[192,384]{1,0:T(8,128)(2,1)} %param.8), channel_id=1, source_target_pairs={{0,256},{32,288},{64,320},{96,352},{128,384},{160,416},{192,448},{... | collective-permute-start | bytes 442376 | tf_op jit(solution)/shard_map/ppermute | solution.py:112
  10.7 4.4 %collective-permute-done = bf16[192,384]{1,0:T(8,128)(2,1)S(1)} collective-permute-done((bf16[192,384]{1,0:T(8,128)(2,1)}, bf16[192,384]{1,0:T(8,128)(2,1)S(1)}, u32[]{:S(2)}, u32[]{:S(2)}) %collective-permute-start) | collective-permute-done | bytes 147488 | tf_op jit(solution)/shard_map/ppermute | solution.py:112
  15.1 1.8 maximum_select_fusion
  16.9 0.0 reduce-scatter.2.cloned.1.call-start
  16.9 1.9 %convert_reduce_fusion = f32[320]{0:T(512)S(1)} fusion(bf16[320,3072]{1,0:T(8,128)(2,1)} %param.6), kind=kLoop, calls=%fused_computation.1 | loop fusion | flops 1965760 | bytes 1967360 | tf_op jit(solution)/shard_map/reduce_sum | solution.py:12
  18.9 0.7 fusion.2
  19.6 46.6 %all-gather.2.cloned.1.call-done = bf16[8,2,192,384]{3,2,0,1:T(8,128)(2,1)} async-done(((bf16[1,2,192,384]{3,2,0,1:T(8,128)(2,1)}), bf16[8,2,192,384]{3,2,0,1:T(8,128)(2,1)}) %all-gather.2.cloned.1.call-update) | async-done | bytes 2359312 | tf_op jit(solution)/shard_map/all_gather | solution.py:114
  66.1 2.9 %convolution_convert_fusion.2 = bf16[320,384]{1,0:T(8,128)(2,1)S(1)} fusion(bf16[3072,384]{1,0:T(8,128)(2,1)} %bitcast.15, bf16[320,3072]{1,0:T(8,128)(2,1)S(1)} %copy-done.1, f32[3072]{0:T(1024)S(1)} %copy-done.5, f32[320]{0:T(512)S(1)} %add_rsqrt_fusion.2, f32[320]{0:T(512)S(1)} %broadcast_multiply_fusion.6), kind=kOutput, calls=%fused_computation.13 | convolution fusion | flops 760012800 | bytes 4585984 | tf_op jit(solution)/shard_map/dot_general | solution.py:116
  69.1 0.1 convert_reduce_fusion.2
  69.2 0.3 fusion.31
  69.5 0.4 fusion.48
  69.9 0.3 multiply_reduce_fusion
  70.2 0.2 convolution_convert_fusion.3
  70.4 0.1 multiply_convert_fusion
  70.5 0.3 convolution_multiply_fusion.1
  70.9 0.8 fusion.33
  71.7 0.4 fusion.36
  72.2 1.2 convolution_convert_fusion.1
  73.4 1.3 copy-done.2
  74.7 0.1 constant_dynamic-slice_fusion.6
  74.8 1.9 %collective-permute-start.1 = (bf16[160,3072]{1,0:T(8,128)(2,1)S(1)}, bf16[160,3072]{1,0:T(8,128)(2,1)}, u32[]{:S(2)}, u32[]{:S(2)}) collective-permute-start(bf16[160,3072]{1,0:T(8,128)(2,1)S(1)} %constant_dynamic-slice_fusion.6), channel_id=1, source_target_pairs={{0,1},{1,0},{2,3},{3,2},{4,5},{5,4},{6,7},{7,6},{8,9},{9,8},{10,11... | collective-permute-start | bytes 2949128 | tf_op jit(solution)/shard_map/ppermute | solution.py:86
  76.9 0.2 convert_reduce_fusion.1
  77.1 0.2 fusion.15
  77.3 2.1 %collective-permute-done.1 = bf16[160,3072]{1,0:T(8,128)(2,1)} collective-permute-done((bf16[160,3072]{1,0:T(8,128)(2,1)S(1)}, bf16[160,3072]{1,0:T(8,128)(2,1)}, u32[]{:S(2)}, u32[]{:S(2)}) %collective-permute-start.1) | collective-permute-done | bytes 983072 | tf_op jit(solution)/shard_map/ppermute | solution.py:86
  79.4 1.8 add_convert_fusion
  81.2 0.8 constant_dynamic-slice_fusion.5
  81.9 3.4 %collective-permute-start.2 = (bf16[40,3072]{1,0:T(8,128)(2,1)}, bf16[40,3072]{1,0:T(8,128)(2,1)}, u32[]{:S(2)}, u32[]{:S(2)}) collective-permute-start(bf16[40,3072]{1,0:T(8,128)(2,1)} %get-tuple-element.13), channel_id=1, source_target_pairs={{0,2},{1,3},{2,4},{3,5},{4,6},{5,7},{6,0},{7,1},{8,10},{9,11},{10,... | collective-permute-start | bytes 737288 | tf_op jit(solution)/shard_map/ppermute | solution.py:86
  85.3 3.1 %collective-permute-start.3 = (bf16[40,3072]{1,0:T(8,128)(2,1)S(1)}, bf16[40,3072]{1,0:T(8,128)(2,1)}, u32[]{:S(2)}, u32[]{:S(2)}) collective-permute-start(bf16[40,3072]{1,0:T(8,128)(2,1)S(1)} %get-tuple-element.15), channel_id=1, source_target_pairs={{0,4},{1,5},{2,6},{3,7},{4,0},{5,1},{6,2},{7,3},{8,12},{9,13},{10,... | collective-permute-start | bytes 737288 | tf_op jit(solution)/shard_map/ppermute | solution.py:86
  88.4 4.0 %collective-permute-start.4 = (bf16[40,3072]{1,0:T(8,128)(2,1)S(1)}, bf16[40,3072]{1,0:T(8,128)(2,1)}, u32[]{:S(2)}, u32[]{:S(2)}) collective-permute-start(bf16[40,3072]{1,0:T(8,128)(2,1)S(1)} %get-tuple-element.14), channel_id=1, source_target_pairs={{0,6},{1,7},{2,0},{3,1},{4,2},{5,3},{6,4},{7,5},{8,14},{9,15},{10,... | collective-permute-start | bytes 737288 | tf_op jit(solution)/shard_map/ppermute | solution.py:86
  92.4 4.3 %convolution_convert_fusion = bf16[3072,384]{1,0:T(8,128)(2,1)} fusion(bf16[320,128]{1,0:T(8,128)(2,1)} %copy-done.9, bf16[320,128]{1,0:T(8,128)(2,1)} %copy-done.4, bf16[320,128]{1,0:T(8,128)(2,1)} %copy-done.3, bf16[320,3072]{1,0:T(8,128)(2,1)S(1)} %copy-done.1, f32[3072]{0:T(1024)S(1)} %copy-done.5, f32[320]{0:T(512)S(1)} %add_rsqrt_fusion.2, ...), kind=kOutput, calls=%fused_computation.4 | convolution fusion | flops 761806848 | bytes 4585984 | tf_op jit(solution)/shard_map/dot_general | solution.py:24
  96.7 1.0 collective-permute-done.3
  97.7 4.1 %collective-permute-done.4 = bf16[40,3072]{1,0:T(8,128)(2,1)} collective-permute-done((bf16[40,3072]{1,0:T(8,128)(2,1)S(1)}, bf16[40,3072]{1,0:T(8,128)(2,1)}, u32[]{:S(2)}, u32[]{:S(2)}) %collective-permute-start.4) | collective-permute-done | bytes 245792 | tf_op jit(solution)/shard_map/ppermute | solution.py:86
  101.8 1.3 add_convert_fusion.1
  103.1 0.1 constant_dynamic-slice_fusion.2
  103.2 3.2 %collective-permute-start.5 = (bf16[10,3072]{1,0:T(8,128)(2,1)S(1)}, bf16[10,3072]{1,0:T(8,128)(2,1)S(1)}, u32[]{:S(2)}, u32[]{:S(2)}) collective-permute-start(bf16[10,3072]{1,0:T(8,128)(2,1)S(1)} %get-tuple-element.16), channel_id=1, source_target_pairs={{0,8},{1,9},{2,10},{3,11},{4,12},{5,13},{6,14},{7,15},{8,16},{9,17... | collective-permute-start | bytes 184328 | tf_op jit(solution)/shard_map/ppermute | solution.py:86
  106.4 6.5 %collective-permute-start.6 = (bf16[10,3072]{1,0:T(8,128)(2,1)S(1)}, bf16[10,3072]{1,0:T(8,128)(2,1)S(1)}, u32[]{:S(2)}, u32[]{:S(2)}) collective-permute-start(bf16[10,3072]{1,0:T(8,128)(2,1)S(1)} %get-tuple-element.18), channel_id=1, source_target_pairs={{0,16},{1,17},{2,18},{3,19},{4,20},{5,21},{6,22},{7,23},{8,24},{9,... | collective-permute-start | bytes 184328 | tf_op jit(solution)/shard_map/ppermute | solution.py:86
  112.9 2.1 %collective-permute-start.7 = (bf16[10,3072]{1,0:T(8,128)(2,1)S(1)}, bf16[10,3072]{1,0:T(8,128)(2,1)S(1)}, u32[]{:S(2)}, u32[]{:S(2)}) collective-permute-start(bf16[10,3072]{1,0:T(8,128)(2,1)S(1)} %get-tuple-element.17), channel_id=1, source_target_pairs={{0,24},{1,25},{2,26},{3,27},{4,28},{5,29},{6,30},{7,31},{8,0},{9,1... | collective-permute-start | bytes 184328 | tf_op jit(solution)/shard_map/ppermute | solution.py:86
  115.1 5.3 %collective-permute-done.6 = bf16[10,3072]{1,0:T(8,128)(2,1)S(1)} collective-permute-done((bf16[10,3072]{1,0:T(8,128)(2,1)S(1)}, bf16[10,3072]{1,0:T(8,128)(2,1)S(1)}, u32[]{:S(2)}, u32[]{:S(2)}) %collective-permute-start.6) | collective-permute-done | bytes 61472 | tf_op jit(solution)/shard_map/ppermute | solution.py:86
  120.4 5.8 %collective-permute-done.7 = bf16[10,3072]{1,0:T(8,128)(2,1)S(1)} collective-permute-done((bf16[10,3072]{1,0:T(8,128)(2,1)S(1)}, bf16[10,3072]{1,0:T(8,128)(2,1)S(1)}, u32[]{:S(2)}, u32[]{:S(2)}) %collective-permute-start.7) | collective-permute-done | bytes 61472 | tf_op jit(solution)/shard_map/ppermute | solution.py:86
  126.1 0.2 fusion.47
  126.4 0.1 fusion.14
  126.5 1.9 %collective-permute-start.8 = (bf16[10,3072]{1,0:T(8,128)(2,1)S(1)}, bf16[10,3072]{1,0:T(8,128)(2,1)S(1)}, u32[]{:S(2)}, u32[]{:S(2)}) collective-permute-start(bf16[10,3072]{1,0:T(8,128)(2,1)S(1)} %fusion.14), channel_id=1, source_target_pairs={{0,8},{1,9},{2,10},{3,11},{4,12},{5,13},{6,14},{7,15},{8,16},{9,17... | collective-permute-start | bytes 184328 | tf_op jit(solution)/shard_map/ppermute | solution.py:100
  128.4 7.1 %collective-permute-start.9 = (bf16[10,3072]{1,0:T(8,128)(2,1)S(1)}, bf16[10,3072]{1,0:T(8,128)(2,1)S(1)}, u32[]{:S(2)}, u32[]{:S(2)}) collective-permute-start(bf16[10,3072]{1,0:T(8,128)(2,1)S(1)} %fusion.14), channel_id=1, source_target_pairs={{0,16},{1,17},{2,18},{3,19},{4,20},{5,21},{6,22},{7,23},{8,24},{9,... | collective-permute-start | bytes 184328 | tf_op jit(solution)/shard_map/ppermute | solution.py:100
  135.5 1.9 %collective-permute-start.10 = (bf16[10,3072]{1,0:T(8,128)(2,1)S(1)}, bf16[10,3072]{1,0:T(8,128)(2,1)S(1)}, u32[]{:S(2)}, u32[]{:S(2)}) collective-permute-start(bf16[10,3072]{1,0:T(8,128)(2,1)S(1)} %fusion.14), channel_id=1, source_target_pairs={{0,24},{1,25},{2,26},{3,27},{4,28},{5,29},{6,30},{7,31},{8,0},{9,1... | collective-permute-start | bytes 184328 | tf_op jit(solution)/shard_map/ppermute | solution.py:100
  137.6 0.6 dynamic_update_slice.30
  138.2 0.7 dynamic_update_slice.31
  138.9 7.0 %collective-permute-done.9 = bf16[10,3072]{1,0:T(8,128)(2,1)S(1)} collective-permute-done((bf16[10,3072]{1,0:T(8,128)(2,1)S(1)}, bf16[10,3072]{1,0:T(8,128)(2,1)S(1)}, u32[]{:S(2)}, u32[]{:S(2)}) %collective-permute-start.9) | collective-permute-done | bytes 61472 | tf_op jit(solution)/shard_map/ppermute | solution.py:100
  145.9 0.8 dynamic_update_slice.32
  146.7 1.7 collective-permute-done.10
  148.4 0.8 dynamic_update_slice.33
  149.2 1.9 %collective-permute-start.11 = (bf16[40,3072]{1,0:T(8,128)(2,1)S(1)}, bf16[40,3072]{1,0:T(8,128)(2,1)S(1)}, u32[]{:S(2)}, u32[]{:S(2)}) collective-permute-start(bf16[40,3072]{1,0:T(8,128)(2,1)S(1)} %dynamic_update_slice.33), channel_id=1, source_target_pairs={{0,2},{1,3},{2,4},{3,5},{4,6},{5,7},{6,0},{7,1},{8,10},{9,11},{10,... | collective-permute-start | bytes 737288 | tf_op jit(solution)/shard_map/ppermute | solution.py:100
  151.2 2.2 %collective-permute-start.12 = (bf16[40,3072]{1,0:T(8,128)(2,1)S(1)}, bf16[40,3072]{1,0:T(8,128)(2,1)S(1)}, u32[]{:S(2)}, u32[]{:S(2)}) collective-permute-start(bf16[40,3072]{1,0:T(8,128)(2,1)S(1)} %dynamic_update_slice.33), channel_id=1, source_target_pairs={{0,4},{1,5},{2,6},{3,7},{4,0},{5,1},{6,2},{7,3},{8,12},{9,13},{10,... | collective-permute-start | bytes 737288 | tf_op jit(solution)/shard_map/ppermute | solution.py:100
  153.4 4.5 %collective-permute-start.13 = (bf16[40,3072]{1,0:T(8,128)(2,1)S(1)}, bf16[40,3072]{1,0:T(8,128)(2,1)S(1)}, u32[]{:S(2)}, u32[]{:S(2)}) collective-permute-start(bf16[40,3072]{1,0:T(8,128)(2,1)S(1)} %dynamic_update_slice.33), channel_id=1, source_target_pairs={{0,6},{1,7},{2,0},{3,1},{4,2},{5,3},{6,4},{7,5},{8,14},{9,15},{10,... | collective-permute-start | bytes 737288 | tf_op jit(solution)/shard_map/ppermute | solution.py:100
  157.9 0.1 broadcast_in_dim.7
  158.1 1.9 collective-permute-done.11
  160.0 3.5 %collective-permute-done.12 = bf16[40,3072]{1,0:T(8,128)(2,1)S(1)} collective-permute-done((bf16[40,3072]{1,0:T(8,128)(2,1)S(1)}, bf16[40,3072]{1,0:T(8,128)(2,1)S(1)}, u32[]{:S(2)}, u32[]{:S(2)}) %collective-permute-start.12) | collective-permute-done | bytes 245792 | tf_op jit(solution)/shard_map/ppermute | solution.py:100
  163.5 4.0 %collective-permute-done.13 = bf16[40,3072]{1,0:T(8,128)(2,1)S(1)} collective-permute-done((bf16[40,3072]{1,0:T(8,128)(2,1)S(1)}, bf16[40,3072]{1,0:T(8,128)(2,1)S(1)}, u32[]{:S(2)}, u32[]{:S(2)}) %collective-permute-start.13) | collective-permute-done | bytes 245792 | tf_op jit(solution)/shard_map/ppermute | solution.py:100
  167.5 2.0 %collective-permute-start.14 = (bf16[160,3072]{1,0:T(8,128)(2,1)S(1)}, bf16[160,3072]{1,0:T(8,128)(2,1)S(1)}, u32[]{:S(2)}, u32[]{:S(2)}) collective-permute-start(bf16[160,3072]{1,0:T(8,128)(2,1)S(1)} %constant_dynamic-update-slice_fusion.2), channel_id=1, source_target_pairs={{0,1},{1,0},{2,3},{3,2},{4,5},{5,4},{6,7},{7,6},{8,9},{9,8},{10,11... | collective-permute-start | bytes 2949128 | tf_op jit(solution)/shard_map/ppermute | solution.py:100
  169.6 1.5 broadcast_in_dim.6
  171.1 1.0 constant_dynamic-update-slice_fusion.1
  172.1 1.0 constant_dynamic-update-slice_fusion
  173.1 8.6 %reduce-scatter.2.cloned.1.call-done = bf16[192,384]{1,0:T(8,128)(2,1)} async-done(((bf16[3072,384]{1,0:T(8,128)(2,1)}), bf16[192,384]{1,0:T(8,128)(2,1)}) %reduce-scatter.2.cloned.1.call-update) | async-done | bytes 147472 | tf_op jit(solution)/shard_map/reduce_scatter | solution.py:118
  181.7 1.6 convert_element_type.104
  (45 shorter events, 0.3 us)
Async XLA Ops:
  7.2 62.8 %copy-start = (bf16[320,128]{1,0:T(8,128)(2,1)S(1)}, bf16[320,128]{1,0:T(8,128)(2,1)}, u32[]{:S(2)}) copy-start(bf16[320,128]{1,0:T(8,128)(2,1)} %param.11) | copy-start | bytes 245764
  7.2 11.7 %copy-start.1 = (bf16[320,3072]{1,0:T(8,128)(2,1)S(1)}, bf16[320,3072]{1,0:T(8,128)(2,1)}, u32[]{:S(2)}) copy-start(bf16[320,3072]{1,0:T(8,128)(2,1)} %param.6) | copy-start | bytes 5898244
  7.2 11.7 %copy-start.8 = (f32[128]{0:T(128)S(1)}, f32[128]{0:T(128)}, u32[]{:S(2)}) copy-start(f32[128]{0:T(128)} %param.10) | copy-start | bytes 1540
  7.2 11.7 %copy-start.7 = (f32[128]{0:T(128)S(1)}, f32[128]{0:T(128)}, u32[]{:S(2)}) copy-start(f32[128]{0:T(128)} %param.9) | copy-start | bytes 1540
  7.2 58.9 %all-gather.2.cloned.1.call-start = ((), (), s32[]{:S(2)}) async-start(), calls=%async_computation.1 | async-start | bytes 2654208 | tf_op jit(solution)/shard_map/all_gather | solution.py:114
  7.3 7.8 %collective-permute-start = (bf16[192,384]{1,0:T(8,128)(2,1)}, bf16[192,384]{1,0:T(8,128)(2,1)S(1)}, u32[]{:S(2)}, u32[]{:S(2)}) collective-permute-start(bf16[192,384]{1,0:T(8,128)(2,1)} %param.8), channel_id=1, source_target_pairs={{0,256},{32,288},{64,320},{96,352},{128,384},{160,416},{192,448},{... | collective-permute-start | bytes 442376 | tf_op jit(solution)/shard_map/ppermute | solution.py:112
  15.1 51.1 %copy-start.5 = (f32[3072]{0:T(1024)S(1)}, f32[3072]{0:T(1024)}, u32[]{:S(2)}) copy-start(f32[3072]{0:T(1024)} %param.7) | copy-start | bytes 36868
  16.9 164.8 %reduce-scatter.2.cloned.1.call-start = ((), (), s32[]{:S(2)}) async-start(), calls=%async_computation.2 | async-start | bytes 2506752 | tf_op jit(solution)/shard_map/reduce_scatter | solution.py:118
  70.2 2.0 %copy-start.6 = (bf16[8,2,192,384]{3,2,0,1:T(8,128)(2,1)S(1)}, bf16[8,2,192,384]{3,2,0,1:T(8,128)(2,1)}, u32[]{:S(2)}) copy-start(bf16[8,2,192,384]{3,2,0,1:T(8,128)(2,1)} %all-gather.2.cloned.1.call-done) | copy-start | bytes 7077892
  70.4 1.7 copy-start.9
  72.1 1.3 copy-start.3
  72.1 1.3 copy-start.4
  73.4 1.3 copy-start.2
  74.8 4.6 %collective-permute-start.1 = (bf16[160,3072]{1,0:T(8,128)(2,1)S(1)}, bf16[160,3072]{1,0:T(8,128)(2,1)}, u32[]{:S(2)}, u32[]{:S(2)}) collective-permute-start(bf16[160,3072]{1,0:T(8,128)(2,1)S(1)} %constant_dynamic-slice_fusion.6), channel_id=1, source_target_pairs={{0,1},{1,0},{2,3},{3,2},{4,5},{5,4},{6,7},{7,6},{8,9},{9,8},{10,11... | collective-permute-start | bytes 2949128 | tf_op jit(solution)/shard_map/ppermute | solution.py:86
  81.9 14.7 %collective-permute-start.2 = (bf16[40,3072]{1,0:T(8,128)(2,1)}, bf16[40,3072]{1,0:T(8,128)(2,1)}, u32[]{:S(2)}, u32[]{:S(2)}) collective-permute-start(bf16[40,3072]{1,0:T(8,128)(2,1)} %get-tuple-element.13), channel_id=1, source_target_pairs={{0,2},{1,3},{2,4},{3,5},{4,6},{5,7},{6,0},{7,1},{8,10},{9,11},{10,... | collective-permute-start | bytes 737288 | tf_op jit(solution)/shard_map/ppermute | solution.py:86
  85.3 12.4 %collective-permute-start.3 = (bf16[40,3072]{1,0:T(8,128)(2,1)S(1)}, bf16[40,3072]{1,0:T(8,128)(2,1)}, u32[]{:S(2)}, u32[]{:S(2)}) collective-permute-start(bf16[40,3072]{1,0:T(8,128)(2,1)S(1)} %get-tuple-element.15), channel_id=1, source_target_pairs={{0,4},{1,5},{2,6},{3,7},{4,0},{5,1},{6,2},{7,3},{8,12},{9,13},{10,... | collective-permute-start | bytes 737288 | tf_op jit(solution)/shard_map/ppermute | solution.py:86
  88.4 13.4 %collective-permute-start.4 = (bf16[40,3072]{1,0:T(8,128)(2,1)S(1)}, bf16[40,3072]{1,0:T(8,128)(2,1)}, u32[]{:S(2)}, u32[]{:S(2)}) collective-permute-start(bf16[40,3072]{1,0:T(8,128)(2,1)S(1)} %get-tuple-element.14), channel_id=1, source_target_pairs={{0,6},{1,7},{2,0},{3,1},{4,2},{5,3},{6,4},{7,5},{8,14},{9,15},{10,... | collective-permute-start | bytes 737288 | tf_op jit(solution)/shard_map/ppermute | solution.py:86
  103.2 11.9 %collective-permute-start.5 = (bf16[10,3072]{1,0:T(8,128)(2,1)S(1)}, bf16[10,3072]{1,0:T(8,128)(2,1)S(1)}, u32[]{:S(2)}, u32[]{:S(2)}) collective-permute-start(bf16[10,3072]{1,0:T(8,128)(2,1)S(1)} %get-tuple-element.16), channel_id=1, source_target_pairs={{0,8},{1,9},{2,10},{3,11},{4,12},{5,13},{6,14},{7,15},{8,16},{9,17... | collective-permute-start | bytes 184328 | tf_op jit(solution)/shard_map/ppermute | solution.py:86
  106.4 13.9 %collective-permute-start.6 = (bf16[10,3072]{1,0:T(8,128)(2,1)S(1)}, bf16[10,3072]{1,0:T(8,128)(2,1)S(1)}, u32[]{:S(2)}, u32[]{:S(2)}) collective-permute-start(bf16[10,3072]{1,0:T(8,128)(2,1)S(1)} %get-tuple-element.18), channel_id=1, source_target_pairs={{0,16},{1,17},{2,18},{3,19},{4,20},{5,21},{6,22},{7,23},{8,24},{9,... | collective-permute-start | bytes 184328 | tf_op jit(solution)/shard_map/ppermute | solution.py:86
  112.9 13.2 %collective-permute-start.7 = (bf16[10,3072]{1,0:T(8,128)(2,1)S(1)}, bf16[10,3072]{1,0:T(8,128)(2,1)S(1)}, u32[]{:S(2)}, u32[]{:S(2)}) collective-permute-start(bf16[10,3072]{1,0:T(8,128)(2,1)S(1)} %get-tuple-element.17), channel_id=1, source_target_pairs={{0,24},{1,25},{2,26},{3,27},{4,28},{5,29},{6,30},{7,31},{8,0},{9,1... | collective-permute-start | bytes 184328 | tf_op jit(solution)/shard_map/ppermute | solution.py:86
  126.5 11.7 %collective-permute-start.8 = (bf16[10,3072]{1,0:T(8,128)(2,1)S(1)}, bf16[10,3072]{1,0:T(8,128)(2,1)S(1)}, u32[]{:S(2)}, u32[]{:S(2)}) collective-permute-start(bf16[10,3072]{1,0:T(8,128)(2,1)S(1)} %fusion.14), channel_id=1, source_target_pairs={{0,8},{1,9},{2,10},{3,11},{4,12},{5,13},{6,14},{7,15},{8,16},{9,17... | collective-permute-start | bytes 184328 | tf_op jit(solution)/shard_map/ppermute | solution.py:100
  128.4 17.5 %collective-permute-start.9 = (bf16[10,3072]{1,0:T(8,128)(2,1)S(1)}, bf16[10,3072]{1,0:T(8,128)(2,1)S(1)}, u32[]{:S(2)}, u32[]{:S(2)}) collective-permute-start(bf16[10,3072]{1,0:T(8,128)(2,1)S(1)} %fusion.14), channel_id=1, source_target_pairs={{0,16},{1,17},{2,18},{3,19},{4,20},{5,21},{6,22},{7,23},{8,24},{9,... | collective-permute-start | bytes 184328 | tf_op jit(solution)/shard_map/ppermute | solution.py:100
  135.5 12.9 %collective-permute-start.10 = (bf16[10,3072]{1,0:T(8,128)(2,1)S(1)}, bf16[10,3072]{1,0:T(8,128)(2,1)S(1)}, u32[]{:S(2)}, u32[]{:S(2)}) collective-permute-start(bf16[10,3072]{1,0:T(8,128)(2,1)S(1)} %fusion.14), channel_id=1, source_target_pairs={{0,24},{1,25},{2,26},{3,27},{4,28},{5,29},{6,30},{7,31},{8,0},{9,1... | collective-permute-start | bytes 184328 | tf_op jit(solution)/shard_map/ppermute | solution.py:100
  149.2 10.7 %collective-permute-start.11 = (bf16[40,3072]{1,0:T(8,128)(2,1)S(1)}, bf16[40,3072]{1,0:T(8,128)(2,1)S(1)}, u32[]{:S(2)}, u32[]{:S(2)}) collective-permute-start(bf16[40,3072]{1,0:T(8,128)(2,1)S(1)} %dynamic_update_slice.33), channel_id=1, source_target_pairs={{0,2},{1,3},{2,4},{3,5},{4,6},{5,7},{6,0},{7,1},{8,10},{9,11},{10,... | collective-permute-start | bytes 737288 | tf_op jit(solution)/shard_map/ppermute | solution.py:100
  151.2 12.3 %collective-permute-start.12 = (bf16[40,3072]{1,0:T(8,128)(2,1)S(1)}, bf16[40,3072]{1,0:T(8,128)(2,1)S(1)}, u32[]{:S(2)}, u32[]{:S(2)}) collective-permute-start(bf16[40,3072]{1,0:T(8,128)(2,1)S(1)} %dynamic_update_slice.33), channel_id=1, source_target_pairs={{0,4},{1,5},{2,6},{3,7},{4,0},{5,1},{6,2},{7,3},{8,12},{9,13},{10,... | collective-permute-start | bytes 737288 | tf_op jit(solution)/shard_map/ppermute | solution.py:100
  153.4 14.1 %collective-permute-start.13 = (bf16[40,3072]{1,0:T(8,128)(2,1)S(1)}, bf16[40,3072]{1,0:T(8,128)(2,1)S(1)}, u32[]{:S(2)}, u32[]{:S(2)}) collective-permute-start(bf16[40,3072]{1,0:T(8,128)(2,1)S(1)} %dynamic_update_slice.33), channel_id=1, source_target_pairs={{0,6},{1,7},{2,0},{3,1},{4,2},{5,3},{6,4},{7,5},{8,14},{9,15},{10,... | collective-permute-start | bytes 737288 | tf_op jit(solution)/shard_map/ppermute | solution.py:100
  167.5 4.6 %collective-permute-start.14 = (bf16[160,3072]{1,0:T(8,128)(2,1)S(1)}, bf16[160,3072]{1,0:T(8,128)(2,1)S(1)}, u32[]{:S(2)}, u32[]{:S(2)}) collective-permute-start(bf16[160,3072]{1,0:T(8,128)(2,1)S(1)} %constant_dynamic-update-slice_fusion.2), channel_id=1, source_target_pairs={{0,1},{1,0},{2,3},{3,2},{4,5},{5,4},{6,7},{7,6},{8,9},{9,8},{10,11... | collective-permute-start | bytes 2949128 | tf_op jit(solution)/shard_map/ppermute | solution.py:100
Sparse Core Ops, SparseCore 0:
  17.0 49.1 all-gather.1
  96.8 84.8 reduce-scatter.1

commit v2 on v0

v2 whole, which is shorter than its diff:
```python
import math

import jax
import jax.numpy as jnp
from jax import lax
from jax.experimental import pallas as pl
from jax.experimental.pallas import tpu as pltpu
from jax.sharding import PartitionSpec as P

EPSILON = 1e-06
Y_LO, Z = 2, 8
Y_HI, X, CORE = 4, 4, 2
MP = Y_HI * X * CORE
AXES = ("dp", "mp")
Z_STEPS = (0, 1, -1, -2, 2, 3, -3, -4)


def normalize(values):
    centred = values - jnp.mean(values, axis=-1, keepdims=True)
    inverse = lax.rsqrt(jnp.mean(centred * centred, axis=-1, keepdims=True) + EPSILON)
    return (centred * inverse, inverse)


def norm_backward(grad_unit, unit_vals, inverse):
    first_mean = jnp.mean(grad_unit, axis=-1, keepdims=True)
    second_mean = jnp.mean(grad_unit * unit_vals, axis=-1, keepdims=True)
    return inverse * (grad_unit - first_mean - unit_vals * second_mean)


def contract(left_op, right_op, left_dim, right_dim):
    return lax.dot_general(
        left_op,
        right_op,
        (((left_dim,), (right_dim,)), ((), ())),
        preferred_element_type=jnp.float32,
    )


def head_grads(qkv_head, cot_head, q_gain, k_gain):
    width = cot_head.shape[1]
    factor = 1.0 / math.sqrt(width)
    q_unit, q_inverse = normalize(qkv_head[:, :width].astype(jnp.float32))
    k_unit, k_inverse = normalize(qkv_head[:, width : 2 * width].astype(jnp.float32))
    values = qkv_head[:, 2 * width :]
    q_normed = (q_unit * q_gain).astype(jnp.bfloat16)
    k_normed = (k_unit * k_gain).astype(jnp.bfloat16)

    def weights_and_grads(rows, columns, row_cot, column_cot, key_axis):
        exp_scores = jnp.exp(contract(rows, columns, 1, 1) * factor)
        attn = exp_scores / jnp.sum(exp_scores, axis=key_axis, keepdims=True)
        grad_attn = contract(row_cot, column_cot, 1, 1)
        centre = jnp.sum(attn * grad_attn, axis=key_axis, keepdims=True)
        return attn, (attn * (grad_attn - centre)).astype(jnp.bfloat16)

    _, grad_scores = weights_and_grads(q_normed, k_normed, cot_head, values, 1)
    attn_t, grad_scores_t = weights_and_grads(k_normed, q_normed, values, cot_head, 0)
    grad_values = contract(attn_t.astype(jnp.bfloat16), cot_head, 1, 0)
    grad_query = norm_backward(
        contract(grad_scores, k_normed, 1, 0) * factor * q_gain, q_unit, q_inverse
    )
    grad_key = norm_backward(
        contract(grad_scores_t, q_normed, 1, 0) * factor * k_gain, k_unit, k_inverse
    )
    return jnp.concatenate([grad_query, grad_key, grad_values], axis=1)


def swap_blocks(rows, outer, inner):
    half = rows.shape[0] // 2
    quarter = half // 2
    rows = jnp.where(outer == 1, jnp.concatenate([rows[half:], rows[:half]]), rows)
    swapped = jnp.concatenate(
        [rows[quarter:half], rows[:quarter], rows[half + quarter :], rows[half : half + quarter]]
    )
    return jnp.where(inner == 1, swapped, rows)


def head_kernel(places, normed, cot, q_gain, k_gain, *refs):
    blocks, refs = refs[:10], refs[10:]
    grad_ref, kept_ref, sent_ref, weights_out, weights, sems, out_sem = refs
    depth = blocks[0].shape[0]
    copies = []
    for ref in blocks:
        for part in range(ref.shape[0] // depth):
            at = len(copies)
            first = pl.multiple_of(places[at] * depth, depth)
            copies.append(
                pltpu.make_async_copy(
                    ref.at[pl.ds(part * depth, depth), :],
                    weights.at[pl.ds(first, depth), :],
                    sems.at[at],
                )
            )
    for copy in copies:
        copy.start()
    for copy in copies:
        copy.wait()
    out_copy = pltpu.make_async_copy(weights, weights_out, out_sem)
    out_copy.start()
    width = weights.shape[1]
    total = None
    for first in range(0, weights.shape[0], width):
        at = pl.ds(first, width)
        product = jnp.dot(normed[:, at], weights[at, :], preferred_element_type=jnp.float32)
        total = product if total is None else total + product
    grads = head_grads(total.astype(jnp.bfloat16), cot[...], q_gain[...], k_gain[...])
    grad_ref[...] = grads.astype(jnp.bfloat16)
    core, outer, inner = places[16], places[17], places[18]
    half = grads.shape[0] // 2
    low, high = grads[:half], grads[half:]
    kept = swap_blocks(jnp.where(core == 0, low, high), outer, inner)
    sent = swap_blocks(jnp.where(core == 0, high, low), inner, outer).astype(jnp.bfloat16)
    kept_ref[...] = kept.astype(jnp.bfloat16)

    for first in range(0, weights.shape[0], width):
        at = pl.ds(first, width)
        sent_ref[:, at] = contract(sent, weights[at, :], 1, 1).astype(jnp.bfloat16)
    out_copy.wait()


def run_head(places, normed, cot, q_gain, k_gain, blocks):
    tokens, features = normed.shape
    width = blocks[0].shape[1]
    in_vmem = pl.BlockSpec(memory_space=pltpu.VMEM)
    anywhere = pl.BlockSpec(memory_space=pl.ANY)
    like = lambda *shape: jax.ShapeDtypeStruct(shape, jnp.bfloat16)
    return pl.pallas_call(
        head_kernel,
        out_shape=(
            like(tokens, width),
            like(tokens // 2, width),
            like(tokens // 2, features),
            like(features, width),
        ),
        in_specs=[pl.BlockSpec(memory_space=pltpu.SMEM)] + [in_vmem] * 4 + [anywhere] * len(blocks),
        out_specs=(in_vmem, in_vmem, in_vmem, anywhere),
        scratch_shapes=[
            pltpu.VMEM((features, width), jnp.bfloat16),
            pltpu.SemaphoreType.DMA((16,)),
            pltpu.SemaphoreType.DMA,
        ],
        compiler_params=pltpu.CompilerParams(vmem_limit_bytes=40 * 2**20),
        cost_estimate=pl.CostEstimate(
            flops=3 * tokens * features * width, bytes_accessed=8 * 2**20, transcendentals=200000
        ),
        name="head",
    )(places, normed, cot, q_gain, k_gain, *blocks)


def norm_kernel(inputs, gain, out):
    unit, _ = normalize(inputs[...].astype(jnp.float32))
    out[...] = (unit * gain[...]).astype(out.dtype)


def run_norm(inputs, gain):
    in_vmem = pl.BlockSpec(memory_space=pltpu.VMEM)
    return pl.pallas_call(
        norm_kernel,
        out_shape=jax.ShapeDtypeStruct(inputs.shape, jnp.bfloat16),
        in_specs=[in_vmem, in_vmem],
        out_specs=in_vmem,
        compiler_params=pltpu.CompilerParams(vmem_limit_bytes=24 * 2**20),
        cost_estimate=pl.CostEstimate(
            flops=8 * inputs.size, bytes_accessed=4 * inputs.size, transcendentals=0
        ),
        name="norm",
    )(inputs, gain)


def terms_kernel(places, normed, grads, out, terms, sems):
    features, width = terms.shape
    depth = features // (Y_LO * Z)
    copies = []
    for first in range(0, features, width):
        at = pl.ds(first, width)
        terms[at, :] = contract(normed[:, at], grads[...], 0, 0).astype(terms.dtype)
        for block in range(first // depth, (first + width) // depth):
            to = pl.multiple_of(places[block] * depth, depth)
            copies.append(
                pltpu.make_async_copy(
                    terms.at[pl.ds(block * depth, depth), :],
                    out.at[pl.ds(to, depth), :],
                    sems.at[block],
                )
            )
            copies[-1].start()
    for copy in copies:
        copy.wait()


def run_terms(places, normed, grads):
    tokens, features = normed.shape
    width = grads.shape[1]
    in_vmem = pl.BlockSpec(memory_space=pltpu.VMEM)
    return pl.pallas_call(
        terms_kernel,
        out_shape=jax.ShapeDtypeStruct((features, width), jnp.bfloat16),
        in_specs=[pl.BlockSpec(memory_space=pltpu.SMEM), in_vmem, in_vmem],
        out_specs=pl.BlockSpec(memory_space=pl.ANY),
        scratch_shapes=[
            pltpu.VMEM((features, width), jnp.bfloat16),
            pltpu.SemaphoreType.DMA((Y_LO * Z,)),
        ],
        compiler_params=pltpu.CompilerParams(vmem_limit_bytes=32 * 2**20),
        cost_estimate=pl.CostEstimate(
            flops=2 * tokens * features * width, bytes_accessed=5 * 2**20, transcendentals=0
        ),
        name="terms",
    )(places, normed, grads)


def pairs_of(partner):
    found = []
    for y_lo in range(Y_LO):
        for z in range(Z):
            for y_hi in range(Y_HI):
                for x in range(X):
                    for core in range(CORE):
                        ends = ((y_lo, z, y_hi, x, core), partner(y_lo, z, y_hi, x, core))
                        found.append(
                            tuple(
                                ((a % Y_LO) * Z + b % Z) * MP
                                + ((c % Y_HI) * X + d % X) * CORE
                                + e % CORE
                                for a, b, c, d, e in ends
                            )
                        )
    return found


def way(at, core):
    return 1 if (at + core) % 2 == 0 else -1


def swap(values, partner):
    return lax.ppermute(values, AXES, pairs_of(partner))


def by_y_lo(a, b, c, d, e):
    return (1 - a, b, c, d, e)


def by_core(a, b, c, d, e):
    return (a, b, c, d, 1 - e)


def by_z(turn):
    return lambda a, b, c, d, e: (a, b + turn * way(b, e), c, d, e)


def by_x(turn):
    return lambda a, b, c, d, e: (a, b, c, d + turn * way(d, e), e)


def by_y_hi(turn):
    return lambda a, b, c, d, e: (a, b, c + turn * way(c, e), d, e)


def along_z(block):
    first = swap(block, by_z(1))
    second = swap(jnp.concatenate([block, first]), by_z(-1))
    third = swap(second, by_z(1))
    fourth = swap(third, by_z(-1))
    return [block, first, second, third, fourth]


def add(left, right):
    return (left.astype(jnp.float32) + right.astype(jnp.float32)).astype(jnp.bfloat16)


def after(values, earlier):
    return lax.optimization_barrier((values, earlier))[0]


def join(own, got, place):
    return jnp.concatenate([jnp.where(place == 0, own, got), jnp.where(place == 0, got, own)])


def per_device(inputs, ln_gain, w_qkv, q_gain, k_gain, cotangent):
    dp_at, mp_at = lax.axis_index("dp"), lax.axis_index("mp")
    y_lo, z = dp_at // Z, dp_at % Z
    core, x = mp_at % CORE, mp_at // CORE % X
    near, far = (x + 1) // 2 % 2, x // 2
    outer, inner = jnp.where(core == 0, near, far), jnp.where(core == 0, far, near)
    z_way = jnp.where((z + core) % 2 == 0, 1, -1)
    z_places = [(z + z_way * step) % Z for step in Z_STEPS]
    places = jnp.stack(
        [y_lo * Z + at for at in z_places]
        + [(1 - y_lo) * Z + at for at in z_places]
        + [core, outer, inner]
    ).astype(jnp.int32)

    other = swap(w_qkv, by_y_lo)
    blocks = along_z(w_qkv) + along_z(other)
    normed = run_norm(inputs, ln_gain.reshape(1, -1))
    grad_qkv, kept, sent, weights = run_head(
        places, normed, cotangent, q_gain.reshape(1, -1), k_gain.reshape(1, -1), blocks
    )

    got = swap(sent, by_core)
    part = contract(kept, weights, 1, 1)
    rows = part.shape[0] // 2
    part, other = add(part[:rows], got[:rows]), add(part[rows:], got[rows:])
    steps = (jnp.arange(Z) - z) * z_way % Z
    order = jnp.array([Z_STEPS.index(step if step in Z_STEPS else step - Z) for step in range(Z)])
    z_order = order[steps]
    term_places = jnp.stack([z_order * Y_LO, z_order * Y_LO + 1]).reshape(-1).astype(jnp.int32)
    terms = run_terms(term_places, normed, after(grad_qkv, other))
    depth = terms.shape[0] // Z
    zero, one, two, three, four = jnp.split(terms, [depth, 2 * depth, 4 * depth, 6 * depth])
    part = add(part, swap(other, by_x(1)))
    got = swap(four, by_z(-1))
    rows = rows // 2
    part, other = part[:rows], after(part[rows:], four)
    part = add(part, swap(other, by_x(-1)))

    three = add(three, after(got, part))
    got = swap(three, by_z(1))
    part = add(part, swap(part, by_y_hi(1)))
    part = after(part, three)
    grad_normed = part.astype(jnp.float32) + swap(part, by_y_hi(-1)).astype(jnp.float32)
    first = ((core * 2 + outer) * 2 + inner) * rows
    own_unit, own_inverse = normalize(
        lax.dynamic_slice_in_dim(inputs, first, rows, 0).astype(jnp.float32)
    )
    own = norm_backward(grad_normed * ln_gain, own_unit, own_inverse).astype(jnp.bfloat16)

    two = add(two, after(got, own))
    got = swap(two, by_z(-1))
    own = after(join(own, swap(own, by_x(-1)), inner), two)

    got = after(got, own)
    zero, one = add(zero, got[:depth]), add(one, got[depth:])
    got = swap(one, by_z(1))
    own = after(join(own, swap(own, by_x(1)), outer), one)

    zero = add(zero, after(got, own))
    depth = zero.shape[0] // 2
    low, high = zero[:depth], zero[depth:]
    share = swap(jnp.where(y_lo == 0, high, low), by_y_lo)
    got = swap(own, by_core)
    grad_input = lax.dynamic_update_slice_in_dim(
        jnp.concatenate([own, own]), got, (1 - core) * own.shape[0], 0
    )
    grad_w_qkv = jnp.where(y_lo == 0, low, high).astype(jnp.float32) + share.astype(jnp.float32)
    return (grad_input, grad_w_qkv)


def solution(mesh):
    placed = (P("dp", None), P(), P("dp", "mp"), P(), P(), P("dp", "mp"))
    return jax.shard_map(
        per_device,
        mesh=mesh,
        in_specs=placed,
        out_specs=(P("dp", None), P("dp", "mp")),
        check_vma=False,
    )
```

time: 480 us -> 159 us (0.33)
  the two profiles are of different devices: /device:TPU:6 before, /device:TPU:16 now
where the time goes in v2:
time: 159 us; the launch traced here: 158 us
  starting transfers between devices  72.8 us (46%)
  waiting for transfers between devices  43 us (27%)
  Pallas kernels  17 us (11%)
  other arithmetic  14 us (9%)
  local copies, waits for them, and re-layouts  6.62 us (4%)
  matrix products  2.65 us (2%)
    ppermute x22, starting transfers between devices, swap(): return lax.ppermute(values, AXES, pairs_of(partner))  72.8 us
    ppermute x22, waiting for transfers between devices, swap(): return lax.ppermute(values, AXES, pairs_of(partner))  43 us
    pallas_call x1, Pallas kernels, run_head(): pl.pallas_call(head_kernel, out_shape=(like(tokens, width), like(tokens /...  8.79 us
    pallas_call x1, Pallas kernels, run_terms(): pl.pallas_call(terms_kernel, out_shape=jax.ShapeDtypeStruct((features, wi...  6.91 us
    convert_element_type x8, other arithmetic, add(): (left.astype(jnp.float32) + right.astype(jnp.float32)).astype(jnp.bfloat16)  6.03 us
    unnamed x30, local copies, waits for them, and re-layouts  5.63 us
  transfers between devices with their start and end apart: 22, of which 14 were waited for; matrix products, arithmetic and copies ran while one was open for 10% of the time, Pallas kernels for 5%

profile of v2, /device:TPU:16, one launch (start us, length us, event | category | flops | bytes accessed | tf_op | source)
XLA Modules:
  0.0 157.6 jit_solution(8721770478305186850)
XLA Ops:
  0.6 3.5 %collective-permute-start.4 = (bf16[192,384]{1,0:T(8,128)(2,1)}, bf16[192,384]{1,0:T(8,128)(2,1)S(1)}, u32[]{:S(2)}, u32[]{:S(2)}) collective-permute-start(bf16[192,384]{1,0:T(8,128)(2,1)} %refs_0_.1), channel_id=1, source_target_pairs={{0,256},{1,257},{2,258},{3,259},{4,260},{5,261},{6,262},{7,263},{8... | collective-permute-start | bytes 442376 | tf_op jit(solution)/shard_map/ppermute | solution.py:235
  4.1 4.3 %collective-permute-start = (bf16[192,384]{1,0:T(8,128)(2,1)}, bf16[192,384]{1,0:T(8,128)(2,1)S(1)}, u32[]{:S(2)}, u32[]{:S(2)}) collective-permute-start(bf16[192,384]{1,0:T(8,128)(2,1)} %refs_0_.1), channel_id=1, source_target_pairs={{0,32},{1,225},{2,34},{3,227},{4,36},{5,229},{6,38},{7,231},{8,40}... | collective-permute-start | bytes 442376 | tf_op jit(solution)/shard_map/ppermute | solution.py:235
  8.4 4.2 %collective-permute-start.5 = (bf16[192,384]{1,0:T(8,128)(2,1)S(1)}, bf16[192,384]{1,0:T(8,128)(2,1)S(1)}, u32[]{:S(2)}, u32[]{:S(2)}) collective-permute-start(bf16[192,384]{1,0:T(8,128)(2,1)S(1)} %collective-permute-done.4.refs_5_), channel_id=1, source_target_pairs={{0,32},{1,225},{2,34},{3,227},{4,36},{5,229},{6,38},{7,231},{8,40}... | collective-permute-start | bytes 442376 | tf_op jit(solution)/shard_map/ppermute | solution.py:235
  12.6 0.9 pad_maximum_fusion.3
  13.6 9.7 %collective-permute-start.1 = (bf16[384,384]{1,0:T(8,128)(2,1)S(1)}, bf16[384,384]{1,0:T(8,128)(2,1)S(1)}, u32[]{:S(2)}, u32[]{:S(2)}) collective-permute-start(bf16[384,384]{1,0:T(8,128)(2,1)S(1)} %pad_maximum_fusion.3), channel_id=1, source_target_pairs={{0,224},{1,33},{2,226},{3,35},{4,228},{5,37},{6,230},{7,39},{8,232... | collective-permute-start | bytes 884744 | tf_op jit(solution)/shard_map/ppermute | solution.py:235
  23.3 3.0 %collective-permute-start.6 = (bf16[384,384]{1,0:T(8,128)(2,1)S(1)}, bf16[384,384]{1,0:T(8,128)(2,1)S(1)}, u32[]{:S(2)}, u32[]{:S(2)}) collective-permute-start(bf16[384,384]{1,0:T(8,128)(2,1)S(1)} %pad_maximum_fusion.4), channel_id=1, source_target_pairs={{0,224},{1,33},{2,226},{3,35},{4,228},{5,37},{6,230},{7,39},{8,232... | collective-permute-start | bytes 884744 | tf_op jit(solution)/shard_map/ppermute | solution.py:235
  26.3 1.6 %collective-permute-done.1.refs_2_ = bf16[384,384]{1,0:T(8,128)(2,1)S(1)} collective-permute-done((bf16[384,384]{1,0:T(8,128)(2,1)S(1)}, bf16[384,384]{1,0:T(8,128)(2,1)S(1)}, u32[]{:S(2)}, u32[]{:S(2)}) %collective-permute-start.1) | collective-permute-done | bytes 294944 | tf_op jit(solution)/shard_map/ppermute | solution.py:235
  28.0 1.9 %collective-permute-start.2 = (bf16[384,384]{1,0:T(8,128)(2,1)S(1)}, bf16[384,384]{1,0:T(8,128)(2,1)S(1)}, u32[]{:S(2)}, u32[]{:S(2)}) collective-permute-start(bf16[384,384]{1,0:T(8,128)(2,1)S(1)} %collective-permute-done.1.refs_2_), channel_id=1, source_target_pairs={{0,32},{1,225},{2,34},{3,227},{4,36},{5,229},{6,38},{7,231},{8,40}... | collective-permute-start | bytes 884744 | tf_op jit(solution)/shard_map/ppermute | solution.py:235
  29.9 4.0 %collective-permute-done.6.refs_7_ = bf16[384,384]{1,0:T(8,128)(2,1)S(1)} collective-permute-done((bf16[384,384]{1,0:T(8,128)(2,1)S(1)}, bf16[384,384]{1,0:T(8,128)(2,1)S(1)}, u32[]{:S(2)}, u32[]{:S(2)}) %collective-permute-start.6) | collective-permute-done | bytes 294944 | tf_op jit(solution)/shard_map/ppermute | solution.py:235
  33.9 1.9 %collective-permute-start.7 = (bf16[384,384]{1,0:T(8,128)(2,1)S(1)}, bf16[384,384]{1,0:T(8,128)(2,1)}, u32[]{:S(2)}, u32[]{:S(2)}) collective-permute-start(bf16[384,384]{1,0:T(8,128)(2,1)S(1)} %collective-permute-done.6.refs_7_), channel_id=1, source_target_pairs={{0,32},{1,225},{2,34},{3,227},{4,36},{5,229},{6,38},{7,231},{8,40}... | collective-permute-start | bytes 884744 | tf_op jit(solution)/shard_map/ppermute | solution.py:235
  35.8 0.8 collective-permute-done.2.refs_3_
  36.6 5.1 %collective-permute-start.3 = (bf16[384,384]{1,0:T(8,128)(2,1)S(1)}, bf16[384,384]{1,0:T(8,128)(2,1)}, u32[]{:S(2)}, u32[]{:S(2)}) collective-permute-start(bf16[384,384]{1,0:T(8,128)(2,1)S(1)} %collective-permute-done.2.refs_3_), channel_id=1, source_target_pairs={{0,224},{1,33},{2,226},{3,35},{4,228},{5,37},{6,230},{7,39},{8,232... | collective-permute-start | bytes 884744 | tf_op jit(solution)/shard_map/ppermute | solution.py:235
  41.7 2.7 %collective-permute-done.7.refs_8_ = bf16[384,384]{1,0:T(8,128)(2,1)} collective-permute-done((bf16[384,384]{1,0:T(8,128)(2,1)S(1)}, bf16[384,384]{1,0:T(8,128)(2,1)}, u32[]{:S(2)}, u32[]{:S(2)}) %collective-permute-start.7) | collective-permute-done | bytes 294944 | tf_op jit(solution)/shard_map/ppermute | solution.py:235
  44.4 1.9 %collective-permute-start.8 = (bf16[384,384]{1,0:T(8,128)(2,1)}, bf16[384,384]{1,0:T(8,128)(2,1)}, u32[]{:S(2)}, u32[]{:S(2)}) collective-permute-start(bf16[384,384]{1,0:T(8,128)(2,1)} %collective-permute-done.7.refs_8_), channel_id=1, source_target_pairs={{0,224},{1,33},{2,226},{3,35},{4,228},{5,37},{6,230},{7,39},{8,232... | collective-permute-start | bytes 884744 | tf_op jit(solution)/shard_map/ppermute | solution.py:235
  46.6 0.1 stack.84.places
  46.7 1.5 copy-done.2
  48.3 0.7 copy-done.6
  49.0 1.3 norm.1.normed
  50.3 4.3 %collective-permute-done.8.refs_9_ = bf16[384,384]{1,0:T(8,128)(2,1)} collective-permute-done((bf16[384,384]{1,0:T(8,128)(2,1)}, bf16[384,384]{1,0:T(8,128)(2,1)}, u32[]{:S(2)}, u32[]{:S(2)}) %collective-permute-start.8) | collective-permute-done | bytes 294944 | tf_op jit(solution)/shard_map/ppermute | solution.py:235
  54.6 8.8 %head.1 = (bf16[320,384]{1,0:T(8,128)(2,1)S(1)}, bf16[160,384]{1,0:T(8,128)(2,1)S(1)}, bf16[160,3072]{1,0:T(8,128)(2,1)}, bf16[3072,384]{1,0:T(8,128)(2,1)S(1)}) custom-call(s32[19]{0:T(128)S(1)} %stack.84.places, bf16[320,3072]{1,0:T(8,128)(2,1)S(1)} %norm.1.normed, bf16[320,128]{1,0:T(8,128)(2,1)S(1)} %copy-done.8, f32[1,128]{1,0:T(1,128)S(1)} %bitcast.31, ...), custom_call_target="tpu_custom_call" | custom-call | flops 1132462080 | bytes 8388608 | tf_op jit(solution)/shard_map/head/pallas_call | solution.py:126
  63.4 1.4 copy-done.3
  64.8 0.6 copy-done.5
  65.5 1.9 %collective-permute-start.9 = (bf16[160,3072]{1,0:T(8,128)(2,1)}, bf16[160,3072]{1,0:T(8,128)(2,1)S(1)}, u32[]{:S(2)}, u32[]{:S(2)}) collective-permute-start(bf16[160,3072]{1,0:T(8,128)(2,1)} %get-tuple-element.17), channel_id=1, source_target_pairs={{0,1},{1,0},{2,3},{3,2},{4,5},{5,4},{6,7},{7,6},{8,9},{9,8},{10,11... | collective-permute-start | bytes 2949128 | tf_op jit(solution)/shard_map/ppermute | solution.py:235
  67.4 0.6 gather_fusion
  68.1 2.6 %fusion.14 = f32[160,3072]{1,0:T(8,128)S(1)} fusion(bf16[160,384]{1,0:T(8,128)(2,1)} %copy-done.5, bf16[3072,384]{1,0:T(8,128)(2,1)} %copy-done.3), kind=kOutput, calls=%fused_computation.52 | convolution fusion | flops 377487360 | bytes 4448256 | tf_op jit(solution)/shard_map/dot_general | solution.py:31
  70.8 1.0 fusion
  71.8 3.4 %collective-permute-start.10 = (bf16[80,3072]{1,0:T(8,128)(2,1)}, bf16[80,3072]{1,0:T(8,128)(2,1)}, u32[]{:S(2)}, u32[]{:S(2)}) collective-permute-start(bf16[80,3072]{1,0:T(8,128)(2,1)} %fusion), channel_id=1, source_target_pairs={{0,2},{1,7},{2,0},{3,5},{4,6},{5,3},{6,4},{7,1},{8,10},{9,15},{10,... | collective-permute-start | bytes 1474568 | tf_op jit(solution)/shard_map/ppermute | solution.py:235
  75.2 0.1 reshape.108.places
  75.3 6.9 %terms.1 = bf16[3072,384]{1,0:T(8,128)(2,1)S(1)} custom-call(s32[16]{0:T(128)S(1)} %reshape.108.places, bf16[320,3072]{1,0:T(8,128)(2,1)S(1)} %norm.1.normed, bf16[320,384]{1,0:T(8,128)(2,1)S(1)} %get-tuple-element.19.grads), custom_call_target="tpu_custom_call" | custom-call | flops 754974720 | bytes 5242880 | tf_op jit(solution)/shard_map/terms/pallas_call | solution.py:194
  82.3 0.5 collective-permute-done.10
  82.8 1.4 add_convert_fusion.2
  84.3 4.4 %collective-permute-start.11 = (bf16[40,3072]{1,0:T(8,128)(2,1)S(1)}, bf16[40,3072]{1,0:T(8,128)(2,1)S(1)}, u32[]{:S(2)}, u32[]{:S(2)}) collective-permute-start(bf16[40,3072]{1,0:T(8,128)(2,1)S(1)} %slice.47), channel_id=1, source_target_pairs={{0,6},{1,3},{2,4},{3,1},{4,2},{5,7},{6,0},{7,5},{8,14},{9,11},{10,... | collective-permute-start | bytes 737288 | tf_op jit(solution)/shard_map/ppermute | solution.py:235
  88.8 1.1 convert_reduce_fusion
  89.8 1.9 %collective-permute-start.13 = (bf16[768,384]{1,0:T(8,128)(2,1)S(1)}, bf16[768,384]{1,0:T(8,128)(2,1)S(1)}, u32[]{:S(2)}, u32[]{:S(2)}) collective-permute-start(bf16[768,384]{1,0:T(8,128)(2,1)S(1)} %split.20), channel_id=1, source_target_pairs={{0,224},{1,33},{2,226},{3,35},{4,228},{5,37},{6,230},{7,39},{8,232... | collective-permute-start | bytes 1769480 | tf_op jit(solution)/shard_map/ppermute | solution.py:235
  91.8 1.8 %collective-permute-done.11 = bf16[40,3072]{1,0:T(8,128)(2,1)S(1)} collective-permute-done((bf16[40,3072]{1,0:T(8,128)(2,1)S(1)}, bf16[40,3072]{1,0:T(8,128)(2,1)S(1)}, u32[]{:S(2)}, u32[]{:S(2)}) %collective-permute-start.11) | collective-permute-done | bytes 245792 | tf_op jit(solution)/shard_map/ppermute | solution.py:235
  93.7 2.4 %collective-permute-start.12 = (bf16[40,3072]{1,0:T(8,128)(2,1)S(1)}, bf16[40,3072]{1,0:T(8,128)(2,1)S(1)}, u32[]{:S(2)}, u32[]{:S(2)}) collective-permute-start(bf16[40,3072]{1,0:T(8,128)(2,1)S(1)} %add_convert_fusion.7), channel_id=1, source_target_pairs={{0,8},{1,25},{2,10},{3,27},{4,12},{5,29},{6,14},{7,31},{8,0},{9,17... | collective-permute-start | bytes 737288 | tf_op jit(solution)/shard_map/ppermute | solution.py:235
  96.1 6.8 %collective-permute-done.13 = bf16[768,384]{1,0:T(8,128)(2,1)S(1)} collective-permute-done((bf16[768,384]{1,0:T(8,128)(2,1)S(1)}, bf16[768,384]{1,0:T(8,128)(2,1)S(1)}, u32[]{:S(2)}, u32[]{:S(2)}) %collective-permute-start.13) | collective-permute-done | bytes 589856 | tf_op jit(solution)/shard_map/ppermute | solution.py:235
  102.8 1.2 add_convert_fusion.1
  104.1 0.3 collective-permute-done.12
  104.4 5.9 %collective-permute-start.14 = (bf16[40,3072]{1,0:T(8,128)(2,1)S(1)}, bf16[40,3072]{1,0:T(8,128)(2,1)S(1)}, u32[]{:S(2)}, u32[]{:S(2)}) collective-permute-start(bf16[40,3072]{1,0:T(8,128)(2,1)S(1)} %add_convert_fusion.6), channel_id=1, source_target_pairs={{0,24},{1,9},{2,26},{3,11},{4,28},{5,13},{6,30},{7,15},{8,16},{9,1... | collective-permute-start | bytes 737288 | tf_op jit(solution)/shard_map/ppermute | solution.py:235
  110.3 1.2 fusion.10
  111.6 1.9 %collective-permute-start.16 = (bf16[768,384]{1,0:T(8,128)(2,1)S(1)}, bf16[768,384]{1,0:T(8,128)(2,1)S(1)}, u32[]{:S(2)}, u32[]{:S(2)}) collective-permute-start(bf16[768,384]{1,0:T(8,128)(2,1)S(1)} %add_convert_fusion.1), channel_id=1, source_target_pairs={{0,32},{1,225},{2,34},{3,227},{4,36},{5,229},{6,38},{7,231},{8,40}... | collective-permute-start | bytes 1769480 | tf_op jit(solution)/shard_map/ppermute | solution.py:235
  113.5 3.8 %collective-permute-done.14 = bf16[40,3072]{1,0:T(8,128)(2,1)S(1)} collective-permute-done((bf16[40,3072]{1,0:T(8,128)(2,1)S(1)}, bf16[40,3072]{1,0:T(8,128)(2,1)S(1)}, u32[]{:S(2)}, u32[]{:S(2)}) %collective-permute-start.14) | collective-permute-done | bytes 245792 | tf_op jit(solution)/shard_map/ppermute | solution.py:235
  117.3 1.2 fusion.11
  118.5 1.2 fusion.9
  119.7 4.2 %collective-permute-start.15 = (bf16[40,3072]{1,0:T(8,128)(2,1)S(1)}, bf16[40,3072]{1,0:T(8,128)(2,1)S(1)}, u32[]{:S(2)}, u32[]{:S(2)}) collective-permute-start(bf16[40,3072]{1,0:T(8,128)(2,1)S(1)} %fusion.9), channel_id=1, source_target_pairs={{0,6},{1,3},{2,4},{3,1},{4,2},{5,7},{6,0},{7,5},{8,14},{9,11},{10,... | collective-permute-start | bytes 737288 | tf_op jit(solution)/shard_map/ppermute | solution.py:235
  123.9 0.1 add_convert_fusion
  124.1 3.5 %collective-permute-start.18 = (bf16[768,384]{1,0:T(8,128)(2,1)S(1)}, bf16[768,384]{1,0:T(8,128)(2,1)}, u32[]{:S(2)}, u32[]{:S(2)}) collective-permute-start(bf16[768,384]{1,0:T(8,128)(2,1)S(1)} %add_convert_fusion), channel_id=1, source_target_pairs={{0,224},{1,33},{2,226},{3,35},{4,228},{5,37},{6,230},{7,39},{8,232... | collective-permute-start | bytes 1769480 | tf_op jit(solution)/shard_map/ppermute | solution.py:235
  127.6 1.4 collective-permute-done.15
  129.1 1.9 %collective-permute-start.17 = (bf16[80,3072]{1,0:T(8,128)(2,1)S(1)}, bf16[80,3072]{1,0:T(8,128)(2,1)}, u32[]{:S(2)}, u32[]{:S(2)}) collective-permute-start(bf16[80,3072]{1,0:T(8,128)(2,1)S(1)} %pad_maximum_fusion.2), channel_id=1, source_target_pairs={{0,2},{1,7},{2,0},{3,5},{4,6},{5,3},{6,4},{7,1},{8,10},{9,15},{10,... | collective-permute-start | bytes 1474568 | tf_op jit(solution)/shard_map/ppermute | solution.py:235
  131.1 6.6 %collective-permute-done.18 = bf16[768,384]{1,0:T(8,128)(2,1)} collective-permute-done((bf16[768,384]{1,0:T(8,128)(2,1)S(1)}, bf16[768,384]{1,0:T(8,128)(2,1)}, u32[]{:S(2)}, u32[]{:S(2)}) %collective-permute-start.18) | collective-permute-done | bytes 589856 | tf_op jit(solution)/shard_map/ppermute | solution.py:235
  137.6 1.0 add_convert_fusion.5
  138.7 1.9 %collective-permute-start.20 = (bf16[384,384]{1,0:T(8,128)(2,1)S(1)}, bf16[384,384]{1,0:T(8,128)(2,1)S(1)}, u32[]{:S(2)}, u32[]{:S(2)}) collective-permute-start(bf16[384,384]{1,0:T(8,128)(2,1)S(1)} %add_convert_fusion.5), channel_id=1, source_target_pairs={{0,32},{1,225},{2,34},{3,227},{4,36},{5,229},{6,38},{7,231},{8,40}... | collective-permute-start | bytes 884744 | tf_op jit(solution)/shard_map/ppermute | solution.py:235
  140.6 1.1 broadcast_select_fusion.1
  141.7 0.1 pad_maximum_fusion.1
  141.8 1.9 %collective-permute-start.19 = (bf16[160,3072]{1,0:T(8,128)(2,1)S(1)}, bf16[160,3072]{1,0:T(8,128)(2,1)S(1)}, u32[]{:S(2)}, u32[]{:S(2)}) collective-permute-start(bf16[160,3072]{1,0:T(8,128)(2,1)S(1)} %pad_maximum_fusion.1), channel_id=1, source_target_pairs={{0,1},{1,0},{2,3},{3,2},{4,5},{5,4},{6,7},{7,6},{8,9},{9,8},{10,11... | collective-permute-start | bytes 2949128 | tf_op jit(solution)/shard_map/ppermute | solution.py:235
  143.7 3.6 %collective-permute-done.20 = bf16[384,384]{1,0:T(8,128)(2,1)S(1)} collective-permute-done((bf16[384,384]{1,0:T(8,128)(2,1)S(1)}, bf16[384,384]{1,0:T(8,128)(2,1)S(1)}, u32[]{:S(2)}, u32[]{:S(2)}) %collective-permute-start.20) | collective-permute-done | bytes 294944 | tf_op jit(solution)/shard_map/ppermute | solution.py:235
  147.3 1.1 add_convert_fusion.3
  148.4 1.9 %collective-permute-start.21 = (bf16[192,384]{1,0:T(8,128)(2,1)S(1)}, bf16[192,384]{1,0:T(8,128)(2,1)S(1)}, u32[]{:S(2)}, u32[]{:S(2)}) collective-permute-start(bf16[192,384]{1,0:T(8,128)(2,1)S(1)} %broadcast_select_fusion.4), channel_id=1, source_target_pairs={{0,256},{1,257},{2,258},{3,259},{4,260},{5,261},{6,262},{7,263},{8... | collective-permute-start | bytes 442376 | tf_op jit(solution)/shard_map/ppermute | solution.py:235
  150.3 0.2 pad_maximum_fusion
  150.5 4.9 %collective-permute-done.21 = bf16[192,384]{1,0:T(8,128)(2,1)S(1)} collective-permute-done((bf16[192,384]{1,0:T(8,128)(2,1)S(1)}, bf16[192,384]{1,0:T(8,128)(2,1)S(1)}, u32[]{:S(2)}, u32[]{:S(2)}) %collective-permute-start.21) | collective-permute-done | bytes 147488 | tf_op jit(solution)/shard_map/ppermute | solution.py:235
  155.4 0.8 convert_add_fusion
  156.2 0.1 constant_dynamic-update-slice_fusion
  156.3 1.3 copy-done.14
  (49 shorter events, 0.5 us)
Async XLA Ops:
  0.6 7.8 %collective-permute-start.4 = (bf16[192,384]{1,0:T(8,128)(2,1)}, bf16[192,384]{1,0:T(8,128)(2,1)S(1)}, u32[]{:S(2)}, u32[]{:S(2)}) collective-permute-start(bf16[192,384]{1,0:T(8,128)(2,1)} %refs_0_.1), channel_id=1, source_target_pairs={{0,256},{1,257},{2,258},{3,259},{4,260},{5,261},{6,262},{7,263},{8... | collective-permute-start | bytes 442376 | tf_op jit(solution)/shard_map/ppermute | solution.py:235
  4.1 8.5 %collective-permute-start = (bf16[192,384]{1,0:T(8,128)(2,1)}, bf16[192,384]{1,0:T(8,128)(2,1)S(1)}, u32[]{:S(2)}, u32[]{:S(2)}) collective-permute-start(bf16[192,384]{1,0:T(8,128)(2,1)} %refs_0_.1), channel_id=1, source_target_pairs={{0,32},{1,225},{2,34},{3,227},{4,36},{5,229},{6,38},{7,231},{8,40}... | collective-permute-start | bytes 442376 | tf_op jit(solution)/shard_map/ppermute | solution.py:235
  8.4 14.9 %collective-permute-start.5 = (bf16[192,384]{1,0:T(8,128)(2,1)S(1)}, bf16[192,384]{1,0:T(8,128)(2,1)S(1)}, u32[]{:S(2)}, u32[]{:S(2)}) collective-permute-start(bf16[192,384]{1,0:T(8,128)(2,1)S(1)} %collective-permute-done.4.refs_5_), channel_id=1, source_target_pairs={{0,32},{1,225},{2,34},{3,227},{4,36},{5,229},{6,38},{7,231},{8,40}... | collective-permute-start | bytes 442376 | tf_op jit(solution)/shard_map/ppermute | solution.py:235
  13.6 14.4 %collective-permute-start.1 = (bf16[384,384]{1,0:T(8,128)(2,1)S(1)}, bf16[384,384]{1,0:T(8,128)(2,1)S(1)}, u32[]{:S(2)}, u32[]{:S(2)}) collective-permute-start(bf16[384,384]{1,0:T(8,128)(2,1)S(1)} %pad_maximum_fusion.3), channel_id=1, source_target_pairs={{0,224},{1,33},{2,226},{3,35},{4,228},{5,37},{6,230},{7,39},{8,232... | collective-permute-start | bytes 884744 | tf_op jit(solution)/shard_map/ppermute | solution.py:235
  23.3 10.6 %collective-permute-start.6 = (bf16[384,384]{1,0:T(8,128)(2,1)S(1)}, bf16[384,384]{1,0:T(8,128)(2,1)S(1)}, u32[]{:S(2)}, u32[]{:S(2)}) collective-permute-start(bf16[384,384]{1,0:T(8,128)(2,1)S(1)} %pad_maximum_fusion.4), channel_id=1, source_target_pairs={{0,224},{1,33},{2,226},{3,35},{4,228},{5,37},{6,230},{7,39},{8,232... | collective-permute-start | bytes 884744 | tf_op jit(solution)/shard_map/ppermute | solution.py:235
  28.0 8.6 %collective-permute-start.2 = (bf16[384,384]{1,0:T(8,128)(2,1)S(1)}, bf16[384,384]{1,0:T(8,128)(2,1)S(1)}, u32[]{:S(2)}, u32[]{:S(2)}) collective-permute-start(bf16[384,384]{1,0:T(8,128)(2,1)S(1)} %collective-permute-done.1.refs_2_), channel_id=1, source_target_pairs={{0,32},{1,225},{2,34},{3,227},{4,36},{5,229},{6,38},{7,231},{8,40}... | collective-permute-start | bytes 884744 | tf_op jit(solution)/shard_map/ppermute | solution.py:235
  33.9 10.5 %collective-permute-start.7 = (bf16[384,384]{1,0:T(8,128)(2,1)S(1)}, bf16[384,384]{1,0:T(8,128)(2,1)}, u32[]{:S(2)}, u32[]{:S(2)}) collective-permute-start(bf16[384,384]{1,0:T(8,128)(2,1)S(1)} %collective-permute-done.6.refs_7_), channel_id=1, source_target_pairs={{0,32},{1,225},{2,34},{3,227},{4,36},{5,229},{6,38},{7,231},{8,40}... | collective-permute-start | bytes 884744 | tf_op jit(solution)/shard_map/ppermute | solution.py:235
  36.6 13.7 %collective-permute-start.3 = (bf16[384,384]{1,0:T(8,128)(2,1)S(1)}, bf16[384,384]{1,0:T(8,128)(2,1)}, u32[]{:S(2)}, u32[]{:S(2)}) collective-permute-start(bf16[384,384]{1,0:T(8,128)(2,1)S(1)} %collective-permute-done.2.refs_3_), channel_id=1, source_target_pairs={{0,224},{1,33},{2,226},{3,35},{4,228},{5,37},{6,230},{7,39},{8,232... | collective-permute-start | bytes 884744 | tf_op jit(solution)/shard_map/ppermute | solution.py:235
  44.4 10.1 %collective-permute-start.8 = (bf16[384,384]{1,0:T(8,128)(2,1)}, bf16[384,384]{1,0:T(8,128)(2,1)}, u32[]{:S(2)}, u32[]{:S(2)}) collective-permute-start(bf16[384,384]{1,0:T(8,128)(2,1)} %collective-permute-done.7.refs_8_), channel_id=1, source_target_pairs={{0,224},{1,33},{2,226},{3,35},{4,228},{5,37},{6,230},{7,39},{8,232... | collective-permute-start | bytes 884744 | tf_op jit(solution)/shard_map/ppermute | solution.py:235
  46.7 1.6 copy-start.2
  48.3 0.7 copy-start.6
  49.0 5.6 %copy-start.4 = (bf16[192,384]{1,0:T(8,128)(2,1)S(1)}, bf16[192,384]{1,0:T(8,128)(2,1)}, u32[]{:S(2)}) copy-start(bf16[192,384]{1,0:T(8,128)(2,1)} %refs_0_.1) | copy-start | bytes 442372
  49.0 5.6 %copy-start.8 = (bf16[320,128]{1,0:T(8,128)(2,1)S(1)}, bf16[320,128]{1,0:T(8,128)(2,1)}, u32[]{:S(2)}) copy-start(bf16[320,128]{1,0:T(8,128)(2,1)} %cot.1) | copy-start | bytes 245764
  49.0 5.6 %copy-start.9 = (f32[128]{0:T(128)S(1)}, f32[128]{0:T(128)}, u32[]{:S(2)}) copy-start(f32[128]{0:T(128)} %param.10) | copy-start | bytes 1540
  49.0 5.6 %copy-start.10 = (f32[128]{0:T(128)S(1)}, f32[128]{0:T(128)}, u32[]{:S(2)}) copy-start(f32[128]{0:T(128)} %param.11) | copy-start | bytes 1540
  54.6 12.8 %copy-start.11 = (s32[8]{0:T(128)S(1)}, s32[8]{0:T(128)}, u32[]{:S(2)}) copy-start(s32[8]{0:T(128)} %constant.155.clone) | copy-start | bytes 100
  63.4 1.4 copy-start.3
  64.8 0.6 copy-start.5
  65.5 5.3 %collective-permute-start.9 = (bf16[160,3072]{1,0:T(8,128)(2,1)}, bf16[160,3072]{1,0:T(8,128)(2,1)S(1)}, u32[]{:S(2)}, u32[]{:S(2)}) collective-permute-start(bf16[160,3072]{1,0:T(8,128)(2,1)} %get-tuple-element.17), channel_id=1, source_target_pairs={{0,1},{1,0},{2,3},{3,2},{4,5},{5,4},{6,7},{7,6},{8,9},{9,8},{10,11... | collective-permute-start | bytes 2949128 | tf_op jit(solution)/shard_map/ppermute | solution.py:235
  70.7 4.5 %copy-start.12 = (f32[160,3072]{1,0:T(8,128)}, f32[160,3072]{1,0:T(8,128)S(1)}, u32[]{:S(2)}) copy-start(f32[160,3072]{1,0:T(8,128)S(1)} %fusion.14) | copy-start | bytes 5898244
  71.8 11.0 %collective-permute-start.10 = (bf16[80,3072]{1,0:T(8,128)(2,1)}, bf16[80,3072]{1,0:T(8,128)(2,1)}, u32[]{:S(2)}, u32[]{:S(2)}) collective-permute-start(bf16[80,3072]{1,0:T(8,128)(2,1)} %fusion), channel_id=1, source_target_pairs={{0,2},{1,7},{2,0},{3,5},{4,6},{5,3},{6,4},{7,1},{8,10},{9,15},{10,... | collective-permute-start | bytes 1474568 | tf_op jit(solution)/shard_map/ppermute | solution.py:235
  75.3 7.5 %copy-start.13 = (f32[160,3072]{1,0:T(8,128)S(1)}, f32[160,3072]{1,0:T(8,128)}, u32[]{:S(2)}) copy-start(f32[160,3072]{1,0:T(8,128)} %copy-done.12) | copy-start | bytes 5898244
  82.2 2.0 %copy-start = (bf16[3072,384]{1,0:T(8,128)(2,1)}, bf16[3072,384]{1,0:T(8,128)(2,1)S(1)}, u32[]{:S(2)}) copy-start(bf16[3072,384]{1,0:T(8,128)(2,1)S(1)} %terms.1) | copy-start | bytes 7077892
  84.3 33.0 %copy-start.7 = (f32[3072]{0:T(1024)S(1)}, f32[3072]{0:T(1024)}, u32[]{:S(2)}) copy-start(f32[3072]{0:T(1024)} %param.8) | copy-start | bytes 36868
  84.3 9.3 %collective-permute-start.11 = (bf16[40,3072]{1,0:T(8,128)(2,1)S(1)}, bf16[40,3072]{1,0:T(8,128)(2,1)S(1)}, u32[]{:S(2)}, u32[]{:S(2)}) collective-permute-start(bf16[40,3072]{1,0:T(8,128)(2,1)S(1)} %slice.47), channel_id=1, source_target_pairs={{0,6},{1,3},{2,4},{3,1},{4,2},{5,7},{6,0},{7,5},{8,14},{9,11},{10,... | collective-permute-start | bytes 737288 | tf_op jit(solution)/shard_map/ppermute | solution.py:235
  89.8 13.0 %collective-permute-start.13 = (bf16[768,384]{1,0:T(8,128)(2,1)S(1)}, bf16[768,384]{1,0:T(8,128)(2,1)S(1)}, u32[]{:S(2)}, u32[]{:S(2)}) collective-permute-start(bf16[768,384]{1,0:T(8,128)(2,1)S(1)} %split.20), channel_id=1, source_target_pairs={{0,224},{1,33},{2,226},{3,35},{4,228},{5,37},{6,230},{7,39},{8,232... | collective-permute-start | bytes 1769480 | tf_op jit(solution)/shard_map/ppermute | solution.py:235
  93.6 30.3 %copy-start.1 = (bf16[3072,384]{1,0:T(8,128)(2,1)S(1)}, bf16[3072,384]{1,0:T(8,128)(2,1)}, u32[]{:S(2)}) copy-start(bf16[3072,384]{1,0:T(8,128)(2,1)} %copy-done) | copy-start | bytes 7077892
  93.7 10.7 %collective-permute-start.12 = (bf16[40,3072]{1,0:T(8,128)(2,1)S(1)}, bf16[40,3072]{1,0:T(8,128)(2,1)S(1)}, u32[]{:S(2)}, u32[]{:S(2)}) collective-permute-start(bf16[40,3072]{1,0:T(8,128)(2,1)S(1)} %add_convert_fusion.7), channel_id=1, source_target_pairs={{0,8},{1,25},{2,10},{3,27},{4,12},{5,29},{6,14},{7,31},{8,0},{9,17... | collective-permute-start | bytes 737288 | tf_op jit(solution)/shard_map/ppermute | solution.py:235
  104.4 12.8 %collective-permute-start.14 = (bf16[40,3072]{1,0:T(8,128)(2,1)S(1)}, bf16[40,3072]{1,0:T(8,128)(2,1)S(1)}, u32[]{:S(2)}, u32[]{:S(2)}) collective-permute-start(bf16[40,3072]{1,0:T(8,128)(2,1)S(1)} %add_convert_fusion.6), channel_id=1, source_target_pairs={{0,24},{1,9},{2,26},{3,11},{4,28},{5,13},{6,30},{7,15},{8,16},{9,1... | collective-permute-start | bytes 737288 | tf_op jit(solution)/shard_map/ppermute | solution.py:235
  111.6 12.3 %collective-permute-start.16 = (bf16[768,384]{1,0:T(8,128)(2,1)S(1)}, bf16[768,384]{1,0:T(8,128)(2,1)S(1)}, u32[]{:S(2)}, u32[]{:S(2)}) collective-permute-start(bf16[768,384]{1,0:T(8,128)(2,1)S(1)} %add_convert_fusion.1), channel_id=1, source_target_pairs={{0,32},{1,225},{2,34},{3,227},{4,36},{5,229},{6,38},{7,231},{8,40}... | collective-permute-start | bytes 1769480 | tf_op jit(solution)/shard_map/ppermute | solution.py:235
  119.7 9.4 %collective-permute-start.15 = (bf16[40,3072]{1,0:T(8,128)(2,1)S(1)}, bf16[40,3072]{1,0:T(8,128)(2,1)S(1)}, u32[]{:S(2)}, u32[]{:S(2)}) collective-permute-start(bf16[40,3072]{1,0:T(8,128)(2,1)S(1)} %fusion.9), channel_id=1, source_target_pairs={{0,6},{1,3},{2,4},{3,1},{4,2},{5,7},{6,0},{7,5},{8,14},{9,11},{10,... | collective-permute-start | bytes 737288 | tf_op jit(solution)/shard_map/ppermute | solution.py:235
  124.1 13.5 %collective-permute-start.18 = (bf16[768,384]{1,0:T(8,128)(2,1)S(1)}, bf16[768,384]{1,0:T(8,128)(2,1)}, u32[]{:S(2)}, u32[]{:S(2)}) collective-permute-start(bf16[768,384]{1,0:T(8,128)(2,1)S(1)} %add_convert_fusion), channel_id=1, source_target_pairs={{0,224},{1,33},{2,226},{3,35},{4,228},{5,37},{6,230},{7,39},{8,232... | collective-permute-start | bytes 1769480 | tf_op jit(solution)/shard_map/ppermute | solution.py:235
  129.1 11.5 %collective-permute-start.17 = (bf16[80,3072]{1,0:T(8,128)(2,1)S(1)}, bf16[80,3072]{1,0:T(8,128)(2,1)}, u32[]{:S(2)}, u32[]{:S(2)}) collective-permute-start(bf16[80,3072]{1,0:T(8,128)(2,1)S(1)} %pad_maximum_fusion.2), channel_id=1, source_target_pairs={{0,2},{1,7},{2,0},{3,5},{4,6},{5,3},{6,4},{7,1},{8,10},{9,15},{10,... | collective-permute-start | bytes 1474568 | tf_op jit(solution)/shard_map/ppermute | solution.py:235
  138.7 8.6 %collective-permute-start.20 = (bf16[384,384]{1,0:T(8,128)(2,1)S(1)}, bf16[384,384]{1,0:T(8,128)(2,1)S(1)}, u32[]{:S(2)}, u32[]{:S(2)}) collective-permute-start(bf16[384,384]{1,0:T(8,128)(2,1)S(1)} %add_convert_fusion.5), channel_id=1, source_target_pairs={{0,32},{1,225},{2,34},{3,227},{4,36},{5,229},{6,38},{7,231},{8,40}... | collective-permute-start | bytes 884744 | tf_op jit(solution)/shard_map/ppermute | solution.py:235
  141.8 14.4 %collective-permute-start.19 = (bf16[160,3072]{1,0:T(8,128)(2,1)S(1)}, bf16[160,3072]{1,0:T(8,128)(2,1)S(1)}, u32[]{:S(2)}, u32[]{:S(2)}) collective-permute-start(bf16[160,3072]{1,0:T(8,128)(2,1)S(1)} %pad_maximum_fusion.1), channel_id=1, source_target_pairs={{0,1},{1,0},{2,3},{3,2},{4,5},{5,4},{6,7},{7,6},{8,9},{9,8},{10,11... | collective-permute-start | bytes 2949128 | tf_op jit(solution)/shard_map/ppermute | solution.py:235
  148.4 7.0 %collective-permute-start.21 = (bf16[192,384]{1,0:T(8,128)(2,1)S(1)}, bf16[192,384]{1,0:T(8,128)(2,1)S(1)}, u32[]{:S(2)}, u32[]{:S(2)}) collective-permute-start(bf16[192,384]{1,0:T(8,128)(2,1)S(1)} %broadcast_select_fusion.4), channel_id=1, source_target_pairs={{0,256},{1,257},{2,258},{3,259},{4,260},{5,261},{6,262},{7,263},{8... | collective-permute-start | bytes 442376 | tf_op jit(solution)/shard_map/ppermute | solution.py:235
  156.3 1.3 copy-start.14

commit v3 on v2

--- a/solution.py
+++ b/solution.py
@@ -76,7 +76,7 @@
 
 def head_kernel(places, normed, cot, q_gain, k_gain, *refs):
     blocks, refs = refs[:10], refs[10:]
-    grad_ref, kept_ref, sent_ref, weights_out, weights, sems, out_sem = refs
+    grad_ref, kept_ref, next_ref, sent_ref, weights, sems = refs
     depth = blocks[0].shape[0]
     copies = []
     for ref in blocks:
@@ -94,8 +94,6 @@
         copy.start()
     for copy in copies:
         copy.wait()
-    out_copy = pltpu.make_async_copy(weights, weights_out, out_sem)
-    out_copy.start()
     width = weights.shape[1]
     total = None
     for first in range(0, weights.shape[0], width):
@@ -107,38 +105,37 @@
     core, outer, inner = places[16], places[17], places[18]
     half = grads.shape[0] // 2
     low, high = grads[:half], grads[half:]
-    kept = swap_blocks(jnp.where(core == 0, low, high), outer, inner)
+    kept = swap_blocks(jnp.where(core == 0, low, high), outer, inner).astype(jnp.bfloat16)
     sent = swap_blocks(jnp.where(core == 0, high, low), inner, outer).astype(jnp.bfloat16)
-    kept_ref[...] = kept.astype(jnp.bfloat16)
-
     for first in range(0, weights.shape[0], width):
         at = pl.ds(first, width)
         sent_ref[:, at] = contract(sent, weights[at, :], 1, 1).astype(jnp.bfloat16)
-    out_copy.wait()
+        term = contract(kept, weights[at, :], 1, 1).astype(jnp.bfloat16)
+        kept_ref[:, at] = term[: half // 2]
+        next_ref[:, at] = term[half // 2 :]
 
 
 def run_head(places, normed, cot, q_gain, k_gain, blocks):
     tokens, features = normed.shape
     width = blocks[0].shape[1]
     in_vmem = pl.BlockSpec(memory_space=pltpu.VMEM)
-    anywhere = pl.BlockSpec(memory_space=pl.ANY)
+    in_hbm = pl.BlockSpec(memory_space=pltpu.HBM)
     like = lambda *shape: jax.ShapeDtypeStruct(shape, jnp.bfloat16)
     return pl.pallas_call(
         head_kernel,
         out_shape=(
             like(tokens, width),
-            like(tokens // 2, width),
+            like(tokens // 4, features),
+            like(tokens // 4, features),
             like(tokens // 2, features),
-            like(features, width),
-        ),
-        in_specs=[pl.BlockSpec(memory_space=pltpu.SMEM)] + [in_vmem] * 4 + [anywhere] * len(blocks),
-        out_specs=(in_vmem, in_vmem, in_vmem, anywhere),
+        ),
+        in_specs=[pl.BlockSpec(memory_space=pltpu.SMEM)] + [in_vmem] * 4 + [in_hbm] * len(blocks),
+        out_specs=(in_vmem,) * 4,
         scratch_shapes=[
             pltpu.VMEM((features, width), jnp.bfloat16),
             pltpu.SemaphoreType.DMA((16,)),
-            pltpu.SemaphoreType.DMA,
         ],
-        compiler_params=pltpu.CompilerParams(vmem_limit_bytes=40 * 2**20),
+        compiler_params=pltpu.CompilerParams(vmem_limit_bytes=16 * 2**20),
         cost_estimate=pl.CostEstimate(
             flops=3 * tokens * features * width, bytes_accessed=8 * 2**20, transcendentals=200000
         ),
@@ -158,7 +155,7 @@
         out_shape=jax.ShapeDtypeStruct(inputs.shape, jnp.bfloat16),
         in_specs=[in_vmem, in_vmem],
         out_specs=in_vmem,
-        compiler_params=pltpu.CompilerParams(vmem_limit_bytes=24 * 2**20),
+        compiler_params=pltpu.CompilerParams(vmem_limit_bytes=12 * 2**20),
         cost_estimate=pl.CostEstimate(
             flops=8 * inputs.size, bytes_accessed=4 * inputs.size, transcendentals=0
         ),
@@ -166,25 +163,14 @@
     )(inputs, gain)
 
 
-def terms_kernel(places, normed, grads, out, terms, sems):
-    features, width = terms.shape
+def terms_kernel(places, normed, grads, out):
+    features, width = out.shape
     depth = features // (Y_LO * Z)
-    copies = []
     for first in range(0, features, width):
-        at = pl.ds(first, width)
-        terms[at, :] = contract(normed[:, at], grads[...], 0, 0).astype(terms.dtype)
-        for block in range(first // depth, (first + width) // depth):
-            to = pl.multiple_of(places[block] * depth, depth)
-            copies.append(
-                pltpu.make_async_copy(
-                    terms.at[pl.ds(block * depth, depth), :],
-                    out.at[pl.ds(to, depth), :],
-                    sems.at[block],
-                )
-            )
-            copies[-1].start()
-    for copy in copies:
-        copy.wait()
+        term = contract(normed[:, pl.ds(first, width)], grads[...], 0, 0).astype(out.dtype)
+        for part in range(width // depth):
+            to = pl.multiple_of(places[first // depth + part] * depth, depth)
+            out[pl.ds(to, depth), :] = term[part * depth : (part + 1) * depth]
 
 
 def run_terms(places, normed, grads):
@@ -195,17 +181,34 @@
         terms_kernel,
         out_shape=jax.ShapeDtypeStruct((features, width), jnp.bfloat16),
         in_specs=[pl.BlockSpec(memory_space=pltpu.SMEM), in_vmem, in_vmem],
-        out_specs=pl.BlockSpec(memory_space=pl.ANY),
-        scratch_shapes=[
-            pltpu.VMEM((features, width), jnp.bfloat16),
-            pltpu.SemaphoreType.DMA((Y_LO * Z,)),
-        ],
-        compiler_params=pltpu.CompilerParams(vmem_limit_bytes=32 * 2**20),
+        out_specs=in_vmem,
+        compiler_params=pltpu.CompilerParams(vmem_limit_bytes=12 * 2**20),
         cost_estimate=pl.CostEstimate(
             flops=2 * tokens * features * width, bytes_accessed=5 * 2**20, transcendentals=0
         ),
         name="terms",
     )(places, normed, grads)
+
+
+def back_kernel(left, right, inputs, gain, out):
+    unit, inverse = normalize(inputs[...].astype(jnp.float32))
+    grads = (left[...].astype(jnp.float32) + right[...].astype(jnp.float32)) * gain[...]
+    out[...] = norm_backward(grads, unit, inverse).astype(out.dtype)
+
+
+def run_back(left, right, inputs, gain):
+    in_vmem = pl.BlockSpec(memory_space=pltpu.VMEM)
+    return pl.pallas_call(
+        back_kernel,
+        out_shape=jax.ShapeDtypeStruct(inputs.shape, jnp.bfloat16),
+        in_specs=[in_vmem] * 4,
+        out_specs=in_vmem,
+        compiler_params=pltpu.CompilerParams(vmem_limit_bytes=8 * 2**20),
+        cost_estimate=pl.CostEstimate(
+            flops=20 * inputs.size, bytes_accessed=8 * inputs.size, transcendentals=0
+        ),
+        name="back",
+    )(left, right, inputs, gain)
 
 
 def pairs_of(partner):
@@ -271,8 +274,8 @@
     return lax.optimization_barrier((values, earlier))[0]
 
 
-def join(own, got, place):
-    return jnp.concatenate([jnp.where(place == 0, own, got), jnp.where(place == 0, got, own)])
+def join(own, got, first):
+    return jnp.concatenate([jnp.where(first, own, got), jnp.where(first, got, own)])
 
 
 def per_device(inputs, ln_gain, w_qkv, q_gain, k_gain, cotangent):
@@ -288,61 +291,86 @@
         + [(1 - y_lo) * Z + at for at in z_places]
         + [core, outer, inner]
     ).astype(jnp.int32)
+    steps = [(at - z) * z_way % Z for at in range(Z)]
+    orders = [
+        jnp.where(
+            step < 2,
+            step,
+            jnp.where(step < 4, step + 2, jnp.where(step < 6, 11 - step, 9 - step)),
+        )
+        for step in steps
+    ]
+    term_places = jnp.stack([Y_LO * order + y for y in range(Y_LO) for order in orders])
+    tokens, features = inputs.shape
+    rows = tokens // 8
+    own_rows = lax.dynamic_slice_in_dim(
+        inputs, ((core * 2 + outer) * 2 + inner) * rows, rows, 0
+    )
+    w_qkv, places, term_places, own_rows, first_core, first_outer, first_inner, first_y = (
+        lax.optimization_barrier(
+            (
+                w_qkv,
+                places,
+                term_places.astype(jnp.int32),
+                own_rows,
+                core == 0,
+                outer == 0,
+                inner == 0,
+                y_lo == 0,
+            )
+        )
+    )
 
     other = swap(w_qkv, by_y_lo)
     blocks = along_z(w_qkv) + along_z(other)
     normed = run_norm(inputs, ln_gain.reshape(1, -1))
-    grad_qkv, kept, sent, weights = run_head(
+    grad_qkv, part, other, sent = run_head(
         places, normed, cotangent, q_gain.reshape(1, -1), k_gain.reshape(1, -1), blocks
     )
 
-    got = swap(sent, by_core)
-    part = contract(kept, weights, 1, 1)
-    rows = part.shape[0] // 2
-    part, other = add(part[:rows], got[:rows]), add(part[rows:], got[rows:])
-    steps = (jnp.arange(Z) - z) * z_way % Z
-    order = jnp.array([Z_STEPS.index(step if step in Z_STEPS else step - Z) for step in range(Z)])
-    z_order = order[steps]
-    term_places = jnp.stack([z_order * Y_LO, z_order * Y_LO + 1]).reshape(-1).astype(jnp.int32)
-    terms = run_terms(term_places, normed, after(grad_qkv, other))
+    terms = run_terms(term_places, normed, grad_qkv)
     depth = terms.shape[0] // Z
     zero, one, two, three, four = jnp.split(terms, [depth, 2 * depth, 4 * depth, 6 * depth])
-    part = add(part, swap(other, by_x(1)))
-    got = swap(four, by_z(-1))
+    got = swap(sent, by_core)
+    rows = part.shape[0]
+    other = after(add(other, got[rows:]), terms)
+    part = add(part, after(got, other)[:rows])
+    got = swap(other, by_x(1))
+    across = swap(four, by_z(-1))
+    part = add(part, got)
     rows = rows // 2
-    part, other = part[:rows], after(part[rows:], four)
-    part = add(part, swap(other, by_x(-1)))
-
-    three = add(three, after(got, part))
-    got = swap(three, by_z(1))
-    part = add(part, swap(part, by_y_hi(1)))
-    part = after(part, three)
-    grad_normed = part.astype(jnp.float32) + swap(part, by_y_hi(-1)).astype(jnp.float32)
-    first = ((core * 2 + outer) * 2 + inner) * rows
-    own_unit, own_inverse = normalize(
-        lax.dynamic_slice_in_dim(inputs, first, rows, 0).astype(jnp.float32)
-    )
-    own = norm_backward(grad_normed * ln_gain, own_unit, own_inverse).astype(jnp.bfloat16)
-
-    two = add(two, after(got, own))
-    got = swap(two, by_z(-1))
-    own = after(join(own, swap(own, by_x(-1)), inner), two)
-
-    got = after(got, own)
-    zero, one = add(zero, got[:depth]), add(one, got[depth:])
-    got = swap(one, by_z(1))
-    own = after(join(own, swap(own, by_x(1)), outer), one)
-
-    zero = add(zero, after(got, own))
+    part, other = part[:rows], part[rows:]
+
+    three = add(three, after(across, other))
+    got = swap(other, by_x(-1))
+    across = swap(three, by_z(1))
+    part = after(add(part, got), three)
+
+    two = add(two, after(across, part))
+    got = swap(part, by_y_hi(1))
+    across = swap(two, by_z(-1))
+    part = after(add(part, got), two)
+
+    across = after(across, part)
+    zero, one = add(zero, across[:depth]), add(one, across[depth:])
+    got = swap(part, by_y_hi(-1))
+    across = swap(one, by_z(1))
+    own = after(run_back(part, got, own_rows, ln_gain.reshape(1, -1)), one)
+
+    zero = add(zero, after(across, own))
     depth = zero.shape[0] // 2
     low, high = zero[:depth], zero[depth:]
-    share = swap(jnp.where(y_lo == 0, high, low), by_y_lo)
+    got = swap(own, by_x(-1))
+    across = swap(jnp.where(first_y, high, low), by_y_lo)
+    own = after(join(own, got, first_inner), zero)
+
+    across = after(across, own).astype(jnp.float32)
+    grad_w_qkv = jnp.where(first_y, low, high).astype(jnp.float32) + across
+    got = swap(own, by_x(1))
+    own = after(join(own, got, first_outer), grad_w_qkv)
+
     got = swap(own, by_core)
-    grad_input = lax.dynamic_update_slice_in_dim(
-        jnp.concatenate([own, own]), got, (1 - core) * own.shape[0], 0
-    )
-    grad_w_qkv = jnp.where(y_lo == 0, low, high).astype(jnp.float32) + share.astype(jnp.float32)
-    return (grad_input, grad_w_qkv)
+    return (join(own, got, first_core), grad_w_qkv)
 
 
 def solution(mesh):

time: 159 us -> 145 us (0.912)
  the two profiles are of different devices: /device:TPU:16 before, /device:TPU:1 now
where the time goes in v3:
time: 145 us
  starting transfers between devices  82.1 us (57%)
  waiting for transfers between devices  42.5 us (29%)
  Pallas kernels  12.8 us (9%)
  other arithmetic  4.41 us (3%)
  between operations  1.68 us (1%)
    ppermute x22, starting transfers between devices, swap(): return lax.ppermute(values, AXES, pairs_of(partner))  82.1 us
    ppermute x22, waiting for transfers between devices, swap(): return lax.ppermute(values, AXES, pairs_of(partner))  42.5 us
    pallas_call x1, Pallas kernels, run_head(): pl.pallas_call(head_kernel, out_shape=(like(tokens, width), like(tokens /...  8.8 us
  transfers between devices with their start and end apart: 22, of which 15 were waited for; matrix products, arithmetic and copies ran while one was open for 2% of the time, Pallas kernels for 3%

profile of v3, /device:TPU:1, one launch (start us, length us, event | category | flops | bytes accessed | tf_op | source)
XLA Modules:
  0.0 144.7 jit_solution(14363407631597776017)
XLA Ops:
  1.3 1.0 constant_dynamic-slice_fusion.inputs
  2.2 0.1 stack.147.places
  2.4 0.1 stack.130.places
  2.5 4.0 %collective-permute-start.4 = (bf16[192,384]{1,0:T(8,128)(2,1)}, bf16[192,384]{1,0:T(8,128)(2,1)S(1)}, u32[]{:S(2)}, u32[]{:S(2)}) collective-permute-start(bf16[192,384]{1,0:T(8,128)(2,1)} %refs_0_), channel_id=1, source_target_pairs={{0,256},{1,257},{2,258},{3,259},{4,260},{5,261},{6,262},{7,263},{8... | collective-permute-start | bytes 442376 | tf_op jit(solution)/shard_map/ppermute | solution.py:238
  6.5 10.7 %collective-permute-start = (bf16[192,384]{1,0:T(8,128)(2,1)}, bf16[192,384]{1,0:T(8,128)(2,1)S(1)}, u32[]{:S(2)}, u32[]{:S(2)}) collective-permute-start(bf16[192,384]{1,0:T(8,128)(2,1)} %refs_0_), channel_id=1, source_target_pairs={{0,32},{1,225},{2,34},{3,227},{4,36},{5,229},{6,38},{7,231},{8,40}... | collective-permute-start | bytes 442376 | tf_op jit(solution)/shard_map/ppermute | solution.py:238
  17.2 3.6 %collective-permute-start.5 = (bf16[192,384]{1,0:T(8,128)(2,1)S(1)}, bf16[192,384]{1,0:T(8,128)(2,1)S(1)}, u32[]{:S(2)}, u32[]{:S(2)}) collective-permute-start(bf16[192,384]{1,0:T(8,128)(2,1)S(1)} %collective-permute-done.4.refs_5_), channel_id=1, source_target_pairs={{0,32},{1,225},{2,34},{3,227},{4,36},{5,229},{6,38},{7,231},{8,40}... | collective-permute-start | bytes 442376 | tf_op jit(solution)/shard_map/ppermute | solution.py:238
  20.8 0.9 pad_maximum_fusion.3
  21.7 1.9 %collective-permute-start.1 = (bf16[384,384]{1,0:T(8,128)(2,1)S(1)}, bf16[384,384]{1,0:T(8,128)(2,1)S(1)}, u32[]{:S(2)}, u32[]{:S(2)}) collective-permute-start(bf16[384,384]{1,0:T(8,128)(2,1)S(1)} %pad_maximum_fusion.3), channel_id=1, source_target_pairs={{0,224},{1,33},{2,226},{3,35},{4,228},{5,37},{6,230},{7,39},{8,232... | collective-permute-start | bytes 884744 | tf_op jit(solution)/shard_map/ppermute | solution.py:238
  23.7 0.6 collective-permute-done.5.refs_6_
  24.3 2.7 %collective-permute-start.6 = (bf16[384,384]{1,0:T(8,128)(2,1)S(1)}, bf16[384,384]{1,0:T(8,128)(2,1)S(1)}, u32[]{:S(2)}, u32[]{:S(2)}) collective-permute-start(bf16[384,384]{1,0:T(8,128)(2,1)S(1)} %pad_maximum_fusion.4), channel_id=1, source_target_pairs={{0,224},{1,33},{2,226},{3,35},{4,228},{5,37},{6,230},{7,39},{8,232... | collective-permute-start | bytes 884744 | tf_op jit(solution)/shard_map/ppermute | solution.py:238
  27.1 2.4 %collective-permute-done.1.refs_2_ = bf16[384,384]{1,0:T(8,128)(2,1)S(1)} collective-permute-done((bf16[384,384]{1,0:T(8,128)(2,1)S(1)}, bf16[384,384]{1,0:T(8,128)(2,1)S(1)}, u32[]{:S(2)}, u32[]{:S(2)}) %collective-permute-start.1) | collective-permute-done | bytes 294944 | tf_op jit(solution)/shard_map/ppermute | solution.py:238
  29.5 3.7 %collective-permute-start.2 = (bf16[384,384]{1,0:T(8,128)(2,1)S(1)}, bf16[384,384]{1,0:T(8,128)(2,1)S(1)}, u32[]{:S(2)}, u32[]{:S(2)}) collective-permute-start(bf16[384,384]{1,0:T(8,128)(2,1)S(1)} %collective-permute-done.1.refs_2_), channel_id=1, source_target_pairs={{0,32},{1,225},{2,34},{3,227},{4,36},{5,229},{6,38},{7,231},{8,40}... | collective-permute-start | bytes 884744 | tf_op jit(solution)/shard_map/ppermute | solution.py:238
  33.2 3.1 %collective-permute-start.7 = (bf16[384,384]{1,0:T(8,128)(2,1)S(1)}, bf16[384,384]{1,0:T(8,128)(2,1)S(1)}, u32[]{:S(2)}, u32[]{:S(2)}) collective-permute-start(bf16[384,384]{1,0:T(8,128)(2,1)S(1)} %collective-permute-done.6.refs_7_), channel_id=1, source_target_pairs={{0,32},{1,225},{2,34},{3,227},{4,36},{5,229},{6,38},{7,231},{8,40}... | collective-permute-start | bytes 884744 | tf_op jit(solution)/shard_map/ppermute | solution.py:238
  36.3 2.6 %collective-permute-done.2.refs_3_ = bf16[384,384]{1,0:T(8,128)(2,1)S(1)} collective-permute-done((bf16[384,384]{1,0:T(8,128)(2,1)S(1)}, bf16[384,384]{1,0:T(8,128)(2,1)S(1)}, u32[]{:S(2)}, u32[]{:S(2)}) %collective-permute-start.2) | collective-permute-done | bytes 294944 | tf_op jit(solution)/shard_map/ppermute | solution.py:238
  39.0 1.9 %collective-permute-start.3 = (bf16[384,384]{1,0:T(8,128)(2,1)S(1)}, bf16[384,384]{1,0:T(8,128)(2,1)S(1)}, u32[]{:S(2)}, u32[]{:S(2)}) collective-permute-start(bf16[384,384]{1,0:T(8,128)(2,1)S(1)} %collective-permute-done.2.refs_3_), channel_id=1, source_target_pairs={{0,224},{1,33},{2,226},{3,35},{4,228},{5,37},{6,230},{7,39},{8,232... | collective-permute-start | bytes 884744 | tf_op jit(solution)/shard_map/ppermute | solution.py:238
  40.9 1.2 collective-permute-done.7.refs_8_
  42.1 2.1 %collective-permute-start.8 = (bf16[384,384]{1,0:T(8,128)(2,1)S(1)}, bf16[384,384]{1,0:T(8,128)(2,1)S(1)}, u32[]{:S(2)}, u32[]{:S(2)}) collective-permute-start(bf16[384,384]{1,0:T(8,128)(2,1)S(1)} %collective-permute-done.7.refs_8_), channel_id=1, source_target_pairs={{0,224},{1,33},{2,226},{3,35},{4,228},{5,37},{6,230},{7,39},{8,232... | collective-permute-start | bytes 884744 | tf_op jit(solution)/shard_map/ppermute | solution.py:238
  44.3 0.0 copy-start.1
  44.3 0.0 copy-start.2
  44.3 0.0 copy-start.4
  44.3 0.0 copy-start.5
  44.3 1.3 norm.1.normed
  45.6 3.0 %collective-permute-done.3.refs_4_ = bf16[384,384]{1,0:T(8,128)(2,1)S(1)} collective-permute-done((bf16[384,384]{1,0:T(8,128)(2,1)S(1)}, bf16[384,384]{1,0:T(8,128)(2,1)S(1)}, u32[]{:S(2)}, u32[]{:S(2)}) %collective-permute-start.3) | collective-permute-done | bytes 294944 | tf_op jit(solution)/shard_map/ppermute | solution.py:238
  48.6 2.9 %collective-permute-done.8.refs_9_ = bf16[384,384]{1,0:T(8,128)(2,1)S(1)} collective-permute-done((bf16[384,384]{1,0:T(8,128)(2,1)S(1)}, bf16[384,384]{1,0:T(8,128)(2,1)S(1)}, u32[]{:S(2)}, u32[]{:S(2)}) %collective-permute-start.8) | collective-permute-done | bytes 294944 | tf_op jit(solution)/shard_map/ppermute | solution.py:238
  51.5 8.8 %head.1 = (bf16[320,384]{1,0:T(8,128)(2,1)S(1)}, bf16[80,3072]{1,0:T(8,128)(2,1)S(1)}, bf16[80,3072]{1,0:T(8,128)(2,1)S(1)}, bf16[160,3072]{1,0:T(8,128)(2,1)S(1)}) custom-call(s32[19]{0:T(128)S(1)} %stack.130.places, bf16[320,3072]{1,0:T(8,128)(2,1)S(1)} %norm.1.normed, bf16[320,128]{1,0:T(8,128)(2,1)S(1)} %copy-done.2, f32[1,128]{1,0:T(1,128)S(1)} %bitcast.40, ...), custom_call_target="tpu_custom_call" | custom-call | flops 1132462080 | bytes 8388608 | tf_op jit(solution)/shard_map/head/pallas_call | solution.py:124
  60.3 7.9 %collective-permute-start.9 = (bf16[160,3072]{1,0:T(8,128)(2,1)S(1)}, bf16[160,3072]{1,0:T(8,128)(2,1)S(1)}, u32[]{:S(2)}, u32[]{:S(2)}) collective-permute-start(bf16[160,3072]{1,0:T(8,128)(2,1)S(1)} %get-tuple-element.32), channel_id=1, source_target_pairs={{0,1},{1,0},{2,3},{3,2},{4,5},{5,4},{6,7},{7,6},{8,9},{9,8},{10,11... | collective-permute-start | bytes 2949128 | tf_op jit(solution)/shard_map/ppermute | solution.py:238
  68.2 2.2 %terms.1 = bf16[3072,384]{1,0:T(8,128)(2,1)S(1)} custom-call(s32[16]{0:T(128)S(1)} %stack.147.places, bf16[320,3072]{1,0:T(8,128)(2,1)S(1)} %norm.1.normed, bf16[320,384]{1,0:T(8,128)(2,1)S(1)} %get-tuple-element.35.grads), custom_call_target="tpu_custom_call" | custom-call | flops 754974720 | bytes 5242880 | tf_op jit(solution)/shard_map/terms/pallas_call | solution.py:180
  70.4 0.1 add_convert_fusion.4
  70.6 4.4 %collective-permute-start.10 = (bf16[80,3072]{1,0:T(8,128)(2,1)S(1)}, bf16[80,3072]{1,0:T(8,128)(2,1)S(1)}, u32[]{:S(2)}, u32[]{:S(2)}) collective-permute-start(bf16[80,3072]{1,0:T(8,128)(2,1)S(1)} %add_convert_fusion.4), channel_id=1, source_target_pairs={{0,2},{1,7},{2,0},{3,5},{4,6},{5,3},{6,4},{7,1},{8,10},{9,15},{10,... | collective-permute-start | bytes 1474568 | tf_op jit(solution)/shard_map/ppermute | solution.py:238
  75.0 0.1 split.21
  75.0 1.9 %collective-permute-start.12 = (bf16[768,384]{1,0:T(8,128)(2,1)S(1)}, bf16[768,384]{1,0:T(8,128)(2,1)S(1)}, u32[]{:S(2)}, u32[]{:S(2)}) collective-permute-start(bf16[768,384]{1,0:T(8,128)(2,1)S(1)} %split.21), channel_id=1, source_target_pairs={{0,224},{1,33},{2,226},{3,35},{4,228},{5,37},{6,230},{7,39},{8,232... | collective-permute-start | bytes 1769480 | tf_op jit(solution)/shard_map/ppermute | solution.py:238
  77.0 4.7 %collective-permute-done.10 = bf16[80,3072]{1,0:T(8,128)(2,1)S(1)} collective-permute-done((bf16[80,3072]{1,0:T(8,128)(2,1)S(1)}, bf16[80,3072]{1,0:T(8,128)(2,1)S(1)}, u32[]{:S(2)}, u32[]{:S(2)}) %collective-permute-start.10) | collective-permute-done | bytes 491552 | tf_op jit(solution)/shard_map/ppermute | solution.py:238
  81.6 0.2 add_convert_fusion.2
  81.9 1.9 %collective-permute-start.11 = (bf16[40,3072]{1,0:T(8,128)(2,1)S(1)}, bf16[40,3072]{1,0:T(8,128)(2,1)S(1)}, u32[]{:S(2)}, u32[]{:S(2)}) collective-permute-start(bf16[40,3072]{1,0:T(8,128)(2,1)S(1)} %slice.34), channel_id=1, source_target_pairs={{0,6},{1,3},{2,4},{3,1},{4,2},{5,7},{6,0},{7,5},{8,14},{9,11},{10,... | collective-permute-start | bytes 737288 | tf_op jit(solution)/shard_map/ppermute | solution.py:238
  83.8 2.2 %collective-permute-done.12 = bf16[768,384]{1,0:T(8,128)(2,1)S(1)} collective-permute-done((bf16[768,384]{1,0:T(8,128)(2,1)S(1)}, bf16[768,384]{1,0:T(8,128)(2,1)S(1)}, u32[]{:S(2)}, u32[]{:S(2)}) %collective-permute-start.12) | collective-permute-done | bytes 589856 | tf_op jit(solution)/shard_map/ppermute | solution.py:238
  86.0 0.1 add_convert_fusion.1
  86.1 1.9 %collective-permute-start.14 = (bf16[768,384]{1,0:T(8,128)(2,1)S(1)}, bf16[768,384]{1,0:T(8,128)(2,1)S(1)}, u32[]{:S(2)}, u32[]{:S(2)}) collective-permute-start(bf16[768,384]{1,0:T(8,128)(2,1)S(1)} %add_convert_fusion.1), channel_id=1, source_target_pairs={{0,32},{1,225},{2,34},{3,227},{4,36},{5,229},{6,38},{7,231},{8,40}... | collective-permute-start | bytes 1769480 | tf_op jit(solution)/shard_map/ppermute | solution.py:238
  88.0 1.1 collective-permute-done.11
  89.1 0.1 add_convert_fusion.9
  89.2 5.5 %collective-permute-start.13 = (bf16[40,3072]{1,0:T(8,128)(2,1)S(1)}, bf16[40,3072]{1,0:T(8,128)(2,1)S(1)}, u32[]{:S(2)}, u32[]{:S(2)}) collective-permute-start(bf16[40,3072]{1,0:T(8,128)(2,1)S(1)} %add_convert_fusion.9), channel_id=1, source_target_pairs={{0,8},{1,25},{2,10},{3,27},{4,12},{5,29},{6,14},{7,31},{8,0},{9,17... | collective-permute-start | bytes 737288 | tf_op jit(solution)/shard_map/ppermute | solution.py:238
  94.7 3.4 %collective-permute-done.14 = bf16[768,384]{1,0:T(8,128)(2,1)S(1)} collective-permute-done((bf16[768,384]{1,0:T(8,128)(2,1)S(1)}, bf16[768,384]{1,0:T(8,128)(2,1)S(1)}, u32[]{:S(2)}, u32[]{:S(2)}) %collective-permute-start.14) | collective-permute-done | bytes 589856 | tf_op jit(solution)/shard_map/ppermute | solution.py:238
  98.1 0.1 add_convert_fusion
  98.2 1.9 %collective-permute-start.16 = (bf16[768,384]{1,0:T(8,128)(2,1)S(1)}, bf16[768,384]{1,0:T(8,128)(2,1)S(1)}, u32[]{:S(2)}, u32[]{:S(2)}) collective-permute-start(bf16[768,384]{1,0:T(8,128)(2,1)S(1)} %add_convert_fusion), channel_id=1, source_target_pairs={{0,224},{1,33},{2,226},{3,35},{4,228},{5,37},{6,230},{7,39},{8,232... | collective-permute-start | bytes 1769480 | tf_op jit(solution)/shard_map/ppermute | solution.py:238
  100.2 0.0 collective-permute-done.13
  100.2 0.1 add_convert_fusion.8.left
  100.3 4.9 %collective-permute-start.15 = (bf16[40,3072]{1,0:T(8,128)(2,1)S(1)}, bf16[40,3072]{1,0:T(8,128)(2,1)S(1)}, u32[]{:S(2)}, u32[]{:S(2)}) collective-permute-start(bf16[40,3072]{1,0:T(8,128)(2,1)S(1)} %add_convert_fusion.8.left), channel_id=1, source_target_pairs={{0,24},{1,9},{2,26},{3,11},{4,28},{5,13},{6,30},{7,15},{8,16},{9,1... | collective-permute-start | bytes 737288 | tf_op jit(solution)/shard_map/ppermute | solution.py:238
  105.1 6.5 %collective-permute-done.15.right = bf16[40,3072]{1,0:T(8,128)(2,1)S(1)} collective-permute-done((bf16[40,3072]{1,0:T(8,128)(2,1)S(1)}, bf16[40,3072]{1,0:T(8,128)(2,1)S(1)}, u32[]{:S(2)}, u32[]{:S(2)}) %collective-permute-start.15) | collective-permute-done | bytes 245792 | tf_op jit(solution)/shard_map/ppermute | solution.py:238
  111.7 0.4 back.1
  112.1 0.1 add_convert_fusion.7
  112.2 1.9 %collective-permute-start.17 = (bf16[40,3072]{1,0:T(8,128)(2,1)S(1)}, bf16[40,3072]{1,0:T(8,128)(2,1)S(1)}, u32[]{:S(2)}, u32[]{:S(2)}) collective-permute-start(bf16[40,3072]{1,0:T(8,128)(2,1)S(1)} %back.1), channel_id=1, source_target_pairs={{0,6},{1,3},{2,4},{3,1},{4,2},{5,7},{6,0},{7,5},{8,14},{9,11},{10,... | collective-permute-start | bytes 737288 | tf_op jit(solution)/shard_map/ppermute | solution.py:238
  114.2 3.5 %collective-permute-start.18 = (bf16[384,384]{1,0:T(8,128)(2,1)S(1)}, bf16[384,384]{1,0:T(8,128)(2,1)S(1)}, u32[]{:S(2)}, u32[]{:S(2)}) collective-permute-start(bf16[384,384]{1,0:T(8,128)(2,1)S(1)} %add_convert_fusion.7), channel_id=1, source_target_pairs={{0,32},{1,225},{2,34},{3,227},{4,36},{5,229},{6,38},{7,231},{8,40}... | collective-permute-start | bytes 884744 | tf_op jit(solution)/shard_map/ppermute | solution.py:238
  117.6 1.6 %collective-permute-done.17 = bf16[40,3072]{1,0:T(8,128)(2,1)S(1)} collective-permute-done((bf16[40,3072]{1,0:T(8,128)(2,1)S(1)}, bf16[40,3072]{1,0:T(8,128)(2,1)S(1)}, u32[]{:S(2)}, u32[]{:S(2)}) %collective-permute-start.17) | collective-permute-done | bytes 245792 | tf_op jit(solution)/shard_map/ppermute | solution.py:238
  119.2 3.9 %collective-permute-done.18 = bf16[384,384]{1,0:T(8,128)(2,1)S(1)} collective-permute-done((bf16[384,384]{1,0:T(8,128)(2,1)S(1)}, bf16[384,384]{1,0:T(8,128)(2,1)S(1)}, u32[]{:S(2)}, u32[]{:S(2)}) %collective-permute-start.18) | collective-permute-done | bytes 294944 | tf_op jit(solution)/shard_map/ppermute | solution.py:238
  123.1 0.1 add_convert_fusion.5
  123.2 4.4 %collective-permute-start.19 = (bf16[80,3072]{1,0:T(8,128)(2,1)S(1)}, bf16[80,3072]{1,0:T(8,128)(2,1)S(1)}, u32[]{:S(2)}, u32[]{:S(2)}) collective-permute-start(bf16[80,3072]{1,0:T(8,128)(2,1)S(1)} %pad_maximum_fusion.2), channel_id=1, source_target_pairs={{0,2},{1,7},{2,0},{3,5},{4,6},{5,3},{6,4},{7,1},{8,10},{9,15},{10,... | collective-permute-start | bytes 1474568 | tf_op jit(solution)/shard_map/ppermute | solution.py:238
  127.7 1.9 %collective-permute-start.20 = (bf16[192,384]{1,0:T(8,128)(2,1)S(1)}, bf16[192,384]{1,0:T(8,128)(2,1)S(1)}, u32[]{:S(2)}, u32[]{:S(2)}) collective-permute-start(bf16[192,384]{1,0:T(8,128)(2,1)S(1)} %broadcast_select_fusion.6), channel_id=1, source_target_pairs={{0,256},{1,257},{2,258},{3,259},{4,260},{5,261},{6,262},{7,263},{8... | collective-permute-start | bytes 442376 | tf_op jit(solution)/shard_map/ppermute | solution.py:238
  129.6 4.3 %collective-permute-done.20 = bf16[192,384]{1,0:T(8,128)(2,1)S(1)} collective-permute-done((bf16[192,384]{1,0:T(8,128)(2,1)S(1)}, bf16[192,384]{1,0:T(8,128)(2,1)S(1)}, u32[]{:S(2)}, u32[]{:S(2)}) %collective-permute-start.20) | collective-permute-done | bytes 147488 | tf_op jit(solution)/shard_map/ppermute | solution.py:238
  133.8 0.8 convert_add_fusion
  134.6 0.1 broadcast_select_fusion.3
  134.7 0.1 pad_maximum_fusion.1
  134.8 6.3 %collective-permute-start.21 = (bf16[160,3072]{1,0:T(8,128)(2,1)S(1)}, bf16[160,3072]{1,0:T(8,128)(2,1)S(1)}, u32[]{:S(2)}, u32[]{:S(2)}) collective-permute-start(bf16[160,3072]{1,0:T(8,128)(2,1)S(1)} %pad_maximum_fusion.1), channel_id=1, source_target_pairs={{0,1},{1,0},{2,3},{3,2},{4,5},{5,4},{6,7},{7,6},{8,9},{9,8},{10,11... | collective-permute-start | bytes 2949128 | tf_op jit(solution)/shard_map/ppermute | solution.py:238
  141.0 2.2 %collective-permute-done.21 = bf16[160,3072]{1,0:T(8,128)(2,1)S(1)} collective-permute-done((bf16[160,3072]{1,0:T(8,128)(2,1)S(1)}, bf16[160,3072]{1,0:T(8,128)(2,1)S(1)}, u32[]{:S(2)}, u32[]{:S(2)}) %collective-permute-start.21) | collective-permute-done | bytes 983072 | tf_op jit(solution)/shard_map/ppermute | solution.py:238
  143.2 0.1 broadcast_select_fusion.1
  143.3 1.4 pad_maximum_fusion
  (19 shorter events, 0.2 us)
Async XLA Ops:
  0.6 43.6 %copy-start = (bf16[320,3072]{1,0:T(8,128)(2,1)S(1)}, bf16[320,3072]{1,0:T(8,128)(2,1)}, u32[]{:S(2)}) copy-start(bf16[320,3072]{1,0:T(8,128)(2,1)} %inputs.1) | copy-start | bytes 5898244
  0.6 43.6 %copy-start.3 = (f32[3072]{0:T(1024)S(1)}, f32[3072]{0:T(1024)}, u32[]{:S(2)}) copy-start(f32[3072]{0:T(1024)} %param.7) | copy-start | bytes 36868
  2.5 14.7 %collective-permute-start.4 = (bf16[192,384]{1,0:T(8,128)(2,1)}, bf16[192,384]{1,0:T(8,128)(2,1)S(1)}, u32[]{:S(2)}, u32[]{:S(2)}) collective-permute-start(bf16[192,384]{1,0:T(8,128)(2,1)} %refs_0_), channel_id=1, source_target_pairs={{0,256},{1,257},{2,258},{3,259},{4,260},{5,261},{6,262},{7,263},{8... | collective-permute-start | bytes 442376 | tf_op jit(solution)/shard_map/ppermute | solution.py:238
  6.5 14.3 %collective-permute-start = (bf16[192,384]{1,0:T(8,128)(2,1)}, bf16[192,384]{1,0:T(8,128)(2,1)S(1)}, u32[]{:S(2)}, u32[]{:S(2)}) collective-permute-start(bf16[192,384]{1,0:T(8,128)(2,1)} %refs_0_), channel_id=1, source_target_pairs={{0,32},{1,225},{2,34},{3,227},{4,36},{5,229},{6,38},{7,231},{8,40}... | collective-permute-start | bytes 442376 | tf_op jit(solution)/shard_map/ppermute | solution.py:238
  17.2 7.1 %collective-permute-start.5 = (bf16[192,384]{1,0:T(8,128)(2,1)S(1)}, bf16[192,384]{1,0:T(8,128)(2,1)S(1)}, u32[]{:S(2)}, u32[]{:S(2)}) collective-permute-start(bf16[192,384]{1,0:T(8,128)(2,1)S(1)} %collective-permute-done.4.refs_5_), channel_id=1, source_target_pairs={{0,32},{1,225},{2,34},{3,227},{4,36},{5,229},{6,38},{7,231},{8,40}... | collective-permute-start | bytes 442376 | tf_op jit(solution)/shard_map/ppermute | solution.py:238
  21.7 7.8 %collective-permute-start.1 = (bf16[384,384]{1,0:T(8,128)(2,1)S(1)}, bf16[384,384]{1,0:T(8,128)(2,1)S(1)}, u32[]{:S(2)}, u32[]{:S(2)}) collective-permute-start(bf16[384,384]{1,0:T(8,128)(2,1)S(1)} %pad_maximum_fusion.3), channel_id=1, source_target_pairs={{0,224},{1,33},{2,226},{3,35},{4,228},{5,37},{6,230},{7,39},{8,232... | collective-permute-start | bytes 884744 | tf_op jit(solution)/shard_map/ppermute | solution.py:238
  24.3 8.9 %collective-permute-start.6 = (bf16[384,384]{1,0:T(8,128)(2,1)S(1)}, bf16[384,384]{1,0:T(8,128)(2,1)S(1)}, u32[]{:S(2)}, u32[]{:S(2)}) collective-permute-start(bf16[384,384]{1,0:T(8,128)(2,1)S(1)} %pad_maximum_fusion.4), channel_id=1, source_target_pairs={{0,224},{1,33},{2,226},{3,35},{4,228},{5,37},{6,230},{7,39},{8,232... | collective-permute-start | bytes 884744 | tf_op jit(solution)/shard_map/ppermute | solution.py:238
  29.5 9.5 %collective-permute-start.2 = (bf16[384,384]{1,0:T(8,128)(2,1)S(1)}, bf16[384,384]{1,0:T(8,128)(2,1)S(1)}, u32[]{:S(2)}, u32[]{:S(2)}) collective-permute-start(bf16[384,384]{1,0:T(8,128)(2,1)S(1)} %collective-permute-done.1.refs_2_), channel_id=1, source_target_pairs={{0,32},{1,225},{2,34},{3,227},{4,36},{5,229},{6,38},{7,231},{8,40}... | collective-permute-start | bytes 884744 | tf_op jit(solution)/shard_map/ppermute | solution.py:238
  33.2 8.9 %collective-permute-start.7 = (bf16[384,384]{1,0:T(8,128)(2,1)S(1)}, bf16[384,384]{1,0:T(8,128)(2,1)S(1)}, u32[]{:S(2)}, u32[]{:S(2)}) collective-permute-start(bf16[384,384]{1,0:T(8,128)(2,1)S(1)} %collective-permute-done.6.refs_7_), channel_id=1, source_target_pairs={{0,32},{1,225},{2,34},{3,227},{4,36},{5,229},{6,38},{7,231},{8,40}... | collective-permute-start | bytes 884744 | tf_op jit(solution)/shard_map/ppermute | solution.py:238
  39.0 9.6 %collective-permute-start.3 = (bf16[384,384]{1,0:T(8,128)(2,1)S(1)}, bf16[384,384]{1,0:T(8,128)(2,1)S(1)}, u32[]{:S(2)}, u32[]{:S(2)}) collective-permute-start(bf16[384,384]{1,0:T(8,128)(2,1)S(1)} %collective-permute-done.2.refs_3_), channel_id=1, source_target_pairs={{0,224},{1,33},{2,226},{3,35},{4,228},{5,37},{6,230},{7,39},{8,232... | collective-permute-start | bytes 884744 | tf_op jit(solution)/shard_map/ppermute | solution.py:238
  42.1 9.3 %collective-permute-start.8 = (bf16[384,384]{1,0:T(8,128)(2,1)S(1)}, bf16[384,384]{1,0:T(8,128)(2,1)S(1)}, u32[]{:S(2)}, u32[]{:S(2)}) collective-permute-start(bf16[384,384]{1,0:T(8,128)(2,1)S(1)} %collective-permute-done.7.refs_8_), channel_id=1, source_target_pairs={{0,224},{1,33},{2,226},{3,35},{4,228},{5,37},{6,230},{7,39},{8,232... | collective-permute-start | bytes 884744 | tf_op jit(solution)/shard_map/ppermute | solution.py:238
  44.3 7.2 %copy-start.1 = (bf16[192,384]{1,0:T(8,128)(2,1)S(1)}, bf16[192,384]{1,0:T(8,128)(2,1)}, u32[]{:S(2)}) copy-start(bf16[192,384]{1,0:T(8,128)(2,1)} %refs_0_) | copy-start | bytes 442372
  44.3 7.2 %copy-start.2 = (bf16[320,128]{1,0:T(8,128)(2,1)S(1)}, bf16[320,128]{1,0:T(8,128)(2,1)}, u32[]{:S(2)}) copy-start(bf16[320,128]{1,0:T(8,128)(2,1)} %cot.1) | copy-start | bytes 245764
  44.3 7.2 %copy-start.4 = (f32[128]{0:T(128)S(1)}, f32[128]{0:T(128)}, u32[]{:S(2)}) copy-start(f32[128]{0:T(128)} %param.9) | copy-start | bytes 1540
  44.3 7.1 %copy-start.5 = (f32[128]{0:T(128)S(1)}, f32[128]{0:T(128)}, u32[]{:S(2)}) copy-start(f32[128]{0:T(128)} %param.10) | copy-start | bytes 1540
  60.3 10.2 %collective-permute-start.9 = (bf16[160,3072]{1,0:T(8,128)(2,1)S(1)}, bf16[160,3072]{1,0:T(8,128)(2,1)S(1)}, u32[]{:S(2)}, u32[]{:S(2)}) collective-permute-start(bf16[160,3072]{1,0:T(8,128)(2,1)S(1)} %get-tuple-element.32), channel_id=1, source_target_pairs={{0,1},{1,0},{2,3},{3,2},{4,5},{5,4},{6,7},{7,6},{8,9},{9,8},{10,11... | collective-permute-start | bytes 2949128 | tf_op jit(solution)/shard_map/ppermute | solution.py:238
  70.6 11.1 %collective-permute-start.10 = (bf16[80,3072]{1,0:T(8,128)(2,1)S(1)}, bf16[80,3072]{1,0:T(8,128)(2,1)S(1)}, u32[]{:S(2)}, u32[]{:S(2)}) collective-permute-start(bf16[80,3072]{1,0:T(8,128)(2,1)S(1)} %add_convert_fusion.4), channel_id=1, source_target_pairs={{0,2},{1,7},{2,0},{3,5},{4,6},{5,3},{6,4},{7,1},{8,10},{9,15},{10,... | collective-permute-start | bytes 1474568 | tf_op jit(solution)/shard_map/ppermute | solution.py:238
  75.0 10.9 %collective-permute-start.12 = (bf16[768,384]{1,0:T(8,128)(2,1)S(1)}, bf16[768,384]{1,0:T(8,128)(2,1)S(1)}, u32[]{:S(2)}, u32[]{:S(2)}) collective-permute-start(bf16[768,384]{1,0:T(8,128)(2,1)S(1)} %split.21), channel_id=1, source_target_pairs={{0,224},{1,33},{2,226},{3,35},{4,228},{5,37},{6,230},{7,39},{8,232... | collective-permute-start | bytes 1769480 | tf_op jit(solution)/shard_map/ppermute | solution.py:238
  81.9 7.2 %collective-permute-start.11 = (bf16[40,3072]{1,0:T(8,128)(2,1)S(1)}, bf16[40,3072]{1,0:T(8,128)(2,1)S(1)}, u32[]{:S(2)}, u32[]{:S(2)}) collective-permute-start(bf16[40,3072]{1,0:T(8,128)(2,1)S(1)} %slice.34), channel_id=1, source_target_pairs={{0,6},{1,3},{2,4},{3,1},{4,2},{5,7},{6,0},{7,5},{8,14},{9,11},{10,... | collective-permute-start | bytes 737288 | tf_op jit(solution)/shard_map/ppermute | solution.py:238
  86.1 12.0 %collective-permute-start.14 = (bf16[768,384]{1,0:T(8,128)(2,1)S(1)}, bf16[768,384]{1,0:T(8,128)(2,1)S(1)}, u32[]{:S(2)}, u32[]{:S(2)}) collective-permute-start(bf16[768,384]{1,0:T(8,128)(2,1)S(1)} %add_convert_fusion.1), channel_id=1, source_target_pairs={{0,32},{1,225},{2,34},{3,227},{4,36},{5,229},{6,38},{7,231},{8,40}... | collective-permute-start | bytes 1769480 | tf_op jit(solution)/shard_map/ppermute | solution.py:238
  89.2 11.1 %collective-permute-start.13 = (bf16[40,3072]{1,0:T(8,128)(2,1)S(1)}, bf16[40,3072]{1,0:T(8,128)(2,1)S(1)}, u32[]{:S(2)}, u32[]{:S(2)}) collective-permute-start(bf16[40,3072]{1,0:T(8,128)(2,1)S(1)} %add_convert_fusion.9), channel_id=1, source_target_pairs={{0,8},{1,25},{2,10},{3,27},{4,12},{5,29},{6,14},{7,31},{8,0},{9,17... | collective-permute-start | bytes 737288 | tf_op jit(solution)/shard_map/ppermute | solution.py:238
  98.2 13.9 %collective-permute-start.16 = (bf16[768,384]{1,0:T(8,128)(2,1)S(1)}, bf16[768,384]{1,0:T(8,128)(2,1)S(1)}, u32[]{:S(2)}, u32[]{:S(2)}) collective-permute-start(bf16[768,384]{1,0:T(8,128)(2,1)S(1)} %add_convert_fusion), channel_id=1, source_target_pairs={{0,224},{1,33},{2,226},{3,35},{4,228},{5,37},{6,230},{7,39},{8,232... | collective-permute-start | bytes 1769480 | tf_op jit(solution)/shard_map/ppermute | solution.py:238
  100.3 11.4 %collective-permute-start.15 = (bf16[40,3072]{1,0:T(8,128)(2,1)S(1)}, bf16[40,3072]{1,0:T(8,128)(2,1)S(1)}, u32[]{:S(2)}, u32[]{:S(2)}) collective-permute-start(bf16[40,3072]{1,0:T(8,128)(2,1)S(1)} %add_convert_fusion.8.left), channel_id=1, source_target_pairs={{0,24},{1,9},{2,26},{3,11},{4,28},{5,13},{6,30},{7,15},{8,16},{9,1... | collective-permute-start | bytes 737288 | tf_op jit(solution)/shard_map/ppermute | solution.py:238
  112.2 6.9 %collective-permute-start.17 = (bf16[40,3072]{1,0:T(8,128)(2,1)S(1)}, bf16[40,3072]{1,0:T(8,128)(2,1)S(1)}, u32[]{:S(2)}, u32[]{:S(2)}) collective-permute-start(bf16[40,3072]{1,0:T(8,128)(2,1)S(1)} %back.1), channel_id=1, source_target_pairs={{0,6},{1,3},{2,4},{3,1},{4,2},{5,7},{6,0},{7,5},{8,14},{9,11},{10,... | collective-permute-start | bytes 737288 | tf_op jit(solution)/shard_map/ppermute | solution.py:238
  114.2 9.0 %collective-permute-start.18 = (bf16[384,384]{1,0:T(8,128)(2,1)S(1)}, bf16[384,384]{1,0:T(8,128)(2,1)S(1)}, u32[]{:S(2)}, u32[]{:S(2)}) collective-permute-start(bf16[384,384]{1,0:T(8,128)(2,1)S(1)} %add_convert_fusion.7), channel_id=1, source_target_pairs={{0,32},{1,225},{2,34},{3,227},{4,36},{5,229},{6,38},{7,231},{8,40}... | collective-permute-start | bytes 884744 | tf_op jit(solution)/shard_map/ppermute | solution.py:238
  123.2 11.4 %collective-permute-start.19 = (bf16[80,3072]{1,0:T(8,128)(2,1)S(1)}, bf16[80,3072]{1,0:T(8,128)(2,1)S(1)}, u32[]{:S(2)}, u32[]{:S(2)}) collective-permute-start(bf16[80,3072]{1,0:T(8,128)(2,1)S(1)} %pad_maximum_fusion.2), channel_id=1, source_target_pairs={{0,2},{1,7},{2,0},{3,5},{4,6},{5,3},{6,4},{7,1},{8,10},{9,15},{10,... | collective-permute-start | bytes 1474568 | tf_op jit(solution)/shard_map/ppermute | solution.py:238
  127.7 6.2 %collective-permute-start.20 = (bf16[192,384]{1,0:T(8,128)(2,1)S(1)}, bf16[192,384]{1,0:T(8,128)(2,1)S(1)}, u32[]{:S(2)}, u32[]{:S(2)}) collective-permute-start(bf16[192,384]{1,0:T(8,128)(2,1)S(1)} %broadcast_select_fusion.6), channel_id=1, source_target_pairs={{0,256},{1,257},{2,258},{3,259},{4,260},{5,261},{6,262},{7,263},{8... | collective-permute-start | bytes 442376 | tf_op jit(solution)/shard_map/ppermute | solution.py:238
  134.8 8.5 %collective-permute-start.21 = (bf16[160,3072]{1,0:T(8,128)(2,1)S(1)}, bf16[160,3072]{1,0:T(8,128)(2,1)S(1)}, u32[]{:S(2)}, u32[]{:S(2)}) collective-permute-start(bf16[160,3072]{1,0:T(8,128)(2,1)S(1)} %pad_maximum_fusion.1), channel_id=1, source_target_pairs={{0,1},{1,0},{2,3},{3,2},{4,5},{5,4},{6,7},{7,6},{8,9},{9,8},{10,11... | collective-permute-start | bytes 2949128 | tf_op jit(solution)/shard_map/ppermute | solution.py:238

commit v4 on v3

--- a/solution.py
+++ b/solution.py
@@ -76,50 +76,40 @@
 
 def head_kernel(places, normed, cot, q_gain, k_gain, *refs):
     blocks, refs = refs[:10], refs[10:]
-    grad_ref, kept_ref, next_ref, sent_ref, weights, sems = refs
+    grad_ref, kept_ref, next_ref, sent_ref, weights = refs
     depth = blocks[0].shape[0]
-    copies = []
+    y_lo, z, z_way = places[0], places[1], places[2]
+    at = 0
     for ref in blocks:
         for part in range(ref.shape[0] // depth):
-            at = len(copies)
-            first = pl.multiple_of(places[at] * depth, depth)
-            copies.append(
-                pltpu.make_async_copy(
-                    ref.at[pl.ds(part * depth, depth), :],
-                    weights.at[pl.ds(first, depth), :],
-                    sems.at[at],
-                )
-            )
-    for copy in copies:
-        copy.start()
-    for copy in copies:
-        copy.wait()
+            y_at = y_lo if at < Z else 1 - y_lo
+            to = y_at * Z + lax.rem(z + z_way * Z_STEPS[at % Z] + Z, Z)
+            weights[pl.ds(pl.multiple_of(to * depth, depth), depth), :] = ref[
+                pl.ds(part * depth, depth), :
+            ]
+            at += 1
     width = weights.shape[1]
-    total = None
-    for first in range(0, weights.shape[0], width):
-        at = pl.ds(first, width)
-        product = jnp.dot(normed[:, at], weights[at, :], preferred_element_type=jnp.float32)
-        total = product if total is None else total + product
+    total = jnp.dot(normed[...], weights[...], preferred_element_type=jnp.float32)
     grads = head_grads(total.astype(jnp.bfloat16), cot[...], q_gain[...], k_gain[...])
     grad_ref[...] = grads.astype(jnp.bfloat16)
-    core, outer, inner = places[16], places[17], places[18]
+    core, outer, inner = places[3], places[4], places[5]
     half = grads.shape[0] // 2
     low, high = grads[:half], grads[half:]
     kept = swap_blocks(jnp.where(core == 0, low, high), outer, inner).astype(jnp.bfloat16)
     sent = swap_blocks(jnp.where(core == 0, high, low), inner, outer).astype(jnp.bfloat16)
+    both = jnp.concatenate([sent, kept])
     for first in range(0, weights.shape[0], width):
         at = pl.ds(first, width)
-        sent_ref[:, at] = contract(sent, weights[at, :], 1, 1).astype(jnp.bfloat16)
-        term = contract(kept, weights[at, :], 1, 1).astype(jnp.bfloat16)
-        kept_ref[:, at] = term[: half // 2]
-        next_ref[:, at] = term[half // 2 :]
+        term = contract(both, weights[at, :], 1, 1).astype(jnp.bfloat16)
+        sent_ref[:, at] = term[:half]
+        kept_ref[:, at] = term[half : half + half // 2]
+        next_ref[:, at] = term[half + half // 2 :]
 
 
 def run_head(places, normed, cot, q_gain, k_gain, blocks):
     tokens, features = normed.shape
     width = blocks[0].shape[1]
     in_vmem = pl.BlockSpec(memory_space=pltpu.VMEM)
-    in_hbm = pl.BlockSpec(memory_space=pltpu.HBM)
     like = lambda *shape: jax.ShapeDtypeStruct(shape, jnp.bfloat16)
     return pl.pallas_call(
         head_kernel,
@@ -129,11 +119,10 @@
             like(tokens // 4, features),
             like(tokens // 2, features),
         ),
-        in_specs=[pl.BlockSpec(memory_space=pltpu.SMEM)] + [in_vmem] * 4 + [in_hbm] * len(blocks),
+        in_specs=[pl.BlockSpec(memory_space=pltpu.SMEM)] + [in_vmem] * (4 + len(blocks)),
         out_specs=(in_vmem,) * 4,
         scratch_shapes=[
             pltpu.VMEM((features, width), jnp.bfloat16),
-            pltpu.SemaphoreType.DMA((16,)),
         ],
         compiler_params=pltpu.CompilerParams(vmem_limit_bytes=16 * 2**20),
         cost_estimate=pl.CostEstimate(
@@ -166,11 +155,15 @@
 def terms_kernel(places, normed, grads, out):
     features, width = out.shape
     depth = features // (Y_LO * Z)
+    z, z_way = places[1], places[2]
     for first in range(0, features, width):
         term = contract(normed[:, pl.ds(first, width)], grads[...], 0, 0).astype(out.dtype)
         for part in range(width // depth):
-            to = pl.multiple_of(places[first // depth + part] * depth, depth)
-            out[pl.ds(to, depth), :] = term[part * depth : (part + 1) * depth]
+            y_at, z_at = divmod(first // depth + part, Z)
+            step = lax.rem((z_at - z) * z_way + 2 * Z, Z)
+            far = jnp.where(step < 4, step + 2, jnp.where(step < 6, 11 - step, 9 - step))
+            to = jnp.where(step < 2, step, far) * Y_LO + y_at
+            out[pl.ds(pl.multiple_of(to * depth, depth), depth), :] = term[part * depth : (part + 1) * depth]
 
 
 def run_terms(places, normed, grads):
@@ -285,34 +278,16 @@
     near, far = (x + 1) // 2 % 2, x // 2
     outer, inner = jnp.where(core == 0, near, far), jnp.where(core == 0, far, near)
     z_way = jnp.where((z + core) % 2 == 0, 1, -1)
-    z_places = [(z + z_way * step) % Z for step in Z_STEPS]
-    places = jnp.stack(
-        [y_lo * Z + at for at in z_places]
-        + [(1 - y_lo) * Z + at for at in z_places]
-        + [core, outer, inner]
-    ).astype(jnp.int32)
-    steps = [(at - z) * z_way % Z for at in range(Z)]
-    orders = [
-        jnp.where(
-            step < 2,
-            step,
-            jnp.where(step < 4, step + 2, jnp.where(step < 6, 11 - step, 9 - step)),
-        )
-        for step in steps
-    ]
-    term_places = jnp.stack([Y_LO * order + y for y in range(Y_LO) for order in orders])
+    places = jnp.stack([y_lo, z, z_way, core, outer, inner]).astype(jnp.int32)
     tokens, features = inputs.shape
     rows = tokens // 8
-    own_rows = lax.dynamic_slice_in_dim(
-        inputs, ((core * 2 + outer) * 2 + inner) * rows, rows, 0
-    )
-    w_qkv, places, term_places, own_rows, first_core, first_outer, first_inner, first_y = (
+    own_first = ((core * 2 + outer) * 2 + inner) * rows
+    w_qkv, places, own_first, first_core, first_outer, first_inner, first_y = (
         lax.optimization_barrier(
             (
                 w_qkv,
                 places,
-                term_places.astype(jnp.int32),
-                own_rows,
+                own_first,
                 core == 0,
                 outer == 0,
                 inner == 0,
@@ -328,7 +303,7 @@
         places, normed, cotangent, q_gain.reshape(1, -1), k_gain.reshape(1, -1), blocks
     )
 
-    terms = run_terms(term_places, normed, grad_qkv)
+    terms = run_terms(places, normed, grad_qkv)
     depth = terms.shape[0] // Z
     zero, one, two, three, four = jnp.split(terms, [depth, 2 * depth, 4 * depth, 6 * depth])
     got = swap(sent, by_core)
@@ -355,22 +330,20 @@
     zero, one = add(zero, across[:depth]), add(one, across[depth:])
     got = swap(part, by_y_hi(-1))
     across = swap(one, by_z(1))
-    own = after(run_back(part, got, own_rows, ln_gain.reshape(1, -1)), one)
+    own = lax.dynamic_slice_in_dim(inputs, own_first, rows, 0, allow_negative_indices=False)
+    own = after(run_back(part, got, own, ln_gain.reshape(1, -1)), one)
+
+    got = swap(own, by_x(-1))
+    own = join(own, got, first_inner)
 
     zero = add(zero, after(across, own))
     depth = zero.shape[0] // 2
     low, high = zero[:depth], zero[depth:]
-    got = swap(own, by_x(-1))
-    across = swap(jnp.where(first_y, high, low), by_y_lo)
-    own = after(join(own, got, first_inner), zero)
-
-    across = after(across, own).astype(jnp.float32)
+    got = swap(own, by_x(1))
+    across = swap(jnp.where(first_y, high, low), by_y_lo).astype(jnp.float32)
     grad_w_qkv = jnp.where(first_y, low, high).astype(jnp.float32) + across
-    got = swap(own, by_x(1))
     own = after(join(own, got, first_outer), grad_w_qkv)
-
-    got = swap(own, by_core)
-    return (join(own, got, first_core), grad_w_qkv)
+    return (join(own, swap(own, by_core), first_core), grad_w_qkv)
 
 
 def solution(mesh):

time: 145 us -> 138 us (0.952)
  waiting for transfers between devices: 42.5 us -> 35.5 us
  Pallas kernels: 12.8 us -> 8.53 us
  local copies, waits for them, and re-layouts: 1.28 us -> 3.47 us
    ppermute x22, waiting for transfers between devices: 42.5 us -> 35.5 us  [swap(): return lax.ppermute(values, AXES, pairs_of(partner))]
    pallas_call x1, Pallas kernels: 8.8 us -> 4.58 us  [run_head(): pl.pallas_call(head_kernel, out_shape=(like(tokens, width), like(tokens /...]
    unnamed x12 -> x14, local copies, waits for them, and re-layouts: 0.03 us -> 2.27 us
  transfers between devices with their start and end apart: 22 -> 22, of which waited for: 15 -> 15; matrix products, arithmetic and copies ran while one was open for 2% -> 3% of each run, Pallas kernels for 3% -> 3%
where the time goes in v4:
time: 138 us; the launch traced here: 136 us
  starting transfers between devices  83.1 us (60%)
  waiting for transfers between devices  35.5 us (26%)
  Pallas kernels  8.53 us (6%)
  other arithmetic  4.53 us (3%)
  local copies, waits for them, and re-layouts  3.47 us (3%)
    ppermute x22, starting transfers between devices, swap(): return lax.ppermute(values, AXES, pairs_of(partner))  83.1 us
    ppermute x22, waiting for transfers between devices, swap(): return lax.ppermute(values, AXES, pairs_of(partner))  35.5 us
    pallas_call x1, Pallas kernels, run_head(): pl.pallas_call(head_kernel, out_shape=(like(tokens, width), like(tokens /...  4.58 us
  transfers between devices with their start and end apart: 22, of which 15 were waited for; matrix products, arithmetic and copies ran while one was open for 3% of the time, Pallas kernels for 3%

profile of v4, /device:TPU:1, one launch (start us, length us, event | category | flops | bytes accessed | tf_op | source)
XLA Modules:
  0.0 136.3 jit_solution(9941049051727724315)
XLA Ops:
  0.8 0.1 stack.27.places
  0.9 4.0 %collective-permute-start.4 = (bf16[192,384]{1,0:T(8,128)(2,1)}, bf16[192,384]{1,0:T(8,128)(2,1)S(1)}, u32[]{:S(2)}, u32[]{:S(2)}) collective-permute-start(bf16[192,384]{1,0:T(8,128)(2,1)} %refs_0_), channel_id=1, source_target_pairs={{0,256},{1,257},{2,258},{3,259},{4,260},{5,261},{6,262},{7,263},{8... | collective-permute-start | bytes 442376 | tf_op jit(solution)/shard_map/ppermute | solution.py:231
  4.9 10.7 %collective-permute-start = (bf16[192,384]{1,0:T(8,128)(2,1)}, bf16[192,384]{1,0:T(8,128)(2,1)S(1)}, u32[]{:S(2)}, u32[]{:S(2)}) collective-permute-start(bf16[192,384]{1,0:T(8,128)(2,1)} %refs_0_), channel_id=1, source_target_pairs={{0,32},{1,225},{2,34},{3,227},{4,36},{5,229},{6,38},{7,231},{8,40}... | collective-permute-start | bytes 442376 | tf_op jit(solution)/shard_map/ppermute | solution.py:231
  15.6 3.6 %collective-permute-start.5 = (bf16[192,384]{1,0:T(8,128)(2,1)S(1)}, bf16[192,384]{1,0:T(8,128)(2,1)S(1)}, u32[]{:S(2)}, u32[]{:S(2)}) collective-permute-start(bf16[192,384]{1,0:T(8,128)(2,1)S(1)} %collective-permute-done.4.refs_5_), channel_id=1, source_target_pairs={{0,32},{1,225},{2,34},{3,227},{4,36},{5,229},{6,38},{7,231},{8,40}... | collective-permute-start | bytes 442376 | tf_op jit(solution)/shard_map/ppermute | solution.py:231
  19.2 0.0 collective-permute-done.refs_1_
  19.2 0.9 pad_maximum_fusion.3
  20.1 1.9 %collective-permute-start.1 = (bf16[384,384]{1,0:T(8,128)(2,1)S(1)}, bf16[384,384]{1,0:T(8,128)(2,1)S(1)}, u32[]{:S(2)}, u32[]{:S(2)}) collective-permute-start(bf16[384,384]{1,0:T(8,128)(2,1)S(1)} %pad_maximum_fusion.3), channel_id=1, source_target_pairs={{0,224},{1,33},{2,226},{3,35},{4,228},{5,37},{6,230},{7,39},{8,232... | collective-permute-start | bytes 884744 | tf_op jit(solution)/shard_map/ppermute | solution.py:231
  22.0 0.6 collective-permute-done.5.refs_6_
  22.7 2.7 %collective-permute-start.6 = (bf16[384,384]{1,0:T(8,128)(2,1)S(1)}, bf16[384,384]{1,0:T(8,128)(2,1)S(1)}, u32[]{:S(2)}, u32[]{:S(2)}) collective-permute-start(bf16[384,384]{1,0:T(8,128)(2,1)S(1)} %pad_maximum_fusion.4), channel_id=1, source_target_pairs={{0,224},{1,33},{2,226},{3,35},{4,228},{5,37},{6,230},{7,39},{8,232... | collective-permute-start | bytes 884744 | tf_op jit(solution)/shard_map/ppermute | solution.py:231
  25.5 2.4 %collective-permute-done.1.refs_2_ = bf16[384,384]{1,0:T(8,128)(2,1)S(1)} collective-permute-done((bf16[384,384]{1,0:T(8,128)(2,1)S(1)}, bf16[384,384]{1,0:T(8,128)(2,1)S(1)}, u32[]{:S(2)}, u32[]{:S(2)}) %collective-permute-start.1) | collective-permute-done | bytes 294944 | tf_op jit(solution)/shard_map/ppermute | solution.py:231
  27.9 3.7 %collective-permute-start.2 = (bf16[384,384]{1,0:T(8,128)(2,1)S(1)}, bf16[384,384]{1,0:T(8,128)(2,1)S(1)}, u32[]{:S(2)}, u32[]{:S(2)}) collective-permute-start(bf16[384,384]{1,0:T(8,128)(2,1)S(1)} %collective-permute-done.1.refs_2_), channel_id=1, source_target_pairs={{0,32},{1,225},{2,34},{3,227},{4,36},{5,229},{6,38},{7,231},{8,40}... | collective-permute-start | bytes 884744 | tf_op jit(solution)/shard_map/ppermute | solution.py:231
  31.6 3.1 %collective-permute-start.7 = (bf16[384,384]{1,0:T(8,128)(2,1)S(1)}, bf16[384,384]{1,0:T(8,128)(2,1)S(1)}, u32[]{:S(2)}, u32[]{:S(2)}) collective-permute-start(bf16[384,384]{1,0:T(8,128)(2,1)S(1)} %collective-permute-done.6.refs_7_), channel_id=1, source_target_pairs={{0,32},{1,225},{2,34},{3,227},{4,36},{5,229},{6,38},{7,231},{8,40}... | collective-permute-start | bytes 884744 | tf_op jit(solution)/shard_map/ppermute | solution.py:231
  34.7 2.6 %collective-permute-done.2.refs_3_ = bf16[384,384]{1,0:T(8,128)(2,1)S(1)} collective-permute-done((bf16[384,384]{1,0:T(8,128)(2,1)S(1)}, bf16[384,384]{1,0:T(8,128)(2,1)S(1)}, u32[]{:S(2)}, u32[]{:S(2)}) %collective-permute-start.2) | collective-permute-done | bytes 294944 | tf_op jit(solution)/shard_map/ppermute | solution.py:231
  37.3 1.9 %collective-permute-start.3 = (bf16[384,384]{1,0:T(8,128)(2,1)S(1)}, bf16[384,384]{1,0:T(8,128)(2,1)S(1)}, u32[]{:S(2)}, u32[]{:S(2)}) collective-permute-start(bf16[384,384]{1,0:T(8,128)(2,1)S(1)} %collective-permute-done.2.refs_3_), channel_id=1, source_target_pairs={{0,224},{1,33},{2,226},{3,35},{4,228},{5,37},{6,230},{7,39},{8,232... | collective-permute-start | bytes 884744 | tf_op jit(solution)/shard_map/ppermute | solution.py:231
  39.3 1.2 collective-permute-done.7.refs_8_
  40.5 2.1 %collective-permute-start.8 = (bf16[384,384]{1,0:T(8,128)(2,1)S(1)}, bf16[384,384]{1,0:T(8,128)(2,1)S(1)}, u32[]{:S(2)}, u32[]{:S(2)}) collective-permute-start(bf16[384,384]{1,0:T(8,128)(2,1)S(1)} %collective-permute-done.7.refs_8_), channel_id=1, source_target_pairs={{0,224},{1,33},{2,226},{3,35},{4,228},{5,37},{6,230},{7,39},{8,232... | collective-permute-start | bytes 884744 | tf_op jit(solution)/shard_map/ppermute | solution.py:231
  42.6 0.0 copy-start
  42.7 1.5 %copy-done = bf16[320,3072]{1,0:T(8,128)(2,1)S(1)} copy-done((bf16[320,3072]{1,0:T(8,128)(2,1)S(1)}, bf16[320,3072]{1,0:T(8,128)(2,1)}, u32[]{:S(2)}) %copy-start) | copy-done | bytes 1966104
  44.2 0.7 copy-done.3
  44.9 1.3 norm.1.normed
  46.2 0.8 collective-permute-done.3.refs_4_
  47.0 2.9 %collective-permute-done.8.refs_9_ = bf16[384,384]{1,0:T(8,128)(2,1)S(1)} collective-permute-done((bf16[384,384]{1,0:T(8,128)(2,1)S(1)}, bf16[384,384]{1,0:T(8,128)(2,1)S(1)}, u32[]{:S(2)}, u32[]{:S(2)}) %collective-permute-start.8) | collective-permute-done | bytes 294944 | tf_op jit(solution)/shard_map/ppermute | solution.py:231
  49.9 4.6 %head.1 = (bf16[320,384]{1,0:T(8,128)(2,1)S(1)}, bf16[80,3072]{1,0:T(8,128)(2,1)S(1)}, bf16[80,3072]{1,0:T(8,128)(2,1)S(1)}, bf16[160,3072]{1,0:T(8,128)(2,1)S(1)}) custom-call(s32[6]{0:T(128)S(1)} %stack.27.places, bf16[320,3072]{1,0:T(8,128)(2,1)S(1)} %norm.1.normed, bf16[320,128]{1,0:T(8,128)(2,1)S(1)} %copy-done.2, f32[1,128]{1,0:T(1,128)S(1)} %bitcast.11, ...), custom_call_target="tpu_custom_call" | custom-call | flops 1132462080 | bytes 8388608 | tf_op jit(solution)/shard_map/head/pallas_call | solution.py:114
  54.4 7.9 %collective-permute-start.9 = (bf16[160,3072]{1,0:T(8,128)(2,1)S(1)}, bf16[160,3072]{1,0:T(8,128)(2,1)S(1)}, u32[]{:S(2)}, u32[]{:S(2)}) collective-permute-start(bf16[160,3072]{1,0:T(8,128)(2,1)S(1)} %get-tuple-element.29), channel_id=1, source_target_pairs={{0,1},{1,0},{2,3},{3,2},{4,5},{5,4},{6,7},{7,6},{8,9},{9,8},{10,11... | collective-permute-start | bytes 2949128 | tf_op jit(solution)/shard_map/ppermute | solution.py:231
  62.4 2.2 %terms.1 = bf16[3072,384]{1,0:T(8,128)(2,1)S(1)} custom-call(s32[6]{0:T(128)S(1)} %stack.27.places, bf16[320,3072]{1,0:T(8,128)(2,1)S(1)} %norm.1.normed, bf16[320,384]{1,0:T(8,128)(2,1)S(1)} %get-tuple-element.31.grads), custom_call_target="tpu_custom_call" | custom-call | flops 754974720 | bytes 5242880 | tf_op jit(solution)/shard_map/terms/pallas_call | solution.py:173
  64.6 0.1 add_convert_fusion.4
  64.7 4.4 %collective-permute-start.10 = (bf16[80,3072]{1,0:T(8,128)(2,1)S(1)}, bf16[80,3072]{1,0:T(8,128)(2,1)S(1)}, u32[]{:S(2)}, u32[]{:S(2)}) collective-permute-start(bf16[80,3072]{1,0:T(8,128)(2,1)S(1)} %add_convert_fusion.4), channel_id=1, source_target_pairs={{0,2},{1,7},{2,0},{3,5},{4,6},{5,3},{6,4},{7,1},{8,10},{9,15},{10,... | collective-permute-start | bytes 1474568 | tf_op jit(solution)/shard_map/ppermute | solution.py:231
  69.1 0.1 split.21
  69.2 1.9 %collective-permute-start.12 = (bf16[768,384]{1,0:T(8,128)(2,1)S(1)}, bf16[768,384]{1,0:T(8,128)(2,1)S(1)}, u32[]{:S(2)}, u32[]{:S(2)}) collective-permute-start(bf16[768,384]{1,0:T(8,128)(2,1)S(1)} %split.21), channel_id=1, source_target_pairs={{0,224},{1,33},{2,226},{3,35},{4,228},{5,37},{6,230},{7,39},{8,232... | collective-permute-start | bytes 1769480 | tf_op jit(solution)/shard_map/ppermute | solution.py:231
  71.1 4.7 %collective-permute-done.10 = bf16[80,3072]{1,0:T(8,128)(2,1)S(1)} collective-permute-done((bf16[80,3072]{1,0:T(8,128)(2,1)S(1)}, bf16[80,3072]{1,0:T(8,128)(2,1)S(1)}, u32[]{:S(2)}, u32[]{:S(2)}) %collective-permute-start.10) | collective-permute-done | bytes 491552 | tf_op jit(solution)/shard_map/ppermute | solution.py:231
  75.8 0.2 add_convert_fusion.2
  76.0 1.9 %collective-permute-start.11 = (bf16[40,3072]{1,0:T(8,128)(2,1)S(1)}, bf16[40,3072]{1,0:T(8,128)(2,1)S(1)}, u32[]{:S(2)}, u32[]{:S(2)}) collective-permute-start(bf16[40,3072]{1,0:T(8,128)(2,1)S(1)} %slice.34), channel_id=1, source_target_pairs={{0,6},{1,3},{2,4},{3,1},{4,2},{5,7},{6,0},{7,5},{8,14},{9,11},{10,... | collective-permute-start | bytes 737288 | tf_op jit(solution)/shard_map/ppermute | solution.py:231
  78.0 2.2 %collective-permute-done.12 = bf16[768,384]{1,0:T(8,128)(2,1)S(1)} collective-permute-done((bf16[768,384]{1,0:T(8,128)(2,1)S(1)}, bf16[768,384]{1,0:T(8,128)(2,1)S(1)}, u32[]{:S(2)}, u32[]{:S(2)}) %collective-permute-start.12) | collective-permute-done | bytes 589856 | tf_op jit(solution)/shard_map/ppermute | solution.py:231
  80.1 0.1 add_convert_fusion.1
  80.3 0.0 copy-start.4
  80.3 1.9 %collective-permute-start.14 = (bf16[768,384]{1,0:T(8,128)(2,1)S(1)}, bf16[768,384]{1,0:T(8,128)(2,1)S(1)}, u32[]{:S(2)}, u32[]{:S(2)}) collective-permute-start(bf16[768,384]{1,0:T(8,128)(2,1)S(1)} %add_convert_fusion.1), channel_id=1, source_target_pairs={{0,32},{1,225},{2,34},{3,227},{4,36},{5,229},{6,38},{7,231},{8,40}... | collective-permute-start | bytes 1769480 | tf_op jit(solution)/shard_map/ppermute | solution.py:231
  82.2 1.0 collective-permute-done.11
  83.3 0.1 add_convert_fusion.9
  83.3 5.5 %collective-permute-start.13 = (bf16[40,3072]{1,0:T(8,128)(2,1)S(1)}, bf16[40,3072]{1,0:T(8,128)(2,1)S(1)}, u32[]{:S(2)}, u32[]{:S(2)}) collective-permute-start(bf16[40,3072]{1,0:T(8,128)(2,1)S(1)} %add_convert_fusion.9), channel_id=1, source_target_pairs={{0,8},{1,25},{2,10},{3,27},{4,12},{5,29},{6,14},{7,31},{8,0},{9,17... | collective-permute-start | bytes 737288 | tf_op jit(solution)/shard_map/ppermute | solution.py:231
  88.8 3.4 %collective-permute-done.14 = bf16[768,384]{1,0:T(8,128)(2,1)S(1)} collective-permute-done((bf16[768,384]{1,0:T(8,128)(2,1)S(1)}, bf16[768,384]{1,0:T(8,128)(2,1)S(1)}, u32[]{:S(2)}, u32[]{:S(2)}) %collective-permute-start.14) | collective-permute-done | bytes 589856 | tf_op jit(solution)/shard_map/ppermute | solution.py:231
  92.3 0.2 add_convert_fusion
  92.4 1.9 %collective-permute-start.16 = (bf16[768,384]{1,0:T(8,128)(2,1)S(1)}, bf16[768,384]{1,0:T(8,128)(2,1)S(1)}, u32[]{:S(2)}, u32[]{:S(2)}) collective-permute-start(bf16[768,384]{1,0:T(8,128)(2,1)S(1)} %add_convert_fusion), channel_id=1, source_target_pairs={{0,224},{1,33},{2,226},{3,35},{4,228},{5,37},{6,230},{7,39},{8,232... | collective-permute-start | bytes 1769480 | tf_op jit(solution)/shard_map/ppermute | solution.py:231
  94.4 0.0 collective-permute-done.13
  94.4 0.1 add_convert_fusion.8.left
  94.4 4.9 %collective-permute-start.15 = (bf16[40,3072]{1,0:T(8,128)(2,1)S(1)}, bf16[40,3072]{1,0:T(8,128)(2,1)S(1)}, u32[]{:S(2)}, u32[]{:S(2)}) collective-permute-start(bf16[40,3072]{1,0:T(8,128)(2,1)S(1)} %add_convert_fusion.8.left), channel_id=1, source_target_pairs={{0,24},{1,9},{2,26},{3,11},{4,28},{5,13},{6,30},{7,15},{8,16},{9,1... | collective-permute-start | bytes 737288 | tf_op jit(solution)/shard_map/ppermute | solution.py:231
  99.3 1.0 constant_dynamic-slice_fusion.inputs
  100.3 5.5 %collective-permute-done.15.right = bf16[40,3072]{1,0:T(8,128)(2,1)S(1)} collective-permute-done((bf16[40,3072]{1,0:T(8,128)(2,1)S(1)}, bf16[40,3072]{1,0:T(8,128)(2,1)S(1)}, u32[]{:S(2)}, u32[]{:S(2)}) %collective-permute-start.15) | collective-permute-done | bytes 245792 | tf_op jit(solution)/shard_map/ppermute | solution.py:231
  105.9 0.4 back.1
  106.3 0.1 add_convert_fusion.7
  106.4 1.9 %collective-permute-start.17 = (bf16[40,3072]{1,0:T(8,128)(2,1)S(1)}, bf16[40,3072]{1,0:T(8,128)(2,1)S(1)}, u32[]{:S(2)}, u32[]{:S(2)}) collective-permute-start(bf16[40,3072]{1,0:T(8,128)(2,1)S(1)} %back.1), channel_id=1, source_target_pairs={{0,6},{1,3},{2,4},{3,1},{4,2},{5,7},{6,0},{7,5},{8,14},{9,11},{10,... | collective-permute-start | bytes 737288 | tf_op jit(solution)/shard_map/ppermute | solution.py:231
  108.3 3.4 %collective-permute-start.19 = (bf16[384,384]{1,0:T(8,128)(2,1)S(1)}, bf16[384,384]{1,0:T(8,128)(2,1)S(1)}, u32[]{:S(2)}, u32[]{:S(2)}) collective-permute-start(bf16[384,384]{1,0:T(8,128)(2,1)S(1)} %add_convert_fusion.7), channel_id=1, source_target_pairs={{0,32},{1,225},{2,34},{3,227},{4,36},{5,229},{6,38},{7,231},{8,40}... | collective-permute-start | bytes 884744 | tf_op jit(solution)/shard_map/ppermute | solution.py:231
  111.8 1.6 %collective-permute-done.17 = bf16[40,3072]{1,0:T(8,128)(2,1)S(1)} collective-permute-done((bf16[40,3072]{1,0:T(8,128)(2,1)S(1)}, bf16[40,3072]{1,0:T(8,128)(2,1)S(1)}, u32[]{:S(2)}, u32[]{:S(2)}) %collective-permute-start.17) | collective-permute-done | bytes 245792 | tf_op jit(solution)/shard_map/ppermute | solution.py:231
  113.4 3.7 %collective-permute-start.18 = (bf16[80,3072]{1,0:T(8,128)(2,1)S(1)}, bf16[80,3072]{1,0:T(8,128)(2,1)S(1)}, u32[]{:S(2)}, u32[]{:S(2)}) collective-permute-start(bf16[80,3072]{1,0:T(8,128)(2,1)S(1)} %pad_maximum_fusion.2), channel_id=1, source_target_pairs={{0,2},{1,7},{2,0},{3,5},{4,6},{5,3},{6,4},{7,1},{8,10},{9,15},{10,... | collective-permute-start | bytes 1474568 | tf_op jit(solution)/shard_map/ppermute | solution.py:231
  117.1 0.2 collective-permute-done.19
  117.3 0.1 add_convert_fusion.5
  117.5 1.9 %collective-permute-start.20 = (bf16[192,384]{1,0:T(8,128)(2,1)S(1)}, bf16[192,384]{1,0:T(8,128)(2,1)S(1)}, u32[]{:S(2)}, u32[]{:S(2)}) collective-permute-start(bf16[192,384]{1,0:T(8,128)(2,1)S(1)} %broadcast_select_fusion.6), channel_id=1, source_target_pairs={{0,256},{1,257},{2,258},{3,259},{4,260},{5,261},{6,262},{7,263},{8... | collective-permute-start | bytes 442376 | tf_op jit(solution)/shard_map/ppermute | solution.py:231
  119.4 4.3 %collective-permute-done.20 = bf16[192,384]{1,0:T(8,128)(2,1)S(1)} collective-permute-done((bf16[192,384]{1,0:T(8,128)(2,1)S(1)}, bf16[192,384]{1,0:T(8,128)(2,1)S(1)}, u32[]{:S(2)}, u32[]{:S(2)}) %collective-permute-start.20) | collective-permute-done | bytes 147488 | tf_op jit(solution)/shard_map/ppermute | solution.py:231
  123.6 0.8 convert_add_fusion
  124.4 0.2 broadcast_select_fusion.3
  124.6 0.1 pad_maximum_fusion.1
  124.6 8.0 %collective-permute-start.21 = (bf16[160,3072]{1,0:T(8,128)(2,1)S(1)}, bf16[160,3072]{1,0:T(8,128)(2,1)S(1)}, u32[]{:S(2)}, u32[]{:S(2)}) collective-permute-start(bf16[160,3072]{1,0:T(8,128)(2,1)S(1)} %pad_maximum_fusion.1), channel_id=1, source_target_pairs={{0,1},{1,0},{2,3},{3,2},{4,5},{5,4},{6,7},{7,6},{8,9},{9,8},{10,11... | collective-permute-start | bytes 2949128 | tf_op jit(solution)/shard_map/ppermute | solution.py:231
  132.6 2.2 %collective-permute-done.21 = bf16[160,3072]{1,0:T(8,128)(2,1)S(1)} collective-permute-done((bf16[160,3072]{1,0:T(8,128)(2,1)S(1)}, bf16[160,3072]{1,0:T(8,128)(2,1)S(1)}, u32[]{:S(2)}, u32[]{:S(2)}) %collective-permute-start.21) | collective-permute-done | bytes 983072 | tf_op jit(solution)/shard_map/ppermute | solution.py:231
  134.8 0.1 broadcast_select_fusion.1
  134.9 1.4 %pad_maximum_fusion = bf16[320,3072]{1,0:T(8,128)(2,1)} fusion(bf16[160,3072]{1,0:T(8,128)(2,1)S(1)} %get-tuple-element.45, bf16[160,3072]{1,0:T(8,128)(2,1)S(1)} %get-tuple-element.44), kind=kLoop, calls=%fused_computation | loop fusion | flops 3932160 | bytes 3932160 | tf_op jit(solution)/shard_map/concatenate | solution.py:271
  (20 shorter events, 0.2 us)
Async XLA Ops:
  0.9 14.7 %collective-permute-start.4 = (bf16[192,384]{1,0:T(8,128)(2,1)}, bf16[192,384]{1,0:T(8,128)(2,1)S(1)}, u32[]{:S(2)}, u32[]{:S(2)}) collective-permute-start(bf16[192,384]{1,0:T(8,128)(2,1)} %refs_0_), channel_id=1, source_target_pairs={{0,256},{1,257},{2,258},{3,259},{4,260},{5,261},{6,262},{7,263},{8... | collective-permute-start | bytes 442376 | tf_op jit(solution)/shard_map/ppermute | solution.py:231
  4.9 14.3 %collective-permute-start = (bf16[192,384]{1,0:T(8,128)(2,1)}, bf16[192,384]{1,0:T(8,128)(2,1)S(1)}, u32[]{:S(2)}, u32[]{:S(2)}) collective-permute-start(bf16[192,384]{1,0:T(8,128)(2,1)} %refs_0_), channel_id=1, source_target_pairs={{0,32},{1,225},{2,34},{3,227},{4,36},{5,229},{6,38},{7,231},{8,40}... | collective-permute-start | bytes 442376 | tf_op jit(solution)/shard_map/ppermute | solution.py:231
  15.6 7.1 %collective-permute-start.5 = (bf16[192,384]{1,0:T(8,128)(2,1)S(1)}, bf16[192,384]{1,0:T(8,128)(2,1)S(1)}, u32[]{:S(2)}, u32[]{:S(2)}) collective-permute-start(bf16[192,384]{1,0:T(8,128)(2,1)S(1)} %collective-permute-done.4.refs_5_), channel_id=1, source_target_pairs={{0,32},{1,225},{2,34},{3,227},{4,36},{5,229},{6,38},{7,231},{8,40}... | collective-permute-start | bytes 442376 | tf_op jit(solution)/shard_map/ppermute | solution.py:231
  20.1 7.8 %collective-permute-start.1 = (bf16[384,384]{1,0:T(8,128)(2,1)S(1)}, bf16[384,384]{1,0:T(8,128)(2,1)S(1)}, u32[]{:S(2)}, u32[]{:S(2)}) collective-permute-start(bf16[384,384]{1,0:T(8,128)(2,1)S(1)} %pad_maximum_fusion.3), channel_id=1, source_target_pairs={{0,224},{1,33},{2,226},{3,35},{4,228},{5,37},{6,230},{7,39},{8,232... | collective-permute-start | bytes 884744 | tf_op jit(solution)/shard_map/ppermute | solution.py:231
  22.7 8.9 %collective-permute-start.6 = (bf16[384,384]{1,0:T(8,128)(2,1)S(1)}, bf16[384,384]{1,0:T(8,128)(2,1)S(1)}, u32[]{:S(2)}, u32[]{:S(2)}) collective-permute-start(bf16[384,384]{1,0:T(8,128)(2,1)S(1)} %pad_maximum_fusion.4), channel_id=1, source_target_pairs={{0,224},{1,33},{2,226},{3,35},{4,228},{5,37},{6,230},{7,39},{8,232... | collective-permute-start | bytes 884744 | tf_op jit(solution)/shard_map/ppermute | solution.py:231
  27.9 9.5 %collective-permute-start.2 = (bf16[384,384]{1,0:T(8,128)(2,1)S(1)}, bf16[384,384]{1,0:T(8,128)(2,1)S(1)}, u32[]{:S(2)}, u32[]{:S(2)}) collective-permute-start(bf16[384,384]{1,0:T(8,128)(2,1)S(1)} %collective-permute-done.1.refs_2_), channel_id=1, source_target_pairs={{0,32},{1,225},{2,34},{3,227},{4,36},{5,229},{6,38},{7,231},{8,40}... | collective-permute-start | bytes 884744 | tf_op jit(solution)/shard_map/ppermute | solution.py:231
  31.6 8.9 %collective-permute-start.7 = (bf16[384,384]{1,0:T(8,128)(2,1)S(1)}, bf16[384,384]{1,0:T(8,128)(2,1)S(1)}, u32[]{:S(2)}, u32[]{:S(2)}) collective-permute-start(bf16[384,384]{1,0:T(8,128)(2,1)S(1)} %collective-permute-done.6.refs_7_), channel_id=1, source_target_pairs={{0,32},{1,225},{2,34},{3,227},{4,36},{5,229},{6,38},{7,231},{8,40}... | collective-permute-start | bytes 884744 | tf_op jit(solution)/shard_map/ppermute | solution.py:231
  37.3 9.6 %collective-permute-start.3 = (bf16[384,384]{1,0:T(8,128)(2,1)S(1)}, bf16[384,384]{1,0:T(8,128)(2,1)S(1)}, u32[]{:S(2)}, u32[]{:S(2)}) collective-permute-start(bf16[384,384]{1,0:T(8,128)(2,1)S(1)} %collective-permute-done.2.refs_3_), channel_id=1, source_target_pairs={{0,224},{1,33},{2,226},{3,35},{4,228},{5,37},{6,230},{7,39},{8,232... | collective-permute-start | bytes 884744 | tf_op jit(solution)/shard_map/ppermute | solution.py:231
  40.5 9.3 %collective-permute-start.8 = (bf16[384,384]{1,0:T(8,128)(2,1)S(1)}, bf16[384,384]{1,0:T(8,128)(2,1)S(1)}, u32[]{:S(2)}, u32[]{:S(2)}) collective-permute-start(bf16[384,384]{1,0:T(8,128)(2,1)S(1)} %collective-permute-done.7.refs_8_), channel_id=1, source_target_pairs={{0,224},{1,33},{2,226},{3,35},{4,228},{5,37},{6,230},{7,39},{8,232... | collective-permute-start | bytes 884744 | tf_op jit(solution)/shard_map/ppermute | solution.py:231
  42.6 1.5 %copy-start = (bf16[320,3072]{1,0:T(8,128)(2,1)S(1)}, bf16[320,3072]{1,0:T(8,128)(2,1)}, u32[]{:S(2)}) copy-start(bf16[320,3072]{1,0:T(8,128)(2,1)} %inputs.1) | copy-start | bytes 5898244
  44.2 0.7 copy-start.3
  44.9 4.9 %copy-start.1 = (bf16[192,384]{1,0:T(8,128)(2,1)S(1)}, bf16[192,384]{1,0:T(8,128)(2,1)}, u32[]{:S(2)}) copy-start(bf16[192,384]{1,0:T(8,128)(2,1)} %refs_0_) | copy-start | bytes 442372
  44.9 4.9 %copy-start.2 = (bf16[320,128]{1,0:T(8,128)(2,1)S(1)}, bf16[320,128]{1,0:T(8,128)(2,1)}, u32[]{:S(2)}) copy-start(bf16[320,128]{1,0:T(8,128)(2,1)} %cot.1) | copy-start | bytes 245764
  44.9 4.9 %copy-start.5 = (f32[128]{0:T(128)S(1)}, f32[128]{0:T(128)}, u32[]{:S(2)}) copy-start(f32[128]{0:T(128)} %param.9) | copy-start | bytes 1540
  44.9 4.9 %copy-start.6 = (f32[128]{0:T(128)S(1)}, f32[128]{0:T(128)}, u32[]{:S(2)}) copy-start(f32[128]{0:T(128)} %param.10) | copy-start | bytes 1540
  54.4 10.2 %collective-permute-start.9 = (bf16[160,3072]{1,0:T(8,128)(2,1)S(1)}, bf16[160,3072]{1,0:T(8,128)(2,1)S(1)}, u32[]{:S(2)}, u32[]{:S(2)}) collective-permute-start(bf16[160,3072]{1,0:T(8,128)(2,1)S(1)} %get-tuple-element.29), channel_id=1, source_target_pairs={{0,1},{1,0},{2,3},{3,2},{4,5},{5,4},{6,7},{7,6},{8,9},{9,8},{10,11... | collective-permute-start | bytes 2949128 | tf_op jit(solution)/shard_map/ppermute | solution.py:231
  64.7 11.1 %collective-permute-start.10 = (bf16[80,3072]{1,0:T(8,128)(2,1)S(1)}, bf16[80,3072]{1,0:T(8,128)(2,1)S(1)}, u32[]{:S(2)}, u32[]{:S(2)}) collective-permute-start(bf16[80,3072]{1,0:T(8,128)(2,1)S(1)} %add_convert_fusion.4), channel_id=1, source_target_pairs={{0,2},{1,7},{2,0},{3,5},{4,6},{5,3},{6,4},{7,1},{8,10},{9,15},{10,... | collective-permute-start | bytes 1474568 | tf_op jit(solution)/shard_map/ppermute | solution.py:231
  69.2 10.9 %collective-permute-start.12 = (bf16[768,384]{1,0:T(8,128)(2,1)S(1)}, bf16[768,384]{1,0:T(8,128)(2,1)S(1)}, u32[]{:S(2)}, u32[]{:S(2)}) collective-permute-start(bf16[768,384]{1,0:T(8,128)(2,1)S(1)} %split.21), channel_id=1, source_target_pairs={{0,224},{1,33},{2,226},{3,35},{4,228},{5,37},{6,230},{7,39},{8,232... | collective-permute-start | bytes 1769480 | tf_op jit(solution)/shard_map/ppermute | solution.py:231
  76.0 7.2 %collective-permute-start.11 = (bf16[40,3072]{1,0:T(8,128)(2,1)S(1)}, bf16[40,3072]{1,0:T(8,128)(2,1)S(1)}, u32[]{:S(2)}, u32[]{:S(2)}) collective-permute-start(bf16[40,3072]{1,0:T(8,128)(2,1)S(1)} %slice.34), channel_id=1, source_target_pairs={{0,6},{1,3},{2,4},{3,1},{4,2},{5,7},{6,0},{7,5},{8,14},{9,11},{10,... | collective-permute-start | bytes 737288 | tf_op jit(solution)/shard_map/ppermute | solution.py:231
  80.3 25.6 %copy-start.4 = (f32[3072]{0:T(1024)S(1)}, f32[3072]{0:T(1024)}, u32[]{:S(2)}) copy-start(f32[3072]{0:T(1024)} %param.7) | copy-start | bytes 36868
  80.3 12.0 %collective-permute-start.14 = (bf16[768,384]{1,0:T(8,128)(2,1)S(1)}, bf16[768,384]{1,0:T(8,128)(2,1)S(1)}, u32[]{:S(2)}, u32[]{:S(2)}) collective-permute-start(bf16[768,384]{1,0:T(8,128)(2,1)S(1)} %add_convert_fusion.1), channel_id=1, source_target_pairs={{0,32},{1,225},{2,34},{3,227},{4,36},{5,229},{6,38},{7,231},{8,40}... | collective-permute-start | bytes 1769480 | tf_op jit(solution)/shard_map/ppermute | solution.py:231
  83.3 11.1 %collective-permute-start.13 = (bf16[40,3072]{1,0:T(8,128)(2,1)S(1)}, bf16[40,3072]{1,0:T(8,128)(2,1)S(1)}, u32[]{:S(2)}, u32[]{:S(2)}) collective-permute-start(bf16[40,3072]{1,0:T(8,128)(2,1)S(1)} %add_convert_fusion.9), channel_id=1, source_target_pairs={{0,8},{1,25},{2,10},{3,27},{4,12},{5,29},{6,14},{7,31},{8,0},{9,17... | collective-permute-start | bytes 737288 | tf_op jit(solution)/shard_map/ppermute | solution.py:231
  92.4 13.9 %collective-permute-start.16 = (bf16[768,384]{1,0:T(8,128)(2,1)S(1)}, bf16[768,384]{1,0:T(8,128)(2,1)S(1)}, u32[]{:S(2)}, u32[]{:S(2)}) collective-permute-start(bf16[768,384]{1,0:T(8,128)(2,1)S(1)} %add_convert_fusion), channel_id=1, source_target_pairs={{0,224},{1,33},{2,226},{3,35},{4,228},{5,37},{6,230},{7,39},{8,232... | collective-permute-start | bytes 1769480 | tf_op jit(solution)/shard_map/ppermute | solution.py:231
  94.4 11.4 %collective-permute-start.15 = (bf16[40,3072]{1,0:T(8,128)(2,1)S(1)}, bf16[40,3072]{1,0:T(8,128)(2,1)S(1)}, u32[]{:S(2)}, u32[]{:S(2)}) collective-permute-start(bf16[40,3072]{1,0:T(8,128)(2,1)S(1)} %add_convert_fusion.8.left), channel_id=1, source_target_pairs={{0,24},{1,9},{2,26},{3,11},{4,28},{5,13},{6,30},{7,15},{8,16},{9,1... | collective-permute-start | bytes 737288 | tf_op jit(solution)/shard_map/ppermute | solution.py:231
  106.4 6.9 %collective-permute-start.17 = (bf16[40,3072]{1,0:T(8,128)(2,1)S(1)}, bf16[40,3072]{1,0:T(8,128)(2,1)S(1)}, u32[]{:S(2)}, u32[]{:S(2)}) collective-permute-start(bf16[40,3072]{1,0:T(8,128)(2,1)S(1)} %back.1), channel_id=1, source_target_pairs={{0,6},{1,3},{2,4},{3,1},{4,2},{5,7},{6,0},{7,5},{8,14},{9,11},{10,... | collective-permute-start | bytes 737288 | tf_op jit(solution)/shard_map/ppermute | solution.py:231
  108.3 9.0 %collective-permute-start.19 = (bf16[384,384]{1,0:T(8,128)(2,1)S(1)}, bf16[384,384]{1,0:T(8,128)(2,1)S(1)}, u32[]{:S(2)}, u32[]{:S(2)}) collective-permute-start(bf16[384,384]{1,0:T(8,128)(2,1)S(1)} %add_convert_fusion.7), channel_id=1, source_target_pairs={{0,32},{1,225},{2,34},{3,227},{4,36},{5,229},{6,38},{7,231},{8,40}... | collective-permute-start | bytes 884744 | tf_op jit(solution)/shard_map/ppermute | solution.py:231
  113.4 11.0 %collective-permute-start.18 = (bf16[80,3072]{1,0:T(8,128)(2,1)S(1)}, bf16[80,3072]{1,0:T(8,128)(2,1)S(1)}, u32[]{:S(2)}, u32[]{:S(2)}) collective-permute-start(bf16[80,3072]{1,0:T(8,128)(2,1)S(1)} %pad_maximum_fusion.2), channel_id=1, source_target_pairs={{0,2},{1,7},{2,0},{3,5},{4,6},{5,3},{6,4},{7,1},{8,10},{9,15},{10,... | collective-permute-start | bytes 1474568 | tf_op jit(solution)/shard_map/ppermute | solution.py:231
  117.5 6.2 %collective-permute-start.20 = (bf16[192,384]{1,0:T(8,128)(2,1)S(1)}, bf16[192,384]{1,0:T(8,128)(2,1)S(1)}, u32[]{:S(2)}, u32[]{:S(2)}) collective-permute-start(bf16[192,384]{1,0:T(8,128)(2,1)S(1)} %broadcast_select_fusion.6), channel_id=1, source_target_pairs={{0,256},{1,257},{2,258},{3,259},{4,260},{5,261},{6,262},{7,263},{8... | collective-permute-start | bytes 442376 | tf_op jit(solution)/shard_map/ppermute | solution.py:231
  124.6 10.2 %collective-permute-start.21 = (bf16[160,3072]{1,0:T(8,128)(2,1)S(1)}, bf16[160,3072]{1,0:T(8,128)(2,1)S(1)}, u32[]{:S(2)}, u32[]{:S(2)}) collective-permute-start(bf16[160,3072]{1,0:T(8,128)(2,1)S(1)} %pad_maximum_fusion.1), channel_id=1, source_target_pairs={{0,1},{1,0},{2,3},{3,2},{4,5},{5,4},{6,7},{7,6},{8,9},{9,8},{10,11... | collective-permute-start | bytes 2949128 | tf_op jit(solution)/shard_map/ppermute | solution.py:231

commit v5 on v4

--- a/solution.py
+++ b/solution.py
@@ -340,10 +340,11 @@
     depth = zero.shape[0] // 2
     low, high = zero[:depth], zero[depth:]
     got = swap(own, by_x(1))
-    across = swap(jnp.where(first_y, high, low), by_y_lo).astype(jnp.float32)
-    grad_w_qkv = jnp.where(first_y, low, high).astype(jnp.float32) + across
-    own = after(join(own, got, first_outer), grad_w_qkv)
-    return (join(own, swap(own, by_core), first_core), grad_w_qkv)
+    across = swap(jnp.where(first_y, high, low), by_y_lo)
+    own = after(join(own, got, first_outer), across)
+    got = swap(own, by_core)
+    grad_w_qkv = jnp.where(first_y, low, high).astype(jnp.float32) + across.astype(jnp.float32)
+    return (join(own, got, first_core), grad_w_qkv)
 
 
 def solution(mesh):

time: 138 us -> 138 us (level)
  no operation moved by 1% of the time
where the time goes in v5:
time: 138 us; the launch traced here: 135 us
  starting transfers between devices  82.3 us (60%)
  waiting for transfers between devices  35.3 us (26%)
  Pallas kernels  8.53 us (6%)
  other arithmetic  4.54 us (3%)
  local copies, waits for them, and re-layouts  3.47 us (3%)
    ppermute x22, starting transfers between devices, swap(): return lax.ppermute(values, AXES, pairs_of(partner))  82.3 us
    ppermute x22, waiting for transfers between devices, swap(): return lax.ppermute(values, AXES, pairs_of(partner))  35.3 us
    pallas_call x1, Pallas kernels, run_head(): pl.pallas_call(head_kernel, out_shape=(like(tokens, width), like(tokens /...  4.58 us
  transfers between devices with their start and end apart: 22, of which 15 were waited for; matrix products, arithmetic and copies ran while one was open for 3% of the time, Pallas kernels for 3%

profile of v5, /device:TPU:1, one launch (start us, length us, event | category | flops | bytes accessed | tf_op | source)
XLA Modules:
  0.0 135.3 jit_solution(16365197213541165816)
XLA Ops:
  0.8 0.1 stack.27.places
  0.9 4.0 %collective-permute-start.4 = (bf16[192,384]{1,0:T(8,128)(2,1)}, bf16[192,384]{1,0:T(8,128)(2,1)S(1)}, u32[]{:S(2)}, u32[]{:S(2)}) collective-permute-start(bf16[192,384]{1,0:T(8,128)(2,1)} %refs_0_), channel_id=1, source_target_pairs={{0,256},{1,257},{2,258},{3,259},{4,260},{5,261},{6,262},{7,263},{8... | collective-permute-start | bytes 442376 | tf_op jit(solution)/shard_map/ppermute | solution.py:231
  4.9 10.7 %collective-permute-start = (bf16[192,384]{1,0:T(8,128)(2,1)}, bf16[192,384]{1,0:T(8,128)(2,1)S(1)}, u32[]{:S(2)}, u32[]{:S(2)}) collective-permute-start(bf16[192,384]{1,0:T(8,128)(2,1)} %refs_0_), channel_id=1, source_target_pairs={{0,32},{1,225},{2,34},{3,227},{4,36},{5,229},{6,38},{7,231},{8,40}... | collective-permute-start | bytes 442376 | tf_op jit(solution)/shard_map/ppermute | solution.py:231
  15.6 3.6 %collective-permute-start.5 = (bf16[192,384]{1,0:T(8,128)(2,1)S(1)}, bf16[192,384]{1,0:T(8,128)(2,1)S(1)}, u32[]{:S(2)}, u32[]{:S(2)}) collective-permute-start(bf16[192,384]{1,0:T(8,128)(2,1)S(1)} %collective-permute-done.4.refs_5_), channel_id=1, source_target_pairs={{0,32},{1,225},{2,34},{3,227},{4,36},{5,229},{6,38},{7,231},{8,40}... | collective-permute-start | bytes 442376 | tf_op jit(solution)/shard_map/ppermute | solution.py:231
  19.2 0.0 collective-permute-done.refs_1_
  19.2 0.9 pad_maximum_fusion.3
  20.1 1.9 %collective-permute-start.1 = (bf16[384,384]{1,0:T(8,128)(2,1)S(1)}, bf16[384,384]{1,0:T(8,128)(2,1)S(1)}, u32[]{:S(2)}, u32[]{:S(2)}) collective-permute-start(bf16[384,384]{1,0:T(8,128)(2,1)S(1)} %pad_maximum_fusion.3), channel_id=1, source_target_pairs={{0,224},{1,33},{2,226},{3,35},{4,228},{5,37},{6,230},{7,39},{8,232... | collective-permute-start | bytes 884744 | tf_op jit(solution)/shard_map/ppermute | solution.py:231
  22.0 0.6 collective-permute-done.5.refs_6_
  22.7 2.7 %collective-permute-start.6 = (bf16[384,384]{1,0:T(8,128)(2,1)S(1)}, bf16[384,384]{1,0:T(8,128)(2,1)S(1)}, u32[]{:S(2)}, u32[]{:S(2)}) collective-permute-start(bf16[384,384]{1,0:T(8,128)(2,1)S(1)} %pad_maximum_fusion.4), channel_id=1, source_target_pairs={{0,224},{1,33},{2,226},{3,35},{4,228},{5,37},{6,230},{7,39},{8,232... | collective-permute-start | bytes 884744 | tf_op jit(solution)/shard_map/ppermute | solution.py:231
  25.5 2.4 %collective-permute-done.1.refs_2_ = bf16[384,384]{1,0:T(8,128)(2,1)S(1)} collective-permute-done((bf16[384,384]{1,0:T(8,128)(2,1)S(1)}, bf16[384,384]{1,0:T(8,128)(2,1)S(1)}, u32[]{:S(2)}, u32[]{:S(2)}) %collective-permute-start.1) | collective-permute-done | bytes 294944 | tf_op jit(solution)/shard_map/ppermute | solution.py:231
  27.9 3.7 %collective-permute-start.2 = (bf16[384,384]{1,0:T(8,128)(2,1)S(1)}, bf16[384,384]{1,0:T(8,128)(2,1)S(1)}, u32[]{:S(2)}, u32[]{:S(2)}) collective-permute-start(bf16[384,384]{1,0:T(8,128)(2,1)S(1)} %collective-permute-done.1.refs_2_), channel_id=1, source_target_pairs={{0,32},{1,225},{2,34},{3,227},{4,36},{5,229},{6,38},{7,231},{8,40}... | collective-permute-start | bytes 884744 | tf_op jit(solution)/shard_map/ppermute | solution.py:231
  31.6 3.1 %collective-permute-start.7 = (bf16[384,384]{1,0:T(8,128)(2,1)S(1)}, bf16[384,384]{1,0:T(8,128)(2,1)S(1)}, u32[]{:S(2)}, u32[]{:S(2)}) collective-permute-start(bf16[384,384]{1,0:T(8,128)(2,1)S(1)} %collective-permute-done.6.refs_7_), channel_id=1, source_target_pairs={{0,32},{1,225},{2,34},{3,227},{4,36},{5,229},{6,38},{7,231},{8,40}... | collective-permute-start | bytes 884744 | tf_op jit(solution)/shard_map/ppermute | solution.py:231
  34.7 2.6 %collective-permute-done.2.refs_3_ = bf16[384,384]{1,0:T(8,128)(2,1)S(1)} collective-permute-done((bf16[384,384]{1,0:T(8,128)(2,1)S(1)}, bf16[384,384]{1,0:T(8,128)(2,1)S(1)}, u32[]{:S(2)}, u32[]{:S(2)}) %collective-permute-start.2) | collective-permute-done | bytes 294944 | tf_op jit(solution)/shard_map/ppermute | solution.py:231
  37.3 1.9 %collective-permute-start.3 = (bf16[384,384]{1,0:T(8,128)(2,1)S(1)}, bf16[384,384]{1,0:T(8,128)(2,1)S(1)}, u32[]{:S(2)}, u32[]{:S(2)}) collective-permute-start(bf16[384,384]{1,0:T(8,128)(2,1)S(1)} %collective-permute-done.2.refs_3_), channel_id=1, source_target_pairs={{0,224},{1,33},{2,226},{3,35},{4,228},{5,37},{6,230},{7,39},{8,232... | collective-permute-start | bytes 884744 | tf_op jit(solution)/shard_map/ppermute | solution.py:231
  39.3 1.2 collective-permute-done.7.refs_8_
  40.5 2.1 %collective-permute-start.8 = (bf16[384,384]{1,0:T(8,128)(2,1)S(1)}, bf16[384,384]{1,0:T(8,128)(2,1)S(1)}, u32[]{:S(2)}, u32[]{:S(2)}) collective-permute-start(bf16[384,384]{1,0:T(8,128)(2,1)S(1)} %collective-permute-done.7.refs_8_), channel_id=1, source_target_pairs={{0,224},{1,33},{2,226},{3,35},{4,228},{5,37},{6,230},{7,39},{8,232... | collective-permute-start | bytes 884744 | tf_op jit(solution)/shard_map/ppermute | solution.py:231
  42.6 0.0 copy-start
  42.7 1.5 %copy-done = bf16[320,3072]{1,0:T(8,128)(2,1)S(1)} copy-done((bf16[320,3072]{1,0:T(8,128)(2,1)S(1)}, bf16[320,3072]{1,0:T(8,128)(2,1)}, u32[]{:S(2)}) %copy-start) | copy-done | bytes 1966104
  44.2 0.7 copy-done.3
  44.9 1.3 norm.1.normed
  46.2 0.8 collective-permute-done.3.refs_4_
  47.0 2.9 %collective-permute-done.8.refs_9_ = bf16[384,384]{1,0:T(8,128)(2,1)S(1)} collective-permute-done((bf16[384,384]{1,0:T(8,128)(2,1)S(1)}, bf16[384,384]{1,0:T(8,128)(2,1)S(1)}, u32[]{:S(2)}, u32[]{:S(2)}) %collective-permute-start.8) | collective-permute-done | bytes 294944 | tf_op jit(solution)/shard_map/ppermute | solution.py:231
  49.9 4.6 %head.1 = (bf16[320,384]{1,0:T(8,128)(2,1)S(1)}, bf16[80,3072]{1,0:T(8,128)(2,1)S(1)}, bf16[80,3072]{1,0:T(8,128)(2,1)S(1)}, bf16[160,3072]{1,0:T(8,128)(2,1)S(1)}) custom-call(s32[6]{0:T(128)S(1)} %stack.27.places, bf16[320,3072]{1,0:T(8,128)(2,1)S(1)} %norm.1.normed, bf16[320,128]{1,0:T(8,128)(2,1)S(1)} %copy-done.2, f32[1,128]{1,0:T(1,128)S(1)} %bitcast.11, ...), custom_call_target="tpu_custom_call" | custom-call | flops 1132462080 | bytes 8388608 | tf_op jit(solution)/shard_map/head/pallas_call | solution.py:114
  54.4 7.9 %collective-permute-start.9 = (bf16[160,3072]{1,0:T(8,128)(2,1)S(1)}, bf16[160,3072]{1,0:T(8,128)(2,1)S(1)}, u32[]{:S(2)}, u32[]{:S(2)}) collective-permute-start(bf16[160,3072]{1,0:T(8,128)(2,1)S(1)} %get-tuple-element.29), channel_id=1, source_target_pairs={{0,1},{1,0},{2,3},{3,2},{4,5},{5,4},{6,7},{7,6},{8,9},{9,8},{10,11... | collective-permute-start | bytes 2949128 | tf_op jit(solution)/shard_map/ppermute | solution.py:231
  62.4 2.2 %terms.1 = bf16[3072,384]{1,0:T(8,128)(2,1)S(1)} custom-call(s32[6]{0:T(128)S(1)} %stack.27.places, bf16[320,3072]{1,0:T(8,128)(2,1)S(1)} %norm.1.normed, bf16[320,384]{1,0:T(8,128)(2,1)S(1)} %get-tuple-element.31.grads), custom_call_target="tpu_custom_call" | custom-call | flops 754974720 | bytes 5242880 | tf_op jit(solution)/shard_map/terms/pallas_call | solution.py:173
  64.6 0.1 add_convert_fusion.4
  64.7 4.4 %collective-permute-start.10 = (bf16[80,3072]{1,0:T(8,128)(2,1)S(1)}, bf16[80,3072]{1,0:T(8,128)(2,1)S(1)}, u32[]{:S(2)}, u32[]{:S(2)}) collective-permute-start(bf16[80,3072]{1,0:T(8,128)(2,1)S(1)} %add_convert_fusion.4), channel_id=1, source_target_pairs={{0,2},{1,7},{2,0},{3,5},{4,6},{5,3},{6,4},{7,1},{8,10},{9,15},{10,... | collective-permute-start | bytes 1474568 | tf_op jit(solution)/shard_map/ppermute | solution.py:231
  69.1 0.1 split.21
  69.2 1.9 %collective-permute-start.12 = (bf16[768,384]{1,0:T(8,128)(2,1)S(1)}, bf16[768,384]{1,0:T(8,128)(2,1)S(1)}, u32[]{:S(2)}, u32[]{:S(2)}) collective-permute-start(bf16[768,384]{1,0:T(8,128)(2,1)S(1)} %split.21), channel_id=1, source_target_pairs={{0,224},{1,33},{2,226},{3,35},{4,228},{5,37},{6,230},{7,39},{8,232... | collective-permute-start | bytes 1769480 | tf_op jit(solution)/shard_map/ppermute | solution.py:231
  71.1 4.7 %collective-permute-done.10 = bf16[80,3072]{1,0:T(8,128)(2,1)S(1)} collective-permute-done((bf16[80,3072]{1,0:T(8,128)(2,1)S(1)}, bf16[80,3072]{1,0:T(8,128)(2,1)S(1)}, u32[]{:S(2)}, u32[]{:S(2)}) %collective-permute-start.10) | collective-permute-done | bytes 491552 | tf_op jit(solution)/shard_map/ppermute | solution.py:231
  75.8 0.2 add_convert_fusion.2
  76.0 1.9 %collective-permute-start.11 = (bf16[40,3072]{1,0:T(8,128)(2,1)S(1)}, bf16[40,3072]{1,0:T(8,128)(2,1)S(1)}, u32[]{:S(2)}, u32[]{:S(2)}) collective-permute-start(bf16[40,3072]{1,0:T(8,128)(2,1)S(1)} %slice.34), channel_id=1, source_target_pairs={{0,6},{1,3},{2,4},{3,1},{4,2},{5,7},{6,0},{7,5},{8,14},{9,11},{10,... | collective-permute-start | bytes 737288 | tf_op jit(solution)/shard_map/ppermute | solution.py:231
  78.0 2.2 %collective-permute-done.12 = bf16[768,384]{1,0:T(8,128)(2,1)S(1)} collective-permute-done((bf16[768,384]{1,0:T(8,128)(2,1)S(1)}, bf16[768,384]{1,0:T(8,128)(2,1)S(1)}, u32[]{:S(2)}, u32[]{:S(2)}) %collective-permute-start.12) | collective-permute-done | bytes 589856 | tf_op jit(solution)/shard_map/ppermute | solution.py:231
  80.1 0.1 add_convert_fusion.1
  80.3 0.0 copy-start.4
  80.3 1.9 %collective-permute-start.14 = (bf16[768,384]{1,0:T(8,128)(2,1)S(1)}, bf16[768,384]{1,0:T(8,128)(2,1)S(1)}, u32[]{:S(2)}, u32[]{:S(2)}) collective-permute-start(bf16[768,384]{1,0:T(8,128)(2,1)S(1)} %add_convert_fusion.1), channel_id=1, source_target_pairs={{0,32},{1,225},{2,34},{3,227},{4,36},{5,229},{6,38},{7,231},{8,40}... | collective-permute-start | bytes 1769480 | tf_op jit(solution)/shard_map/ppermute | solution.py:231
  82.2 1.0 collective-permute-done.11
  83.3 0.1 add_convert_fusion.9
  83.3 5.5 %collective-permute-start.13 = (bf16[40,3072]{1,0:T(8,128)(2,1)S(1)}, bf16[40,3072]{1,0:T(8,128)(2,1)S(1)}, u32[]{:S(2)}, u32[]{:S(2)}) collective-permute-start(bf16[40,3072]{1,0:T(8,128)(2,1)S(1)} %add_convert_fusion.9), channel_id=1, source_target_pairs={{0,8},{1,25},{2,10},{3,27},{4,12},{5,29},{6,14},{7,31},{8,0},{9,17... | collective-permute-start | bytes 737288 | tf_op jit(solution)/shard_map/ppermute | solution.py:231
  88.8 3.4 %collective-permute-done.14 = bf16[768,384]{1,0:T(8,128)(2,1)S(1)} collective-permute-done((bf16[768,384]{1,0:T(8,128)(2,1)S(1)}, bf16[768,384]{1,0:T(8,128)(2,1)S(1)}, u32[]{:S(2)}, u32[]{:S(2)}) %collective-permute-start.14) | collective-permute-done | bytes 589856 | tf_op jit(solution)/shard_map/ppermute | solution.py:231
  92.3 0.2 add_convert_fusion
  92.4 1.9 %collective-permute-start.16 = (bf16[768,384]{1,0:T(8,128)(2,1)S(1)}, bf16[768,384]{1,0:T(8,128)(2,1)S(1)}, u32[]{:S(2)}, u32[]{:S(2)}) collective-permute-start(bf16[768,384]{1,0:T(8,128)(2,1)S(1)} %add_convert_fusion), channel_id=1, source_target_pairs={{0,224},{1,33},{2,226},{3,35},{4,228},{5,37},{6,230},{7,39},{8,232... | collective-permute-start | bytes 1769480 | tf_op jit(solution)/shard_map/ppermute | solution.py:231
  94.4 0.0 collective-permute-done.13
  94.4 0.1 add_convert_fusion.8.left
  94.4 4.9 %collective-permute-start.15 = (bf16[40,3072]{1,0:T(8,128)(2,1)S(1)}, bf16[40,3072]{1,0:T(8,128)(2,1)S(1)}, u32[]{:S(2)}, u32[]{:S(2)}) collective-permute-start(bf16[40,3072]{1,0:T(8,128)(2,1)S(1)} %add_convert_fusion.8.left), channel_id=1, source_target_pairs={{0,24},{1,9},{2,26},{3,11},{4,28},{5,13},{6,30},{7,15},{8,16},{9,1... | collective-permute-start | bytes 737288 | tf_op jit(solution)/shard_map/ppermute | solution.py:231
  99.3 1.0 constant_dynamic-slice_fusion.inputs
  100.3 5.5 %collective-permute-done.15.right = bf16[40,3072]{1,0:T(8,128)(2,1)S(1)} collective-permute-done((bf16[40,3072]{1,0:T(8,128)(2,1)S(1)}, bf16[40,3072]{1,0:T(8,128)(2,1)S(1)}, u32[]{:S(2)}, u32[]{:S(2)}) %collective-permute-start.15) | collective-permute-done | bytes 245792 | tf_op jit(solution)/shard_map/ppermute | solution.py:231
  105.9 0.4 back.1
  106.3 0.1 add_convert_fusion.7
  106.4 1.9 %collective-permute-start.17 = (bf16[40,3072]{1,0:T(8,128)(2,1)S(1)}, bf16[40,3072]{1,0:T(8,128)(2,1)S(1)}, u32[]{:S(2)}, u32[]{:S(2)}) collective-permute-start(bf16[40,3072]{1,0:T(8,128)(2,1)S(1)} %back.1), channel_id=1, source_target_pairs={{0,6},{1,3},{2,4},{3,1},{4,2},{5,7},{6,0},{7,5},{8,14},{9,11},{10,... | collective-permute-start | bytes 737288 | tf_op jit(solution)/shard_map/ppermute | solution.py:231
  108.3 3.4 %collective-permute-start.19 = (bf16[384,384]{1,0:T(8,128)(2,1)S(1)}, bf16[384,384]{1,0:T(8,128)(2,1)S(1)}, u32[]{:S(2)}, u32[]{:S(2)}) collective-permute-start(bf16[384,384]{1,0:T(8,128)(2,1)S(1)} %add_convert_fusion.7), channel_id=1, source_target_pairs={{0,32},{1,225},{2,34},{3,227},{4,36},{5,229},{6,38},{7,231},{8,40}... | collective-permute-start | bytes 884744 | tf_op jit(solution)/shard_map/ppermute | solution.py:231
  111.8 1.6 %collective-permute-done.17 = bf16[40,3072]{1,0:T(8,128)(2,1)S(1)} collective-permute-done((bf16[40,3072]{1,0:T(8,128)(2,1)S(1)}, bf16[40,3072]{1,0:T(8,128)(2,1)S(1)}, u32[]{:S(2)}, u32[]{:S(2)}) %collective-permute-start.17) | collective-permute-done | bytes 245792 | tf_op jit(solution)/shard_map/ppermute | solution.py:231
  113.4 3.7 %collective-permute-start.18 = (bf16[80,3072]{1,0:T(8,128)(2,1)S(1)}, bf16[80,3072]{1,0:T(8,128)(2,1)S(1)}, u32[]{:S(2)}, u32[]{:S(2)}) collective-permute-start(bf16[80,3072]{1,0:T(8,128)(2,1)S(1)} %pad_maximum_fusion.2), channel_id=1, source_target_pairs={{0,2},{1,7},{2,0},{3,5},{4,6},{5,3},{6,4},{7,1},{8,10},{9,15},{10,... | collective-permute-start | bytes 1474568 | tf_op jit(solution)/shard_map/ppermute | solution.py:231
  117.1 0.2 collective-permute-done.19
  117.3 0.1 add_convert_fusion.5
  117.5 1.9 %collective-permute-start.20 = (bf16[192,384]{1,0:T(8,128)(2,1)S(1)}, bf16[192,384]{1,0:T(8,128)(2,1)S(1)}, u32[]{:S(2)}, u32[]{:S(2)}) collective-permute-start(bf16[192,384]{1,0:T(8,128)(2,1)S(1)} %broadcast_select_fusion.6), channel_id=1, source_target_pairs={{0,256},{1,257},{2,258},{3,259},{4,260},{5,261},{6,262},{7,263},{8... | collective-permute-start | bytes 442376 | tf_op jit(solution)/shard_map/ppermute | solution.py:231
  119.4 4.8 %collective-permute-done.18 = bf16[80,3072]{1,0:T(8,128)(2,1)S(1)} collective-permute-done((bf16[80,3072]{1,0:T(8,128)(2,1)S(1)}, bf16[80,3072]{1,0:T(8,128)(2,1)S(1)}, u32[]{:S(2)}, u32[]{:S(2)}) %collective-permute-start.18) | collective-permute-done | bytes 491552 | tf_op jit(solution)/shard_map/ppermute | solution.py:231
  124.2 0.2 broadcast_select_fusion.3
  124.4 0.1 pad_maximum_fusion.1
  124.5 7.1 %collective-permute-start.21 = (bf16[160,3072]{1,0:T(8,128)(2,1)S(1)}, bf16[160,3072]{1,0:T(8,128)(2,1)S(1)}, u32[]{:S(2)}, u32[]{:S(2)}) collective-permute-start(bf16[160,3072]{1,0:T(8,128)(2,1)S(1)} %pad_maximum_fusion.1), channel_id=1, source_target_pairs={{0,1},{1,0},{2,3},{3,2},{4,5},{5,4},{6,7},{7,6},{8,9},{9,8},{10,11... | collective-permute-start | bytes 2949128 | tf_op jit(solution)/shard_map/ppermute | solution.py:231
  131.6 0.8 convert_add_fusion
  132.4 1.4 %collective-permute-done.21 = bf16[160,3072]{1,0:T(8,128)(2,1)S(1)} collective-permute-done((bf16[160,3072]{1,0:T(8,128)(2,1)S(1)}, bf16[160,3072]{1,0:T(8,128)(2,1)S(1)}, u32[]{:S(2)}, u32[]{:S(2)}) %collective-permute-start.21) | collective-permute-done | bytes 983072 | tf_op jit(solution)/shard_map/ppermute | solution.py:231
  133.8 0.1 broadcast_select_fusion.1
  133.9 1.4 %pad_maximum_fusion = bf16[320,3072]{1,0:T(8,128)(2,1)} fusion(bf16[160,3072]{1,0:T(8,128)(2,1)S(1)} %get-tuple-element.45, bf16[160,3072]{1,0:T(8,128)(2,1)S(1)} %get-tuple-element.44), kind=kLoop, calls=%fused_computation | loop fusion | flops 3932160 | bytes 3932160 | tf_op jit(solution)/shard_map/concatenate | solution.py:271
  (20 shorter events, 0.2 us)
Async XLA Ops:
  0.9 14.7 %collective-permute-start.4 = (bf16[192,384]{1,0:T(8,128)(2,1)}, bf16[192,384]{1,0:T(8,128)(2,1)S(1)}, u32[]{:S(2)}, u32[]{:S(2)}) collective-permute-start(bf16[192,384]{1,0:T(8,128)(2,1)} %refs_0_), channel_id=1, source_target_pairs={{0,256},{1,257},{2,258},{3,259},{4,260},{5,261},{6,262},{7,263},{8... | collective-permute-start | bytes 442376 | tf_op jit(solution)/shard_map/ppermute | solution.py:231
  4.9 14.3 %collective-permute-start = (bf16[192,384]{1,0:T(8,128)(2,1)}, bf16[192,384]{1,0:T(8,128)(2,1)S(1)}, u32[]{:S(2)}, u32[]{:S(2)}) collective-permute-start(bf16[192,384]{1,0:T(8,128)(2,1)} %refs_0_), channel_id=1, source_target_pairs={{0,32},{1,225},{2,34},{3,227},{4,36},{5,229},{6,38},{7,231},{8,40}... | collective-permute-start | bytes 442376 | tf_op jit(solution)/shard_map/ppermute | solution.py:231
  15.6 7.1 %collective-permute-start.5 = (bf16[192,384]{1,0:T(8,128)(2,1)S(1)}, bf16[192,384]{1,0:T(8,128)(2,1)S(1)}, u32[]{:S(2)}, u32[]{:S(2)}) collective-permute-start(bf16[192,384]{1,0:T(8,128)(2,1)S(1)} %collective-permute-done.4.refs_5_), channel_id=1, source_target_pairs={{0,32},{1,225},{2,34},{3,227},{4,36},{5,229},{6,38},{7,231},{8,40}... | collective-permute-start | bytes 442376 | tf_op jit(solution)/shard_map/ppermute | solution.py:231
  20.1 7.8 %collective-permute-start.1 = (bf16[384,384]{1,0:T(8,128)(2,1)S(1)}, bf16[384,384]{1,0:T(8,128)(2,1)S(1)}, u32[]{:S(2)}, u32[]{:S(2)}) collective-permute-start(bf16[384,384]{1,0:T(8,128)(2,1)S(1)} %pad_maximum_fusion.3), channel_id=1, source_target_pairs={{0,224},{1,33},{2,226},{3,35},{4,228},{5,37},{6,230},{7,39},{8,232... | collective-permute-start | bytes 884744 | tf_op jit(solution)/shard_map/ppermute | solution.py:231
  22.7 8.9 %collective-permute-start.6 = (bf16[384,384]{1,0:T(8,128)(2,1)S(1)}, bf16[384,384]{1,0:T(8,128)(2,1)S(1)}, u32[]{:S(2)}, u32[]{:S(2)}) collective-permute-start(bf16[384,384]{1,0:T(8,128)(2,1)S(1)} %pad_maximum_fusion.4), channel_id=1, source_target_pairs={{0,224},{1,33},{2,226},{3,35},{4,228},{5,37},{6,230},{7,39},{8,232... | collective-permute-start | bytes 884744 | tf_op jit(solution)/shard_map/ppermute | solution.py:231
  27.9 9.5 %collective-permute-start.2 = (bf16[384,384]{1,0:T(8,128)(2,1)S(1)}, bf16[384,384]{1,0:T(8,128)(2,1)S(1)}, u32[]{:S(2)}, u32[]{:S(2)}) collective-permute-start(bf16[384,384]{1,0:T(8,128)(2,1)S(1)} %collective-permute-done.1.refs_2_), channel_id=1, source_target_pairs={{0,32},{1,225},{2,34},{3,227},{4,36},{5,229},{6,38},{7,231},{8,40}... | collective-permute-start | bytes 884744 | tf_op jit(solution)/shard_map/ppermute | solution.py:231
  31.6 8.9 %collective-permute-start.7 = (bf16[384,384]{1,0:T(8,128)(2,1)S(1)}, bf16[384,384]{1,0:T(8,128)(2,1)S(1)}, u32[]{:S(2)}, u32[]{:S(2)}) collective-permute-start(bf16[384,384]{1,0:T(8,128)(2,1)S(1)} %collective-permute-done.6.refs_7_), channel_id=1, source_target_pairs={{0,32},{1,225},{2,34},{3,227},{4,36},{5,229},{6,38},{7,231},{8,40}... | collective-permute-start | bytes 884744 | tf_op jit(solution)/shard_map/ppermute | solution.py:231
  37.3 9.6 %collective-permute-start.3 = (bf16[384,384]{1,0:T(8,128)(2,1)S(1)}, bf16[384,384]{1,0:T(8,128)(2,1)S(1)}, u32[]{:S(2)}, u32[]{:S(2)}) collective-permute-start(bf16[384,384]{1,0:T(8,128)(2,1)S(1)} %collective-permute-done.2.refs_3_), channel_id=1, source_target_pairs={{0,224},{1,33},{2,226},{3,35},{4,228},{5,37},{6,230},{7,39},{8,232... | collective-permute-start | bytes 884744 | tf_op jit(solution)/shard_map/ppermute | solution.py:231
  40.5 9.3 %collective-permute-start.8 = (bf16[384,384]{1,0:T(8,128)(2,1)S(1)}, bf16[384,384]{1,0:T(8,128)(2,1)S(1)}, u32[]{:S(2)}, u32[]{:S(2)}) collective-permute-start(bf16[384,384]{1,0:T(8,128)(2,1)S(1)} %collective-permute-done.7.refs_8_), channel_id=1, source_target_pairs={{0,224},{1,33},{2,226},{3,35},{4,228},{5,37},{6,230},{7,39},{8,232... | collective-permute-start | bytes 884744 | tf_op jit(solution)/shard_map/ppermute | solution.py:231
  42.6 1.5 %copy-start = (bf16[320,3072]{1,0:T(8,128)(2,1)S(1)}, bf16[320,3072]{1,0:T(8,128)(2,1)}, u32[]{:S(2)}) copy-start(bf16[320,3072]{1,0:T(8,128)(2,1)} %inputs.1) | copy-start | bytes 5898244
  44.2 0.7 copy-start.3
  44.9 4.9 %copy-start.1 = (bf16[192,384]{1,0:T(8,128)(2,1)S(1)}, bf16[192,384]{1,0:T(8,128)(2,1)}, u32[]{:S(2)}) copy-start(bf16[192,384]{1,0:T(8,128)(2,1)} %refs_0_) | copy-start | bytes 442372
  44.9 4.9 %copy-start.2 = (bf16[320,128]{1,0:T(8,128)(2,1)S(1)}, bf16[320,128]{1,0:T(8,128)(2,1)}, u32[]{:S(2)}) copy-start(bf16[320,128]{1,0:T(8,128)(2,1)} %cot.1) | copy-start | bytes 245764
  44.9 4.9 %copy-start.5 = (f32[128]{0:T(128)S(1)}, f32[128]{0:T(128)}, u32[]{:S(2)}) copy-start(f32[128]{0:T(128)} %param.9) | copy-start | bytes 1540
  44.9 4.9 %copy-start.6 = (f32[128]{0:T(128)S(1)}, f32[128]{0:T(128)}, u32[]{:S(2)}) copy-start(f32[128]{0:T(128)} %param.10) | copy-start | bytes 1540
  54.4 10.2 %collective-permute-start.9 = (bf16[160,3072]{1,0:T(8,128)(2,1)S(1)}, bf16[160,3072]{1,0:T(8,128)(2,1)S(1)}, u32[]{:S(2)}, u32[]{:S(2)}) collective-permute-start(bf16[160,3072]{1,0:T(8,128)(2,1)S(1)} %get-tuple-element.29), channel_id=1, source_target_pairs={{0,1},{1,0},{2,3},{3,2},{4,5},{5,4},{6,7},{7,6},{8,9},{9,8},{10,11... | collective-permute-start | bytes 2949128 | tf_op jit(solution)/shard_map/ppermute | solution.py:231
  64.7 11.1 %collective-permute-start.10 = (bf16[80,3072]{1,0:T(8,128)(2,1)S(1)}, bf16[80,3072]{1,0:T(8,128)(2,1)S(1)}, u32[]{:S(2)}, u32[]{:S(2)}) collective-permute-start(bf16[80,3072]{1,0:T(8,128)(2,1)S(1)} %add_convert_fusion.4), channel_id=1, source_target_pairs={{0,2},{1,7},{2,0},{3,5},{4,6},{5,3},{6,4},{7,1},{8,10},{9,15},{10,... | collective-permute-start | bytes 1474568 | tf_op jit(solution)/shard_map/ppermute | solution.py:231
  69.2 10.9 %collective-permute-start.12 = (bf16[768,384]{1,0:T(8,128)(2,1)S(1)}, bf16[768,384]{1,0:T(8,128)(2,1)S(1)}, u32[]{:S(2)}, u32[]{:S(2)}) collective-permute-start(bf16[768,384]{1,0:T(8,128)(2,1)S(1)} %split.21), channel_id=1, source_target_pairs={{0,224},{1,33},{2,226},{3,35},{4,228},{5,37},{6,230},{7,39},{8,232... | collective-permute-start | bytes 1769480 | tf_op jit(solution)/shard_map/ppermute | solution.py:231
  76.0 7.2 %collective-permute-start.11 = (bf16[40,3072]{1,0:T(8,128)(2,1)S(1)}, bf16[40,3072]{1,0:T(8,128)(2,1)S(1)}, u32[]{:S(2)}, u32[]{:S(2)}) collective-permute-start(bf16[40,3072]{1,0:T(8,128)(2,1)S(1)} %slice.34), channel_id=1, source_target_pairs={{0,6},{1,3},{2,4},{3,1},{4,2},{5,7},{6,0},{7,5},{8,14},{9,11},{10,... | collective-permute-start | bytes 737288 | tf_op jit(solution)/shard_map/ppermute | solution.py:231
  80.3 25.6 %copy-start.4 = (f32[3072]{0:T(1024)S(1)}, f32[3072]{0:T(1024)}, u32[]{:S(2)}) copy-start(f32[3072]{0:T(1024)} %param.7) | copy-start | bytes 36868
  80.3 12.0 %collective-permute-start.14 = (bf16[768,384]{1,0:T(8,128)(2,1)S(1)}, bf16[768,384]{1,0:T(8,128)(2,1)S(1)}, u32[]{:S(2)}, u32[]{:S(2)}) collective-permute-start(bf16[768,384]{1,0:T(8,128)(2,1)S(1)} %add_convert_fusion.1), channel_id=1, source_target_pairs={{0,32},{1,225},{2,34},{3,227},{4,36},{5,229},{6,38},{7,231},{8,40}... | collective-permute-start | bytes 1769480 | tf_op jit(solution)/shard_map/ppermute | solution.py:231
  83.3 11.1 %collective-permute-start.13 = (bf16[40,3072]{1,0:T(8,128)(2,1)S(1)}, bf16[40,3072]{1,0:T(8,128)(2,1)S(1)}, u32[]{:S(2)}, u32[]{:S(2)}) collective-permute-start(bf16[40,3072]{1,0:T(8,128)(2,1)S(1)} %add_convert_fusion.9), channel_id=1, source_target_pairs={{0,8},{1,25},{2,10},{3,27},{4,12},{5,29},{6,14},{7,31},{8,0},{9,17... | collective-permute-start | bytes 737288 | tf_op jit(solution)/shard_map/ppermute | solution.py:231
  92.4 13.9 %collective-permute-start.16 = (bf16[768,384]{1,0:T(8,128)(2,1)S(1)}, bf16[768,384]{1,0:T(8,128)(2,1)S(1)}, u32[]{:S(2)}, u32[]{:S(2)}) collective-permute-start(bf16[768,384]{1,0:T(8,128)(2,1)S(1)} %add_convert_fusion), channel_id=1, source_target_pairs={{0,224},{1,33},{2,226},{3,35},{4,228},{5,37},{6,230},{7,39},{8,232... | collective-permute-start | bytes 1769480 | tf_op jit(solution)/shard_map/ppermute | solution.py:231
  94.4 11.4 %collective-permute-start.15 = (bf16[40,3072]{1,0:T(8,128)(2,1)S(1)}, bf16[40,3072]{1,0:T(8,128)(2,1)S(1)}, u32[]{:S(2)}, u32[]{:S(2)}) collective-permute-start(bf16[40,3072]{1,0:T(8,128)(2,1)S(1)} %add_convert_fusion.8.left), channel_id=1, source_target_pairs={{0,24},{1,9},{2,26},{3,11},{4,28},{5,13},{6,30},{7,15},{8,16},{9,1... | collective-permute-start | bytes 737288 | tf_op jit(solution)/shard_map/ppermute | solution.py:231
  106.4 6.9 %collective-permute-start.17 = (bf16[40,3072]{1,0:T(8,128)(2,1)S(1)}, bf16[40,3072]{1,0:T(8,128)(2,1)S(1)}, u32[]{:S(2)}, u32[]{:S(2)}) collective-permute-start(bf16[40,3072]{1,0:T(8,128)(2,1)S(1)} %back.1), channel_id=1, source_target_pairs={{0,6},{1,3},{2,4},{3,1},{4,2},{5,7},{6,0},{7,5},{8,14},{9,11},{10,... | collective-permute-start | bytes 737288 | tf_op jit(solution)/shard_map/ppermute | solution.py:231
  108.3 9.0 %collective-permute-start.19 = (bf16[384,384]{1,0:T(8,128)(2,1)S(1)}, bf16[384,384]{1,0:T(8,128)(2,1)S(1)}, u32[]{:S(2)}, u32[]{:S(2)}) collective-permute-start(bf16[384,384]{1,0:T(8,128)(2,1)S(1)} %add_convert_fusion.7), channel_id=1, source_target_pairs={{0,32},{1,225},{2,34},{3,227},{4,36},{5,229},{6,38},{7,231},{8,40}... | collective-permute-start | bytes 884744 | tf_op jit(solution)/shard_map/ppermute | solution.py:231
  113.4 10.8 %collective-permute-start.18 = (bf16[80,3072]{1,0:T(8,128)(2,1)S(1)}, bf16[80,3072]{1,0:T(8,128)(2,1)S(1)}, u32[]{:S(2)}, u32[]{:S(2)}) collective-permute-start(bf16[80,3072]{1,0:T(8,128)(2,1)S(1)} %pad_maximum_fusion.2), channel_id=1, source_target_pairs={{0,2},{1,7},{2,0},{3,5},{4,6},{5,3},{6,4},{7,1},{8,10},{9,15},{10,... | collective-permute-start | bytes 1474568 | tf_op jit(solution)/shard_map/ppermute | solution.py:231
  117.5 7.0 %collective-permute-start.20 = (bf16[192,384]{1,0:T(8,128)(2,1)S(1)}, bf16[192,384]{1,0:T(8,128)(2,1)S(1)}, u32[]{:S(2)}, u32[]{:S(2)}) collective-permute-start(bf16[192,384]{1,0:T(8,128)(2,1)S(1)} %broadcast_select_fusion.6), channel_id=1, source_target_pairs={{0,256},{1,257},{2,258},{3,259},{4,260},{5,261},{6,262},{7,263},{8... | collective-permute-start | bytes 442376 | tf_op jit(solution)/shard_map/ppermute | solution.py:231
  124.5 9.3 %collective-permute-start.21 = (bf16[160,3072]{1,0:T(8,128)(2,1)S(1)}, bf16[160,3072]{1,0:T(8,128)(2,1)S(1)}, u32[]{:S(2)}, u32[]{:S(2)}) collective-permute-start(bf16[160,3072]{1,0:T(8,128)(2,1)S(1)} %pad_maximum_fusion.1), channel_id=1, source_target_pairs={{0,1},{1,0},{2,3},{3,2},{4,5},{5,4},{6,7},{7,6},{8,9},{9,8},{10,11... | collective-permute-start | bytes 2949128 | tf_op jit(solution)/shard_map/ppermute | solution.py:231

commit v6 on v5

--- a/solution.py
+++ b/solution.py
@@ -296,6 +296,10 @@
         )
     )
 
+    later = [pair for pair in pairs_of(by_y_lo) if pair[0] % CORE == 1]
+    got_gain = lax.ppermute(q_gain, AXES, later)
+    w_qkv, got_gain = lax.optimization_barrier((w_qkv, got_gain))
+    q_gain = jnp.where(first_core, q_gain, got_gain)
     other = swap(w_qkv, by_y_lo)
     blocks = along_z(w_qkv) + along_z(other)
     normed = run_norm(inputs, ln_gain.reshape(1, -1))

time: 138 us -> 137 us (level)
  the two profiles are of different devices: /device:TPU:1 before, /device:TPU:41 now
where the time goes in v6:
time: 137 us; the launch traced here: 136 us
  starting transfers between devices  82.5 us (60%)
  waiting for transfers between devices  35.6 us (26%)
  Pallas kernels  8.54 us (6%)
  other arithmetic  4.54 us (3%)
  local copies, waits for them, and re-layouts  3.47 us (3%)
    ppermute x22, starting transfers between devices, swap(): return lax.ppermute(values, AXES, pairs_of(partner))  79.5 us
    ppermute x22, waiting for transfers between devices, swap(): return lax.ppermute(values, AXES, pairs_of(partner))  34.4 us
    pallas_call x1, Pallas kernels, run_head(): pl.pallas_call(head_kernel, out_shape=(like(tokens, width), like(tokens /...  4.59 us
    ppermute x1, starting transfers between devices, per_device(): got_gain = lax.ppermute(q_gain, AXES, later)  2.98 us
  transfers between devices with their start and end apart: 23, of which 16 were waited for; matrix products, arithmetic and copies ran while one was open for 3% of the time, Pallas kernels for 3%

profile of v6, /device:TPU:41, one launch (start us, length us, event | category | flops | bytes accessed | tf_op | source)
XLA Modules:
  0.0 135.8 jit_solution(8292339075157246158)
XLA Ops:
  0.6 3.0 %collective-permute-start = (f32[128]{0:T(128)}, f32[128]{0:T(128)S(1)}, u32[]{:S(2)}, u32[]{:S(2)}) collective-permute-start(f32[128]{0:T(128)} %param.9), channel_id=1, source_target_pairs={{1,257},{3,259},{5,261},{7,263},{9,265},{11,267},{13,269},{15,271}... | collective-permute-start | bytes 1544 | tf_op jit(solution)/shard_map/ppermute | solution.py:300
  3.8 0.1 stack.27.places
  3.8 1.2 collective-permute-done
  5.0 3.0 %collective-permute-start.5 = (bf16[192,384]{1,0:T(8,128)(2,1)}, bf16[192,384]{1,0:T(8,128)(2,1)S(1)}, u32[]{:S(2)}, u32[]{:S(2)}) collective-permute-start(bf16[192,384]{1,0:T(8,128)(2,1)} %refs_0_), channel_id=1, source_target_pairs={{0,256},{1,257},{2,258},{3,259},{4,260},{5,261},{6,262},{7,263},{8... | collective-permute-start | bytes 442376 | tf_op jit(solution)/shard_map/ppermute | solution.py:231
  8.0 10.7 %collective-permute-start.1 = (bf16[192,384]{1,0:T(8,128)(2,1)}, bf16[192,384]{1,0:T(8,128)(2,1)S(1)}, u32[]{:S(2)}, u32[]{:S(2)}) collective-permute-start(bf16[192,384]{1,0:T(8,128)(2,1)} %refs_0_), channel_id=1, source_target_pairs={{0,32},{1,225},{2,34},{3,227},{4,36},{5,229},{6,38},{7,231},{8,40}... | collective-permute-start | bytes 442376 | tf_op jit(solution)/shard_map/ppermute | solution.py:231
  18.7 3.4 %collective-permute-start.6 = (bf16[192,384]{1,0:T(8,128)(2,1)S(1)}, bf16[192,384]{1,0:T(8,128)(2,1)S(1)}, u32[]{:S(2)}, u32[]{:S(2)}) collective-permute-start(bf16[192,384]{1,0:T(8,128)(2,1)S(1)} %collective-permute-done.5.refs_5_), channel_id=1, source_target_pairs={{0,32},{1,225},{2,34},{3,227},{4,36},{5,229},{6,38},{7,231},{8,40}... | collective-permute-start | bytes 442376 | tf_op jit(solution)/shard_map/ppermute | solution.py:231
  22.1 0.9 pad_maximum_fusion.3
  23.1 1.9 %collective-permute-start.2 = (bf16[384,384]{1,0:T(8,128)(2,1)S(1)}, bf16[384,384]{1,0:T(8,128)(2,1)S(1)}, u32[]{:S(2)}, u32[]{:S(2)}) collective-permute-start(bf16[384,384]{1,0:T(8,128)(2,1)S(1)} %pad_maximum_fusion.3), channel_id=1, source_target_pairs={{0,224},{1,33},{2,226},{3,35},{4,228},{5,37},{6,230},{7,39},{8,232... | collective-permute-start | bytes 884744 | tf_op jit(solution)/shard_map/ppermute | solution.py:231
  25.0 1.5 %collective-permute-done.6.refs_6_ = bf16[192,384]{1,0:T(8,128)(2,1)S(1)} collective-permute-done((bf16[192,384]{1,0:T(8,128)(2,1)S(1)}, bf16[192,384]{1,0:T(8,128)(2,1)S(1)}, u32[]{:S(2)}, u32[]{:S(2)}) %collective-permute-start.6) | collective-permute-done | bytes 147488 | tf_op jit(solution)/shard_map/ppermute | solution.py:231
  26.5 1.9 %collective-permute-start.7 = (bf16[384,384]{1,0:T(8,128)(2,1)S(1)}, bf16[384,384]{1,0:T(8,128)(2,1)S(1)}, u32[]{:S(2)}, u32[]{:S(2)}) collective-permute-start(bf16[384,384]{1,0:T(8,128)(2,1)S(1)} %pad_maximum_fusion.4), channel_id=1, source_target_pairs={{0,224},{1,33},{2,226},{3,35},{4,228},{5,37},{6,230},{7,39},{8,232... | collective-permute-start | bytes 884744 | tf_op jit(solution)/shard_map/ppermute | solution.py:231
  28.4 2.1 %collective-permute-done.2.refs_2_ = bf16[384,384]{1,0:T(8,128)(2,1)S(1)} collective-permute-done((bf16[384,384]{1,0:T(8,128)(2,1)S(1)}, bf16[384,384]{1,0:T(8,128)(2,1)S(1)}, u32[]{:S(2)}, u32[]{:S(2)}) %collective-permute-start.2) | collective-permute-done | bytes 294944 | tf_op jit(solution)/shard_map/ppermute | solution.py:231
  30.5 4.2 %collective-permute-start.3 = (bf16[384,384]{1,0:T(8,128)(2,1)S(1)}, bf16[384,384]{1,0:T(8,128)(2,1)S(1)}, u32[]{:S(2)}, u32[]{:S(2)}) collective-permute-start(bf16[384,384]{1,0:T(8,128)(2,1)S(1)} %collective-permute-done.2.refs_2_), channel_id=1, source_target_pairs={{0,32},{1,225},{2,34},{3,227},{4,36},{5,229},{6,38},{7,231},{8,40}... | collective-permute-start | bytes 884744 | tf_op jit(solution)/shard_map/ppermute | solution.py:231
  34.7 2.8 %collective-permute-start.8 = (bf16[384,384]{1,0:T(8,128)(2,1)S(1)}, bf16[384,384]{1,0:T(8,128)(2,1)S(1)}, u32[]{:S(2)}, u32[]{:S(2)}) collective-permute-start(bf16[384,384]{1,0:T(8,128)(2,1)S(1)} %collective-permute-done.7.refs_7_), channel_id=1, source_target_pairs={{0,32},{1,225},{2,34},{3,227},{4,36},{5,229},{6,38},{7,231},{8,40}... | collective-permute-start | bytes 884744 | tf_op jit(solution)/shard_map/ppermute | solution.py:231
  37.6 1.6 %collective-permute-done.3.refs_3_ = bf16[384,384]{1,0:T(8,128)(2,1)S(1)} collective-permute-done((bf16[384,384]{1,0:T(8,128)(2,1)S(1)}, bf16[384,384]{1,0:T(8,128)(2,1)S(1)}, u32[]{:S(2)}, u32[]{:S(2)}) %collective-permute-start.3) | collective-permute-done | bytes 294944 | tf_op jit(solution)/shard_map/ppermute | solution.py:231
  39.2 1.9 %collective-permute-start.4 = (bf16[384,384]{1,0:T(8,128)(2,1)S(1)}, bf16[384,384]{1,0:T(8,128)(2,1)S(1)}, u32[]{:S(2)}, u32[]{:S(2)}) collective-permute-start(bf16[384,384]{1,0:T(8,128)(2,1)S(1)} %collective-permute-done.3.refs_3_), channel_id=1, source_target_pairs={{0,224},{1,33},{2,226},{3,35},{4,228},{5,37},{6,230},{7,39},{8,232... | collective-permute-start | bytes 884744 | tf_op jit(solution)/shard_map/ppermute | solution.py:231
  41.1 2.3 %collective-permute-done.8.refs_8_ = bf16[384,384]{1,0:T(8,128)(2,1)S(1)} collective-permute-done((bf16[384,384]{1,0:T(8,128)(2,1)S(1)}, bf16[384,384]{1,0:T(8,128)(2,1)S(1)}, u32[]{:S(2)}, u32[]{:S(2)}) %collective-permute-start.8) | collective-permute-done | bytes 294944 | tf_op jit(solution)/shard_map/ppermute | solution.py:231
  43.4 1.9 %collective-permute-start.9 = (bf16[384,384]{1,0:T(8,128)(2,1)S(1)}, bf16[384,384]{1,0:T(8,128)(2,1)S(1)}, u32[]{:S(2)}, u32[]{:S(2)}) collective-permute-start(bf16[384,384]{1,0:T(8,128)(2,1)S(1)} %collective-permute-done.8.refs_8_), channel_id=1, source_target_pairs={{0,224},{1,33},{2,226},{3,35},{4,228},{5,37},{6,230},{7,39},{8,232... | collective-permute-start | bytes 884744 | tf_op jit(solution)/shard_map/ppermute | solution.py:231
  45.3 0.0 copy-start
  45.3 1.5 %copy-done = bf16[320,3072]{1,0:T(8,128)(2,1)S(1)} copy-done((bf16[320,3072]{1,0:T(8,128)(2,1)S(1)}, bf16[320,3072]{1,0:T(8,128)(2,1)}, u32[]{:S(2)}) %copy-start) | copy-done | bytes 1966104
  46.9 0.7 copy-done.3
  47.6 1.3 norm.1.normed
  48.9 2.2 %collective-permute-done.9.refs_9_ = bf16[384,384]{1,0:T(8,128)(2,1)S(1)} collective-permute-done((bf16[384,384]{1,0:T(8,128)(2,1)S(1)}, bf16[384,384]{1,0:T(8,128)(2,1)S(1)}, u32[]{:S(2)}, u32[]{:S(2)}) %collective-permute-start.9) | collective-permute-done | bytes 294944 | tf_op jit(solution)/shard_map/ppermute | solution.py:231
  51.2 4.6 %head.1 = (bf16[320,384]{1,0:T(8,128)(2,1)S(1)}, bf16[80,3072]{1,0:T(8,128)(2,1)S(1)}, bf16[80,3072]{1,0:T(8,128)(2,1)S(1)}, bf16[160,3072]{1,0:T(8,128)(2,1)S(1)}) custom-call(s32[6]{0:T(128)S(1)} %stack.27.places, bf16[320,3072]{1,0:T(8,128)(2,1)S(1)} %norm.1.normed, bf16[320,128]{1,0:T(8,128)(2,1)S(1)} %copy-done.2, f32[1,128]{1,0:T(1,128)S(1)} %fusion.q_gain, ...), custom_call_target="tpu_custom_call" | custom-call | flops 1132462080 | bytes 8388608 | tf_op jit(solution)/shard_map/head/pallas_call | solution.py:114
  55.7 3.7 %collective-permute-start.10 = (bf16[160,3072]{1,0:T(8,128)(2,1)S(1)}, bf16[160,3072]{1,0:T(8,128)(2,1)S(1)}, u32[]{:S(2)}, u32[]{:S(2)}) collective-permute-start(bf16[160,3072]{1,0:T(8,128)(2,1)S(1)} %get-tuple-element.33), channel_id=1, source_target_pairs={{0,1},{1,0},{2,3},{3,2},{4,5},{5,4},{6,7},{7,6},{8,9},{9,8},{10,11... | collective-permute-start | bytes 2949128 | tf_op jit(solution)/shard_map/ppermute | solution.py:231
  59.4 2.2 %terms.1 = bf16[3072,384]{1,0:T(8,128)(2,1)S(1)} custom-call(s32[6]{0:T(128)S(1)} %stack.27.places, bf16[320,3072]{1,0:T(8,128)(2,1)S(1)} %norm.1.normed, bf16[320,384]{1,0:T(8,128)(2,1)S(1)} %get-tuple-element.35.grads), custom_call_target="tpu_custom_call" | custom-call | flops 754974720 | bytes 5242880 | tf_op jit(solution)/shard_map/terms/pallas_call | solution.py:173
  61.7 0.1 add_convert_fusion.4
  61.8 4.4 %collective-permute-start.11 = (bf16[80,3072]{1,0:T(8,128)(2,1)S(1)}, bf16[80,3072]{1,0:T(8,128)(2,1)S(1)}, u32[]{:S(2)}, u32[]{:S(2)}) collective-permute-start(bf16[80,3072]{1,0:T(8,128)(2,1)S(1)} %add_convert_fusion.4), channel_id=1, source_target_pairs={{0,2},{1,7},{2,0},{3,5},{4,6},{5,3},{6,4},{7,1},{8,10},{9,15},{10,... | collective-permute-start | bytes 1474568 | tf_op jit(solution)/shard_map/ppermute | solution.py:231
  66.2 0.1 split.21
  66.2 1.9 %collective-permute-start.13 = (bf16[768,384]{1,0:T(8,128)(2,1)S(1)}, bf16[768,384]{1,0:T(8,128)(2,1)S(1)}, u32[]{:S(2)}, u32[]{:S(2)}) collective-permute-start(bf16[768,384]{1,0:T(8,128)(2,1)S(1)} %split.21), channel_id=1, source_target_pairs={{0,224},{1,33},{2,226},{3,35},{4,228},{5,37},{6,230},{7,39},{8,232... | collective-permute-start | bytes 1769480 | tf_op jit(solution)/shard_map/ppermute | solution.py:231
  68.2 4.7 %collective-permute-done.11 = bf16[80,3072]{1,0:T(8,128)(2,1)S(1)} collective-permute-done((bf16[80,3072]{1,0:T(8,128)(2,1)S(1)}, bf16[80,3072]{1,0:T(8,128)(2,1)S(1)}, u32[]{:S(2)}, u32[]{:S(2)}) %collective-permute-start.11) | collective-permute-done | bytes 491552 | tf_op jit(solution)/shard_map/ppermute | solution.py:231
  72.9 0.2 add_convert_fusion.2
  73.1 1.9 %collective-permute-start.12 = (bf16[40,3072]{1,0:T(8,128)(2,1)S(1)}, bf16[40,3072]{1,0:T(8,128)(2,1)S(1)}, u32[]{:S(2)}, u32[]{:S(2)}) collective-permute-start(bf16[40,3072]{1,0:T(8,128)(2,1)S(1)} %slice.34), channel_id=1, source_target_pairs={{0,6},{1,3},{2,4},{3,1},{4,2},{5,7},{6,0},{7,5},{8,14},{9,11},{10,... | collective-permute-start | bytes 737288 | tf_op jit(solution)/shard_map/ppermute | solution.py:231
  75.0 2.2 %collective-permute-done.13 = bf16[768,384]{1,0:T(8,128)(2,1)S(1)} collective-permute-done((bf16[768,384]{1,0:T(8,128)(2,1)S(1)}, bf16[768,384]{1,0:T(8,128)(2,1)S(1)}, u32[]{:S(2)}, u32[]{:S(2)}) %collective-permute-start.13) | collective-permute-done | bytes 589856 | tf_op jit(solution)/shard_map/ppermute | solution.py:231
  77.2 0.1 add_convert_fusion.1
  77.3 0.0 copy-start.4
  77.3 2.8 %collective-permute-start.15 = (bf16[768,384]{1,0:T(8,128)(2,1)S(1)}, bf16[768,384]{1,0:T(8,128)(2,1)S(1)}, u32[]{:S(2)}, u32[]{:S(2)}) collective-permute-start(bf16[768,384]{1,0:T(8,128)(2,1)S(1)} %add_convert_fusion.1), channel_id=1, source_target_pairs={{0,32},{1,225},{2,34},{3,227},{4,36},{5,229},{6,38},{7,231},{8,40}... | collective-permute-start | bytes 1769480 | tf_op jit(solution)/shard_map/ppermute | solution.py:231
  80.2 0.2 collective-permute-done.12
  80.3 0.1 add_convert_fusion.9
  80.4 2.4 %collective-permute-start.14 = (bf16[40,3072]{1,0:T(8,128)(2,1)S(1)}, bf16[40,3072]{1,0:T(8,128)(2,1)S(1)}, u32[]{:S(2)}, u32[]{:S(2)}) collective-permute-start(bf16[40,3072]{1,0:T(8,128)(2,1)S(1)} %add_convert_fusion.9), channel_id=1, source_target_pairs={{0,8},{1,25},{2,10},{3,27},{4,12},{5,29},{6,14},{7,31},{8,0},{9,17... | collective-permute-start | bytes 737288 | tf_op jit(solution)/shard_map/ppermute | solution.py:231
  82.8 6.5 %collective-permute-done.15 = bf16[768,384]{1,0:T(8,128)(2,1)S(1)} collective-permute-done((bf16[768,384]{1,0:T(8,128)(2,1)S(1)}, bf16[768,384]{1,0:T(8,128)(2,1)S(1)}, u32[]{:S(2)}, u32[]{:S(2)}) %collective-permute-start.15) | collective-permute-done | bytes 589856 | tf_op jit(solution)/shard_map/ppermute | solution.py:231
  89.3 0.2 add_convert_fusion
  89.5 1.9 %collective-permute-start.17 = (bf16[768,384]{1,0:T(8,128)(2,1)S(1)}, bf16[768,384]{1,0:T(8,128)(2,1)S(1)}, u32[]{:S(2)}, u32[]{:S(2)}) collective-permute-start(bf16[768,384]{1,0:T(8,128)(2,1)S(1)} %add_convert_fusion), channel_id=1, source_target_pairs={{0,224},{1,33},{2,226},{3,35},{4,228},{5,37},{6,230},{7,39},{8,232... | collective-permute-start | bytes 1769480 | tf_op jit(solution)/shard_map/ppermute | solution.py:231
  91.4 0.2 collective-permute-done.14
  91.6 0.1 add_convert_fusion.8.left
  91.7 2.2 %collective-permute-start.16 = (bf16[40,3072]{1,0:T(8,128)(2,1)S(1)}, bf16[40,3072]{1,0:T(8,128)(2,1)S(1)}, u32[]{:S(2)}, u32[]{:S(2)}) collective-permute-start(bf16[40,3072]{1,0:T(8,128)(2,1)S(1)} %add_convert_fusion.8.left), channel_id=1, source_target_pairs={{0,24},{1,9},{2,26},{3,11},{4,28},{5,13},{6,30},{7,15},{8,16},{9,1... | collective-permute-start | bytes 737288 | tf_op jit(solution)/shard_map/ppermute | solution.py:231
  93.9 1.0 constant_dynamic-slice_fusion.inputs
  95.0 4.9 %collective-permute-done.16.right = bf16[40,3072]{1,0:T(8,128)(2,1)S(1)} collective-permute-done((bf16[40,3072]{1,0:T(8,128)(2,1)S(1)}, bf16[40,3072]{1,0:T(8,128)(2,1)S(1)}, u32[]{:S(2)}, u32[]{:S(2)}) %collective-permute-start.16) | collective-permute-done | bytes 245792 | tf_op jit(solution)/shard_map/ppermute | solution.py:231
  99.9 0.4 back.1
  100.3 0.1 collective-permute-done.17
  100.4 0.1 add_convert_fusion.7
  100.5 1.9 %collective-permute-start.18 = (bf16[40,3072]{1,0:T(8,128)(2,1)S(1)}, bf16[40,3072]{1,0:T(8,128)(2,1)S(1)}, u32[]{:S(2)}, u32[]{:S(2)}) collective-permute-start(bf16[40,3072]{1,0:T(8,128)(2,1)S(1)} %back.1), channel_id=1, source_target_pairs={{0,6},{1,3},{2,4},{3,1},{4,2},{5,7},{6,0},{7,5},{8,14},{9,11},{10,... | collective-permute-start | bytes 737288 | tf_op jit(solution)/shard_map/ppermute | solution.py:231
  102.4 3.9 %collective-permute-start.20 = (bf16[384,384]{1,0:T(8,128)(2,1)S(1)}, bf16[384,384]{1,0:T(8,128)(2,1)S(1)}, u32[]{:S(2)}, u32[]{:S(2)}) collective-permute-start(bf16[384,384]{1,0:T(8,128)(2,1)S(1)} %add_convert_fusion.7), channel_id=1, source_target_pairs={{0,32},{1,225},{2,34},{3,227},{4,36},{5,229},{6,38},{7,231},{8,40}... | collective-permute-start | bytes 884744 | tf_op jit(solution)/shard_map/ppermute | solution.py:231
  106.3 1.1 collective-permute-done.18
  107.5 4.5 %collective-permute-start.19 = (bf16[80,3072]{1,0:T(8,128)(2,1)S(1)}, bf16[80,3072]{1,0:T(8,128)(2,1)S(1)}, u32[]{:S(2)}, u32[]{:S(2)}) collective-permute-start(bf16[80,3072]{1,0:T(8,128)(2,1)S(1)} %pad_maximum_fusion.2), channel_id=1, source_target_pairs={{0,2},{1,7},{2,0},{3,5},{4,6},{5,3},{6,4},{7,1},{8,10},{9,15},{10,... | collective-permute-start | bytes 1474568 | tf_op jit(solution)/shard_map/ppermute | solution.py:231
  112.0 0.1 add_convert_fusion.5
  112.2 5.3 %collective-permute-start.21 = (bf16[192,384]{1,0:T(8,128)(2,1)S(1)}, bf16[192,384]{1,0:T(8,128)(2,1)S(1)}, u32[]{:S(2)}, u32[]{:S(2)}) collective-permute-start(bf16[192,384]{1,0:T(8,128)(2,1)S(1)} %broadcast_select_fusion.6), channel_id=1, source_target_pairs={{0,256},{1,257},{2,258},{3,259},{4,260},{5,261},{6,262},{7,263},{8... | collective-permute-start | bytes 442376 | tf_op jit(solution)/shard_map/ppermute | solution.py:231
  117.4 3.5 %collective-permute-done.19 = bf16[80,3072]{1,0:T(8,128)(2,1)S(1)} collective-permute-done((bf16[80,3072]{1,0:T(8,128)(2,1)S(1)}, bf16[80,3072]{1,0:T(8,128)(2,1)S(1)}, u32[]{:S(2)}, u32[]{:S(2)}) %collective-permute-start.19) | collective-permute-done | bytes 491552 | tf_op jit(solution)/shard_map/ppermute | solution.py:231
  120.9 0.2 broadcast_select_fusion.3
  121.1 0.1 pad_maximum_fusion.1
  121.2 11.0 %collective-permute-start.22 = (bf16[160,3072]{1,0:T(8,128)(2,1)S(1)}, bf16[160,3072]{1,0:T(8,128)(2,1)S(1)}, u32[]{:S(2)}, u32[]{:S(2)}) collective-permute-start(bf16[160,3072]{1,0:T(8,128)(2,1)S(1)} %pad_maximum_fusion.1), channel_id=1, source_target_pairs={{0,1},{1,0},{2,3},{3,2},{4,5},{5,4},{6,7},{7,6},{8,9},{9,8},{10,11... | collective-permute-start | bytes 2949128 | tf_op jit(solution)/shard_map/ppermute | solution.py:231
  132.1 0.8 convert_add_fusion
  132.9 1.4 %collective-permute-done.22 = bf16[160,3072]{1,0:T(8,128)(2,1)S(1)} collective-permute-done((bf16[160,3072]{1,0:T(8,128)(2,1)S(1)}, bf16[160,3072]{1,0:T(8,128)(2,1)S(1)}, u32[]{:S(2)}, u32[]{:S(2)}) %collective-permute-start.22) | collective-permute-done | bytes 983072 | tf_op jit(solution)/shard_map/ppermute | solution.py:231
  134.3 0.1 broadcast_select_fusion.1
  134.4 1.4 %pad_maximum_fusion = bf16[320,3072]{1,0:T(8,128)(2,1)} fusion(bf16[160,3072]{1,0:T(8,128)(2,1)S(1)} %get-tuple-element.49, bf16[160,3072]{1,0:T(8,128)(2,1)S(1)} %get-tuple-element.48), kind=kLoop, calls=%fused_computation | loop fusion | flops 3932160 | bytes 3932160 | tf_op jit(solution)/shard_map/concatenate | solution.py:271
  (23 shorter events, 0.2 us)
Async XLA Ops:
  0.6 4.4 %collective-permute-start = (f32[128]{0:T(128)}, f32[128]{0:T(128)S(1)}, u32[]{:S(2)}, u32[]{:S(2)}) collective-permute-start(f32[128]{0:T(128)} %param.9), channel_id=1, source_target_pairs={{1,257},{3,259},{5,261},{7,263},{9,265},{11,267},{13,269},{15,271}... | collective-permute-start | bytes 1544 | tf_op jit(solution)/shard_map/ppermute | solution.py:300
  5.0 13.7 %collective-permute-start.5 = (bf16[192,384]{1,0:T(8,128)(2,1)}, bf16[192,384]{1,0:T(8,128)(2,1)S(1)}, u32[]{:S(2)}, u32[]{:S(2)}) collective-permute-start(bf16[192,384]{1,0:T(8,128)(2,1)} %refs_0_), channel_id=1, source_target_pairs={{0,256},{1,257},{2,258},{3,259},{4,260},{5,261},{6,262},{7,263},{8... | collective-permute-start | bytes 442376 | tf_op jit(solution)/shard_map/ppermute | solution.py:231
  8.0 14.1 %collective-permute-start.1 = (bf16[192,384]{1,0:T(8,128)(2,1)}, bf16[192,384]{1,0:T(8,128)(2,1)S(1)}, u32[]{:S(2)}, u32[]{:S(2)}) collective-permute-start(bf16[192,384]{1,0:T(8,128)(2,1)} %refs_0_), channel_id=1, source_target_pairs={{0,32},{1,225},{2,34},{3,227},{4,36},{5,229},{6,38},{7,231},{8,40}... | collective-permute-start | bytes 442376 | tf_op jit(solution)/shard_map/ppermute | solution.py:231
  18.7 7.7 %collective-permute-start.6 = (bf16[192,384]{1,0:T(8,128)(2,1)S(1)}, bf16[192,384]{1,0:T(8,128)(2,1)S(1)}, u32[]{:S(2)}, u32[]{:S(2)}) collective-permute-start(bf16[192,384]{1,0:T(8,128)(2,1)S(1)} %collective-permute-done.5.refs_5_), channel_id=1, source_target_pairs={{0,32},{1,225},{2,34},{3,227},{4,36},{5,229},{6,38},{7,231},{8,40}... | collective-permute-start | bytes 442376 | tf_op jit(solution)/shard_map/ppermute | solution.py:231
  23.1 7.5 %collective-permute-start.2 = (bf16[384,384]{1,0:T(8,128)(2,1)S(1)}, bf16[384,384]{1,0:T(8,128)(2,1)S(1)}, u32[]{:S(2)}, u32[]{:S(2)}) collective-permute-start(bf16[384,384]{1,0:T(8,128)(2,1)S(1)} %pad_maximum_fusion.3), channel_id=1, source_target_pairs={{0,224},{1,33},{2,226},{3,35},{4,228},{5,37},{6,230},{7,39},{8,232... | collective-permute-start | bytes 884744 | tf_op jit(solution)/shard_map/ppermute | solution.py:231
  26.5 8.2 %collective-permute-start.7 = (bf16[384,384]{1,0:T(8,128)(2,1)S(1)}, bf16[384,384]{1,0:T(8,128)(2,1)S(1)}, u32[]{:S(2)}, u32[]{:S(2)}) collective-permute-start(bf16[384,384]{1,0:T(8,128)(2,1)S(1)} %pad_maximum_fusion.4), channel_id=1, source_target_pairs={{0,224},{1,33},{2,226},{3,35},{4,228},{5,37},{6,230},{7,39},{8,232... | collective-permute-start | bytes 884744 | tf_op jit(solution)/shard_map/ppermute | solution.py:231
  30.5 8.7 %collective-permute-start.3 = (bf16[384,384]{1,0:T(8,128)(2,1)S(1)}, bf16[384,384]{1,0:T(8,128)(2,1)S(1)}, u32[]{:S(2)}, u32[]{:S(2)}) collective-permute-start(bf16[384,384]{1,0:T(8,128)(2,1)S(1)} %collective-permute-done.2.refs_2_), channel_id=1, source_target_pairs={{0,32},{1,225},{2,34},{3,227},{4,36},{5,229},{6,38},{7,231},{8,40}... | collective-permute-start | bytes 884744 | tf_op jit(solution)/shard_map/ppermute | solution.py:231
  34.7 8.7 %collective-permute-start.8 = (bf16[384,384]{1,0:T(8,128)(2,1)S(1)}, bf16[384,384]{1,0:T(8,128)(2,1)S(1)}, u32[]{:S(2)}, u32[]{:S(2)}) collective-permute-start(bf16[384,384]{1,0:T(8,128)(2,1)S(1)} %collective-permute-done.7.refs_7_), channel_id=1, source_target_pairs={{0,32},{1,225},{2,34},{3,227},{4,36},{5,229},{6,38},{7,231},{8,40}... | collective-permute-start | bytes 884744 | tf_op jit(solution)/shard_map/ppermute | solution.py:231
  39.2 9.7 %collective-permute-start.4 = (bf16[384,384]{1,0:T(8,128)(2,1)S(1)}, bf16[384,384]{1,0:T(8,128)(2,1)S(1)}, u32[]{:S(2)}, u32[]{:S(2)}) collective-permute-start(bf16[384,384]{1,0:T(8,128)(2,1)S(1)} %collective-permute-done.3.refs_3_), channel_id=1, source_target_pairs={{0,224},{1,33},{2,226},{3,35},{4,228},{5,37},{6,230},{7,39},{8,232... | collective-permute-start | bytes 884744 | tf_op jit(solution)/shard_map/ppermute | solution.py:231
  43.4 7.8 %collective-permute-start.9 = (bf16[384,384]{1,0:T(8,128)(2,1)S(1)}, bf16[384,384]{1,0:T(8,128)(2,1)S(1)}, u32[]{:S(2)}, u32[]{:S(2)}) collective-permute-start(bf16[384,384]{1,0:T(8,128)(2,1)S(1)} %collective-permute-done.8.refs_8_), channel_id=1, source_target_pairs={{0,224},{1,33},{2,226},{3,35},{4,228},{5,37},{6,230},{7,39},{8,232... | collective-permute-start | bytes 884744 | tf_op jit(solution)/shard_map/ppermute | solution.py:231
  45.3 1.5 %copy-start = (bf16[320,3072]{1,0:T(8,128)(2,1)S(1)}, bf16[320,3072]{1,0:T(8,128)(2,1)}, u32[]{:S(2)}) copy-start(bf16[320,3072]{1,0:T(8,128)(2,1)} %inputs.1) | copy-start | bytes 5898244
  46.9 0.7 copy-start.3
  47.6 1.3 copy-start.6
  47.6 3.6 %copy-start.1 = (bf16[192,384]{1,0:T(8,128)(2,1)S(1)}, bf16[192,384]{1,0:T(8,128)(2,1)}, u32[]{:S(2)}) copy-start(bf16[192,384]{1,0:T(8,128)(2,1)} %refs_0_) | copy-start | bytes 442372
  47.6 3.6 %copy-start.2 = (bf16[320,128]{1,0:T(8,128)(2,1)S(1)}, bf16[320,128]{1,0:T(8,128)(2,1)}, u32[]{:S(2)}) copy-start(bf16[320,128]{1,0:T(8,128)(2,1)} %cot.1) | copy-start | bytes 245764
  47.6 3.6 %copy-start.5 = (f32[128]{0:T(128)S(1)}, f32[128]{0:T(128)}, u32[]{:S(2)}) copy-start(f32[128]{0:T(128)} %param.10) | copy-start | bytes 1540
  55.7 5.9 %collective-permute-start.10 = (bf16[160,3072]{1,0:T(8,128)(2,1)S(1)}, bf16[160,3072]{1,0:T(8,128)(2,1)S(1)}, u32[]{:S(2)}, u32[]{:S(2)}) collective-permute-start(bf16[160,3072]{1,0:T(8,128)(2,1)S(1)} %get-tuple-element.33), channel_id=1, source_target_pairs={{0,1},{1,0},{2,3},{3,2},{4,5},{5,4},{6,7},{7,6},{8,9},{9,8},{10,11... | collective-permute-start | bytes 2949128 | tf_op jit(solution)/shard_map/ppermute | solution.py:231
  61.8 11.1 %collective-permute-start.11 = (bf16[80,3072]{1,0:T(8,128)(2,1)S(1)}, bf16[80,3072]{1,0:T(8,128)(2,1)S(1)}, u32[]{:S(2)}, u32[]{:S(2)}) collective-permute-start(bf16[80,3072]{1,0:T(8,128)(2,1)S(1)} %add_convert_fusion.4), channel_id=1, source_target_pairs={{0,2},{1,7},{2,0},{3,5},{4,6},{5,3},{6,4},{7,1},{8,10},{9,15},{10,... | collective-permute-start | bytes 1474568 | tf_op jit(solution)/shard_map/ppermute | solution.py:231
  66.2 10.9 %collective-permute-start.13 = (bf16[768,384]{1,0:T(8,128)(2,1)S(1)}, bf16[768,384]{1,0:T(8,128)(2,1)S(1)}, u32[]{:S(2)}, u32[]{:S(2)}) collective-permute-start(bf16[768,384]{1,0:T(8,128)(2,1)S(1)} %split.21), channel_id=1, source_target_pairs={{0,224},{1,33},{2,226},{3,35},{4,228},{5,37},{6,230},{7,39},{8,232... | collective-permute-start | bytes 1769480 | tf_op jit(solution)/shard_map/ppermute | solution.py:231
  73.1 7.2 %collective-permute-start.12 = (bf16[40,3072]{1,0:T(8,128)(2,1)S(1)}, bf16[40,3072]{1,0:T(8,128)(2,1)S(1)}, u32[]{:S(2)}, u32[]{:S(2)}) collective-permute-start(bf16[40,3072]{1,0:T(8,128)(2,1)S(1)} %slice.34), channel_id=1, source_target_pairs={{0,6},{1,3},{2,4},{3,1},{4,2},{5,7},{6,0},{7,5},{8,14},{9,11},{10,... | collective-permute-start | bytes 737288 | tf_op jit(solution)/shard_map/ppermute | solution.py:231
  77.3 22.6 %copy-start.4 = (f32[3072]{0:T(1024)S(1)}, f32[3072]{0:T(1024)}, u32[]{:S(2)}) copy-start(f32[3072]{0:T(1024)} %param.7) | copy-start | bytes 36868
  77.3 12.0 %collective-permute-start.15 = (bf16[768,384]{1,0:T(8,128)(2,1)S(1)}, bf16[768,384]{1,0:T(8,128)(2,1)S(1)}, u32[]{:S(2)}, u32[]{:S(2)}) collective-permute-start(bf16[768,384]{1,0:T(8,128)(2,1)S(1)} %add_convert_fusion.1), channel_id=1, source_target_pairs={{0,32},{1,225},{2,34},{3,227},{4,36},{5,229},{6,38},{7,231},{8,40}... | collective-permute-start | bytes 1769480 | tf_op jit(solution)/shard_map/ppermute | solution.py:231
  80.4 11.3 %collective-permute-start.14 = (bf16[40,3072]{1,0:T(8,128)(2,1)S(1)}, bf16[40,3072]{1,0:T(8,128)(2,1)S(1)}, u32[]{:S(2)}, u32[]{:S(2)}) collective-permute-start(bf16[40,3072]{1,0:T(8,128)(2,1)S(1)} %add_convert_fusion.9), channel_id=1, source_target_pairs={{0,8},{1,25},{2,10},{3,27},{4,12},{5,29},{6,14},{7,31},{8,0},{9,17... | collective-permute-start | bytes 737288 | tf_op jit(solution)/shard_map/ppermute | solution.py:231
  89.5 10.9 %collective-permute-start.17 = (bf16[768,384]{1,0:T(8,128)(2,1)S(1)}, bf16[768,384]{1,0:T(8,128)(2,1)S(1)}, u32[]{:S(2)}, u32[]{:S(2)}) collective-permute-start(bf16[768,384]{1,0:T(8,128)(2,1)S(1)} %add_convert_fusion), channel_id=1, source_target_pairs={{0,224},{1,33},{2,226},{3,35},{4,228},{5,37},{6,230},{7,39},{8,232... | collective-permute-start | bytes 1769480 | tf_op jit(solution)/shard_map/ppermute | solution.py:231
  91.7 8.2 %collective-permute-start.16 = (bf16[40,3072]{1,0:T(8,128)(2,1)S(1)}, bf16[40,3072]{1,0:T(8,128)(2,1)S(1)}, u32[]{:S(2)}, u32[]{:S(2)}) collective-permute-start(bf16[40,3072]{1,0:T(8,128)(2,1)S(1)} %add_convert_fusion.8.left), channel_id=1, source_target_pairs={{0,24},{1,9},{2,26},{3,11},{4,28},{5,13},{6,30},{7,15},{8,16},{9,1... | collective-permute-start | bytes 737288 | tf_op jit(solution)/shard_map/ppermute | solution.py:231
  100.5 6.9 %collective-permute-start.18 = (bf16[40,3072]{1,0:T(8,128)(2,1)S(1)}, bf16[40,3072]{1,0:T(8,128)(2,1)S(1)}, u32[]{:S(2)}, u32[]{:S(2)}) collective-permute-start(bf16[40,3072]{1,0:T(8,128)(2,1)S(1)} %back.1), channel_id=1, source_target_pairs={{0,6},{1,3},{2,4},{3,1},{4,2},{5,7},{6,0},{7,5},{8,14},{9,11},{10,... | collective-permute-start | bytes 737288 | tf_op jit(solution)/shard_map/ppermute | solution.py:231
  102.4 9.6 %collective-permute-start.20 = (bf16[384,384]{1,0:T(8,128)(2,1)S(1)}, bf16[384,384]{1,0:T(8,128)(2,1)S(1)}, u32[]{:S(2)}, u32[]{:S(2)}) collective-permute-start(bf16[384,384]{1,0:T(8,128)(2,1)S(1)} %add_convert_fusion.7), channel_id=1, source_target_pairs={{0,32},{1,225},{2,34},{3,227},{4,36},{5,229},{6,38},{7,231},{8,40}... | collective-permute-start | bytes 884744 | tf_op jit(solution)/shard_map/ppermute | solution.py:231
  107.5 13.4 %collective-permute-start.19 = (bf16[80,3072]{1,0:T(8,128)(2,1)S(1)}, bf16[80,3072]{1,0:T(8,128)(2,1)S(1)}, u32[]{:S(2)}, u32[]{:S(2)}) collective-permute-start(bf16[80,3072]{1,0:T(8,128)(2,1)S(1)} %pad_maximum_fusion.2), channel_id=1, source_target_pairs={{0,2},{1,7},{2,0},{3,5},{4,6},{5,3},{6,4},{7,1},{8,10},{9,15},{10,... | collective-permute-start | bytes 1474568 | tf_op jit(solution)/shard_map/ppermute | solution.py:231
  112.2 9.0 %collective-permute-start.21 = (bf16[192,384]{1,0:T(8,128)(2,1)S(1)}, bf16[192,384]{1,0:T(8,128)(2,1)S(1)}, u32[]{:S(2)}, u32[]{:S(2)}) collective-permute-start(bf16[192,384]{1,0:T(8,128)(2,1)S(1)} %broadcast_select_fusion.6), channel_id=1, source_target_pairs={{0,256},{1,257},{2,258},{3,259},{4,260},{5,261},{6,262},{7,263},{8... | collective-permute-start | bytes 442376 | tf_op jit(solution)/shard_map/ppermute | solution.py:231
  121.2 13.1 %collective-permute-start.22 = (bf16[160,3072]{1,0:T(8,128)(2,1)S(1)}, bf16[160,3072]{1,0:T(8,128)(2,1)S(1)}, u32[]{:S(2)}, u32[]{:S(2)}) collective-permute-start(bf16[160,3072]{1,0:T(8,128)(2,1)S(1)} %pad_maximum_fusion.1), channel_id=1, source_target_pairs={{0,1},{1,0},{2,3},{3,2},{4,5},{5,4},{6,7},{7,6},{8,9},{9,8},{10,11... | collective-permute-start | bytes 2949128 | tf_op jit(solution)/shard_map/ppermute | solution.py:231

commit v7 on v6

--- a/solution.py
+++ b/solution.py
@@ -312,7 +312,10 @@
     zero, one, two, three, four = jnp.split(terms, [depth, 2 * depth, 4 * depth, 6 * depth])
     got = swap(sent, by_core)
     rows = part.shape[0]
+    got_gain = lax.ppermute(after(ln_gain, terms), AXES, later)
     other = after(add(other, got[rows:]), terms)
+    other, got_gain = lax.optimization_barrier((other, got_gain))
+    ln_gain = jnp.where(first_core, ln_gain, got_gain)
     part = add(part, after(got, other)[:rows])
     got = swap(other, by_x(1))
     across = swap(four, by_z(-1))

time: 137 us -> 135 us (0.985)
  the two profiles are of different devices: /device:TPU:41 before, /device:TPU:1 now
where the time goes in v7:
time: 135 us; the launch traced here: 134 us
  starting transfers between devices  80.8 us (60%)
  waiting for transfers between devices  35.3 us (26%)
  Pallas kernels  8.53 us (6%)
  other arithmetic  4.53 us (3%)
  local copies, waits for them, and re-layouts  3.47 us (3%)
    ppermute x22, starting transfers between devices, swap(): return lax.ppermute(values, AXES, pairs_of(partner))  74.5 us
    ppermute x22, waiting for transfers between devices, swap(): return lax.ppermute(values, AXES, pairs_of(partner))  32.4 us
    pallas_call x1, Pallas kernels, run_head(): pl.pallas_call(head_kernel, out_shape=(like(tokens, width), like(tokens /...  4.58 us
    ppermute x1, starting transfers between devices, per_device(): got_gain = lax.ppermute(q_gain, AXES, later)  4.04 us
  transfers between devices with their start and end apart: 24, of which 15 were waited for; matrix products, arithmetic and copies ran while one was open for 3% of the time, Pallas kernels for 3%

profile of v7, /device:TPU:1, one launch (start us, length us, event | category | flops | bytes accessed | tf_op | source)
XLA Modules:
  0.0 133.8 jit_solution(485964995130719320)
XLA Ops:
  0.6 4.0 %collective-permute-start = (f32[128]{0:T(128)}, f32[128]{0:T(128)S(1)}, u32[]{:S(2)}, u32[]{:S(2)}) collective-permute-start(f32[128]{0:T(128)} %param.9), channel_id=1, source_target_pairs={{1,257},{3,259},{5,261},{7,263},{9,265},{11,267},{13,269},{15,271}... | collective-permute-start | bytes 1544 | tf_op jit(solution)/shard_map/ppermute | solution.py:300
  4.8 0.1 stack.27.places
  4.9 0.8 collective-permute-done
  5.7 3.4 %collective-permute-start.5 = (bf16[192,384]{1,0:T(8,128)(2,1)}, bf16[192,384]{1,0:T(8,128)(2,1)S(1)}, u32[]{:S(2)}, u32[]{:S(2)}) collective-permute-start(bf16[192,384]{1,0:T(8,128)(2,1)} %refs_0_), channel_id=1, source_target_pairs={{0,256},{1,257},{2,258},{3,259},{4,260},{5,261},{6,262},{7,263},{8... | collective-permute-start | bytes 442376 | tf_op jit(solution)/shard_map/ppermute | solution.py:231
  9.1 10.7 %collective-permute-start.1 = (bf16[192,384]{1,0:T(8,128)(2,1)}, bf16[192,384]{1,0:T(8,128)(2,1)S(1)}, u32[]{:S(2)}, u32[]{:S(2)}) collective-permute-start(bf16[192,384]{1,0:T(8,128)(2,1)} %refs_0_), channel_id=1, source_target_pairs={{0,32},{1,225},{2,34},{3,227},{4,36},{5,229},{6,38},{7,231},{8,40}... | collective-permute-start | bytes 442376 | tf_op jit(solution)/shard_map/ppermute | solution.py:231
  19.8 3.1 %collective-permute-start.6 = (bf16[192,384]{1,0:T(8,128)(2,1)S(1)}, bf16[192,384]{1,0:T(8,128)(2,1)S(1)}, u32[]{:S(2)}, u32[]{:S(2)}) collective-permute-start(bf16[192,384]{1,0:T(8,128)(2,1)S(1)} %collective-permute-done.5.refs_5_), channel_id=1, source_target_pairs={{0,32},{1,225},{2,34},{3,227},{4,36},{5,229},{6,38},{7,231},{8,40}... | collective-permute-start | bytes 442376 | tf_op jit(solution)/shard_map/ppermute | solution.py:231
  22.9 0.9 pad_maximum_fusion.3
  23.9 1.9 %collective-permute-start.2 = (bf16[384,384]{1,0:T(8,128)(2,1)S(1)}, bf16[384,384]{1,0:T(8,128)(2,1)S(1)}, u32[]{:S(2)}, u32[]{:S(2)}) collective-permute-start(bf16[384,384]{1,0:T(8,128)(2,1)S(1)} %pad_maximum_fusion.3), channel_id=1, source_target_pairs={{0,224},{1,33},{2,226},{3,35},{4,228},{5,37},{6,230},{7,39},{8,232... | collective-permute-start | bytes 884744 | tf_op jit(solution)/shard_map/ppermute | solution.py:231
  25.8 1.7 %collective-permute-done.6.refs_6_ = bf16[192,384]{1,0:T(8,128)(2,1)S(1)} collective-permute-done((bf16[192,384]{1,0:T(8,128)(2,1)S(1)}, bf16[192,384]{1,0:T(8,128)(2,1)S(1)}, u32[]{:S(2)}, u32[]{:S(2)}) %collective-permute-start.6) | collective-permute-done | bytes 147488 | tf_op jit(solution)/shard_map/ppermute | solution.py:231
  27.5 1.9 %collective-permute-start.7 = (bf16[384,384]{1,0:T(8,128)(2,1)S(1)}, bf16[384,384]{1,0:T(8,128)(2,1)S(1)}, u32[]{:S(2)}, u32[]{:S(2)}) collective-permute-start(bf16[384,384]{1,0:T(8,128)(2,1)S(1)} %pad_maximum_fusion.4), channel_id=1, source_target_pairs={{0,224},{1,33},{2,226},{3,35},{4,228},{5,37},{6,230},{7,39},{8,232... | collective-permute-start | bytes 884744 | tf_op jit(solution)/shard_map/ppermute | solution.py:231
  29.5 1.9 %collective-permute-done.2.refs_2_ = bf16[384,384]{1,0:T(8,128)(2,1)S(1)} collective-permute-done((bf16[384,384]{1,0:T(8,128)(2,1)S(1)}, bf16[384,384]{1,0:T(8,128)(2,1)S(1)}, u32[]{:S(2)}, u32[]{:S(2)}) %collective-permute-start.2) | collective-permute-done | bytes 294944 | tf_op jit(solution)/shard_map/ppermute | solution.py:231
  31.4 4.4 %collective-permute-start.3 = (bf16[384,384]{1,0:T(8,128)(2,1)S(1)}, bf16[384,384]{1,0:T(8,128)(2,1)S(1)}, u32[]{:S(2)}, u32[]{:S(2)}) collective-permute-start(bf16[384,384]{1,0:T(8,128)(2,1)S(1)} %collective-permute-done.2.refs_2_), channel_id=1, source_target_pairs={{0,32},{1,225},{2,34},{3,227},{4,36},{5,229},{6,38},{7,231},{8,40}... | collective-permute-start | bytes 884744 | tf_op jit(solution)/shard_map/ppermute | solution.py:231
  35.8 2.8 %collective-permute-start.8 = (bf16[384,384]{1,0:T(8,128)(2,1)S(1)}, bf16[384,384]{1,0:T(8,128)(2,1)S(1)}, u32[]{:S(2)}, u32[]{:S(2)}) collective-permute-start(bf16[384,384]{1,0:T(8,128)(2,1)S(1)} %collective-permute-done.7.refs_7_), channel_id=1, source_target_pairs={{0,32},{1,225},{2,34},{3,227},{4,36},{5,229},{6,38},{7,231},{8,40}... | collective-permute-start | bytes 884744 | tf_op jit(solution)/shard_map/ppermute | solution.py:231
  38.6 1.4 %collective-permute-done.3.refs_3_ = bf16[384,384]{1,0:T(8,128)(2,1)S(1)} collective-permute-done((bf16[384,384]{1,0:T(8,128)(2,1)S(1)}, bf16[384,384]{1,0:T(8,128)(2,1)S(1)}, u32[]{:S(2)}, u32[]{:S(2)}) %collective-permute-start.3) | collective-permute-done | bytes 294944 | tf_op jit(solution)/shard_map/ppermute | solution.py:231
  40.0 1.9 %collective-permute-start.4 = (bf16[384,384]{1,0:T(8,128)(2,1)S(1)}, bf16[384,384]{1,0:T(8,128)(2,1)S(1)}, u32[]{:S(2)}, u32[]{:S(2)}) collective-permute-start(bf16[384,384]{1,0:T(8,128)(2,1)S(1)} %collective-permute-done.3.refs_3_), channel_id=1, source_target_pairs={{0,224},{1,33},{2,226},{3,35},{4,228},{5,37},{6,230},{7,39},{8,232... | collective-permute-start | bytes 884744 | tf_op jit(solution)/shard_map/ppermute | solution.py:231
  41.9 2.5 %collective-permute-done.8.refs_8_ = bf16[384,384]{1,0:T(8,128)(2,1)S(1)} collective-permute-done((bf16[384,384]{1,0:T(8,128)(2,1)S(1)}, bf16[384,384]{1,0:T(8,128)(2,1)S(1)}, u32[]{:S(2)}, u32[]{:S(2)}) %collective-permute-start.8) | collective-permute-done | bytes 294944 | tf_op jit(solution)/shard_map/ppermute | solution.py:231
  44.5 1.9 %collective-permute-start.9 = (bf16[384,384]{1,0:T(8,128)(2,1)S(1)}, bf16[384,384]{1,0:T(8,128)(2,1)S(1)}, u32[]{:S(2)}, u32[]{:S(2)}) collective-permute-start(bf16[384,384]{1,0:T(8,128)(2,1)S(1)} %collective-permute-done.8.refs_8_), channel_id=1, source_target_pairs={{0,224},{1,33},{2,226},{3,35},{4,228},{5,37},{6,230},{7,39},{8,232... | collective-permute-start | bytes 884744 | tf_op jit(solution)/shard_map/ppermute | solution.py:231
  46.4 0.0 copy-start
  46.4 1.5 %copy-done = bf16[320,3072]{1,0:T(8,128)(2,1)S(1)} copy-done((bf16[320,3072]{1,0:T(8,128)(2,1)S(1)}, bf16[320,3072]{1,0:T(8,128)(2,1)}, u32[]{:S(2)}) %copy-start) | copy-done | bytes 1966104
  47.9 0.7 copy-done.3
  48.6 1.3 norm.1.normed
  50.0 2.2 %collective-permute-done.9.refs_9_ = bf16[384,384]{1,0:T(8,128)(2,1)S(1)} collective-permute-done((bf16[384,384]{1,0:T(8,128)(2,1)S(1)}, bf16[384,384]{1,0:T(8,128)(2,1)S(1)}, u32[]{:S(2)}, u32[]{:S(2)}) %collective-permute-start.9) | collective-permute-done | bytes 294944 | tf_op jit(solution)/shard_map/ppermute | solution.py:231
  52.2 4.6 %head.1 = (bf16[320,384]{1,0:T(8,128)(2,1)S(1)}, bf16[80,3072]{1,0:T(8,128)(2,1)S(1)}, bf16[80,3072]{1,0:T(8,128)(2,1)S(1)}, bf16[160,3072]{1,0:T(8,128)(2,1)S(1)}) custom-call(s32[6]{0:T(128)S(1)} %stack.27.places, bf16[320,3072]{1,0:T(8,128)(2,1)S(1)} %norm.1.normed, bf16[320,128]{1,0:T(8,128)(2,1)S(1)} %copy-done.2, f32[1,128]{1,0:T(1,128)S(1)} %fusion.q_gain, ...), custom_call_target="tpu_custom_call" | custom-call | flops 1132462080 | bytes 8388608 | tf_op jit(solution)/shard_map/head/pallas_call | solution.py:114
  56.8 3.7 %collective-permute-start.10 = (bf16[160,3072]{1,0:T(8,128)(2,1)S(1)}, bf16[160,3072]{1,0:T(8,128)(2,1)S(1)}, u32[]{:S(2)}, u32[]{:S(2)}) collective-permute-start(bf16[160,3072]{1,0:T(8,128)(2,1)S(1)} %get-tuple-element.36), channel_id=1, source_target_pairs={{0,1},{1,0},{2,3},{3,2},{4,5},{5,4},{6,7},{7,6},{8,9},{9,8},{10,11... | collective-permute-start | bytes 2949128 | tf_op jit(solution)/shard_map/ppermute | solution.py:231
  60.5 0.0 copy-start.4
  60.5 2.2 %terms.1 = bf16[3072,384]{1,0:T(8,128)(2,1)S(1)} custom-call(s32[6]{0:T(128)S(1)} %stack.27.places, bf16[320,3072]{1,0:T(8,128)(2,1)S(1)} %norm.1.normed, bf16[320,384]{1,0:T(8,128)(2,1)S(1)} %get-tuple-element.38.grads), custom_call_target="tpu_custom_call" | custom-call | flops 754974720 | bytes 5242880 | tf_op jit(solution)/shard_map/terms/pallas_call | solution.py:173
  62.7 2.2 %collective-permute-start.11 = (f32[3072]{0:T(1024)S(1)}, f32[3072]{0:T(1024)S(1)}, u32[]{:S(2)}, u32[]{:S(2)}) collective-permute-start(f32[3072]{0:T(1024)S(1)} %copy-done.4), channel_id=1, source_target_pairs={{1,257},{3,259},{5,261},{7,263},{9,265},{11,267},{13,269},{15,271}... | collective-permute-start | bytes 36872 | tf_op jit(solution)/shard_map/ppermute | solution.py:315
  64.9 0.1 add_convert_fusion.4
  65.0 2.1 %collective-permute-done.11 = f32[3072]{0:T(1024)S(1)} collective-permute-done((f32[3072]{0:T(1024)S(1)}, f32[3072]{0:T(1024)S(1)}, u32[]{:S(2)}, u32[]{:S(2)}) %collective-permute-start.11) | collective-permute-done | bytes 12320 | tf_op jit(solution)/shard_map/ppermute | solution.py:315
  67.2 4.4 %collective-permute-start.12 = (bf16[80,3072]{1,0:T(8,128)(2,1)S(1)}, bf16[80,3072]{1,0:T(8,128)(2,1)S(1)}, u32[]{:S(2)}, u32[]{:S(2)}) collective-permute-start(bf16[80,3072]{1,0:T(8,128)(2,1)S(1)} %add_convert_fusion.4), channel_id=1, source_target_pairs={{0,2},{1,7},{2,0},{3,5},{4,6},{5,3},{6,4},{7,1},{8,10},{9,15},{10,... | collective-permute-start | bytes 1474568 | tf_op jit(solution)/shard_map/ppermute | solution.py:231
  71.5 0.1 split.21
  71.6 1.9 %collective-permute-start.14 = (bf16[768,384]{1,0:T(8,128)(2,1)S(1)}, bf16[768,384]{1,0:T(8,128)(2,1)S(1)}, u32[]{:S(2)}, u32[]{:S(2)}) collective-permute-start(bf16[768,384]{1,0:T(8,128)(2,1)S(1)} %split.21), channel_id=1, source_target_pairs={{0,224},{1,33},{2,226},{3,35},{4,228},{5,37},{6,230},{7,39},{8,232... | collective-permute-start | bytes 1769480 | tf_op jit(solution)/shard_map/ppermute | solution.py:231
  73.5 4.7 %collective-permute-done.12 = bf16[80,3072]{1,0:T(8,128)(2,1)S(1)} collective-permute-done((bf16[80,3072]{1,0:T(8,128)(2,1)S(1)}, bf16[80,3072]{1,0:T(8,128)(2,1)S(1)}, u32[]{:S(2)}, u32[]{:S(2)}) %collective-permute-start.12) | collective-permute-done | bytes 491552 | tf_op jit(solution)/shard_map/ppermute | solution.py:231
  78.2 0.2 add_convert_fusion.2
  78.4 1.9 %collective-permute-start.13 = (bf16[40,3072]{1,0:T(8,128)(2,1)S(1)}, bf16[40,3072]{1,0:T(8,128)(2,1)S(1)}, u32[]{:S(2)}, u32[]{:S(2)}) collective-permute-start(bf16[40,3072]{1,0:T(8,128)(2,1)S(1)} %slice.34), channel_id=1, source_target_pairs={{0,6},{1,3},{2,4},{3,1},{4,2},{5,7},{6,0},{7,5},{8,14},{9,11},{10,... | collective-permute-start | bytes 737288 | tf_op jit(solution)/shard_map/ppermute | solution.py:231
  80.4 2.2 %collective-permute-done.14 = bf16[768,384]{1,0:T(8,128)(2,1)S(1)} collective-permute-done((bf16[768,384]{1,0:T(8,128)(2,1)S(1)}, bf16[768,384]{1,0:T(8,128)(2,1)S(1)}, u32[]{:S(2)}, u32[]{:S(2)}) %collective-permute-start.14) | collective-permute-done | bytes 589856 | tf_op jit(solution)/shard_map/ppermute | solution.py:231
  82.5 0.1 add_convert_fusion.1
  82.7 2.8 %collective-permute-start.16 = (bf16[768,384]{1,0:T(8,128)(2,1)S(1)}, bf16[768,384]{1,0:T(8,128)(2,1)S(1)}, u32[]{:S(2)}, u32[]{:S(2)}) collective-permute-start(bf16[768,384]{1,0:T(8,128)(2,1)S(1)} %add_convert_fusion.1), channel_id=1, source_target_pairs={{0,32},{1,225},{2,34},{3,227},{4,36},{5,229},{6,38},{7,231},{8,40}... | collective-permute-start | bytes 1769480 | tf_op jit(solution)/shard_map/ppermute | solution.py:231
  85.5 0.2 collective-permute-done.13
  85.7 0.1 add_convert_fusion.9
  85.7 5.2 %collective-permute-start.15 = (bf16[40,3072]{1,0:T(8,128)(2,1)S(1)}, bf16[40,3072]{1,0:T(8,128)(2,1)S(1)}, u32[]{:S(2)}, u32[]{:S(2)}) collective-permute-start(bf16[40,3072]{1,0:T(8,128)(2,1)S(1)} %add_convert_fusion.9), channel_id=1, source_target_pairs={{0,8},{1,25},{2,10},{3,27},{4,12},{5,29},{6,14},{7,31},{8,0},{9,17... | collective-permute-start | bytes 737288 | tf_op jit(solution)/shard_map/ppermute | solution.py:231
  90.9 3.7 %collective-permute-done.16 = bf16[768,384]{1,0:T(8,128)(2,1)S(1)} collective-permute-done((bf16[768,384]{1,0:T(8,128)(2,1)S(1)}, bf16[768,384]{1,0:T(8,128)(2,1)S(1)}, u32[]{:S(2)}, u32[]{:S(2)}) %collective-permute-start.16) | collective-permute-done | bytes 589856 | tf_op jit(solution)/shard_map/ppermute | solution.py:231
  94.7 0.1 add_convert_fusion
  94.8 1.9 %collective-permute-start.18 = (bf16[768,384]{1,0:T(8,128)(2,1)S(1)}, bf16[768,384]{1,0:T(8,128)(2,1)S(1)}, u32[]{:S(2)}, u32[]{:S(2)}) collective-permute-start(bf16[768,384]{1,0:T(8,128)(2,1)S(1)} %add_convert_fusion), channel_id=1, source_target_pairs={{0,224},{1,33},{2,226},{3,35},{4,228},{5,37},{6,230},{7,39},{8,232... | collective-permute-start | bytes 1769480 | tf_op jit(solution)/shard_map/ppermute | solution.py:231
  96.8 0.1 add_convert_fusion.8.left
  96.8 4.9 %collective-permute-start.17 = (bf16[40,3072]{1,0:T(8,128)(2,1)S(1)}, bf16[40,3072]{1,0:T(8,128)(2,1)S(1)}, u32[]{:S(2)}, u32[]{:S(2)}) collective-permute-start(bf16[40,3072]{1,0:T(8,128)(2,1)S(1)} %add_convert_fusion.8.left), channel_id=1, source_target_pairs={{0,24},{1,9},{2,26},{3,11},{4,28},{5,13},{6,30},{7,15},{8,16},{9,1... | collective-permute-start | bytes 737288 | tf_op jit(solution)/shard_map/ppermute | solution.py:231
  101.7 1.0 constant_dynamic-slice_fusion.inputs
  102.8 5.2 %collective-permute-done.17.right = bf16[40,3072]{1,0:T(8,128)(2,1)S(1)} collective-permute-done((bf16[40,3072]{1,0:T(8,128)(2,1)S(1)}, bf16[40,3072]{1,0:T(8,128)(2,1)S(1)}, u32[]{:S(2)}, u32[]{:S(2)}) %collective-permute-start.17) | collective-permute-done | bytes 245792 | tf_op jit(solution)/shard_map/ppermute | solution.py:231
  107.9 0.4 back.1
  108.4 0.1 add_convert_fusion.7
  108.5 1.9 %collective-permute-start.19 = (bf16[40,3072]{1,0:T(8,128)(2,1)S(1)}, bf16[40,3072]{1,0:T(8,128)(2,1)S(1)}, u32[]{:S(2)}, u32[]{:S(2)}) collective-permute-start(bf16[40,3072]{1,0:T(8,128)(2,1)S(1)} %back.1), channel_id=1, source_target_pairs={{0,6},{1,3},{2,4},{3,1},{4,2},{5,7},{6,0},{7,5},{8,14},{9,11},{10,... | collective-permute-start | bytes 737288 | tf_op jit(solution)/shard_map/ppermute | solution.py:231
  110.4 3.6 %collective-permute-start.21 = (bf16[384,384]{1,0:T(8,128)(2,1)S(1)}, bf16[384,384]{1,0:T(8,128)(2,1)S(1)}, u32[]{:S(2)}, u32[]{:S(2)}) collective-permute-start(bf16[384,384]{1,0:T(8,128)(2,1)S(1)} %add_convert_fusion.7), channel_id=1, source_target_pairs={{0,32},{1,225},{2,34},{3,227},{4,36},{5,229},{6,38},{7,231},{8,40}... | collective-permute-start | bytes 884744 | tf_op jit(solution)/shard_map/ppermute | solution.py:231
  114.0 1.7 %collective-permute-done.19 = bf16[40,3072]{1,0:T(8,128)(2,1)S(1)} collective-permute-done((bf16[40,3072]{1,0:T(8,128)(2,1)S(1)}, bf16[40,3072]{1,0:T(8,128)(2,1)S(1)}, u32[]{:S(2)}, u32[]{:S(2)}) %collective-permute-start.19) | collective-permute-done | bytes 245792 | tf_op jit(solution)/shard_map/ppermute | solution.py:231
  115.8 4.1 %collective-permute-start.20 = (bf16[80,3072]{1,0:T(8,128)(2,1)S(1)}, bf16[80,3072]{1,0:T(8,128)(2,1)S(1)}, u32[]{:S(2)}, u32[]{:S(2)}) collective-permute-start(bf16[80,3072]{1,0:T(8,128)(2,1)S(1)} %pad_maximum_fusion.2), channel_id=1, source_target_pairs={{0,2},{1,7},{2,0},{3,5},{4,6},{5,3},{6,4},{7,1},{8,10},{9,15},{10,... | collective-permute-start | bytes 1474568 | tf_op jit(solution)/shard_map/ppermute | solution.py:231
  119.9 0.1 add_convert_fusion.5
  120.0 2.9 %collective-permute-start.22 = (bf16[192,384]{1,0:T(8,128)(2,1)S(1)}, bf16[192,384]{1,0:T(8,128)(2,1)S(1)}, u32[]{:S(2)}, u32[]{:S(2)}) collective-permute-start(bf16[192,384]{1,0:T(8,128)(2,1)S(1)} %broadcast_select_fusion.6), channel_id=1, source_target_pairs={{0,256},{1,257},{2,258},{3,259},{4,260},{5,261},{6,262},{7,263},{8... | collective-permute-start | bytes 442376 | tf_op jit(solution)/shard_map/ppermute | solution.py:231
  122.9 3.6 %collective-permute-done.20 = bf16[80,3072]{1,0:T(8,128)(2,1)S(1)} collective-permute-done((bf16[80,3072]{1,0:T(8,128)(2,1)S(1)}, bf16[80,3072]{1,0:T(8,128)(2,1)S(1)}, u32[]{:S(2)}, u32[]{:S(2)}) %collective-permute-start.20) | collective-permute-done | bytes 491552 | tf_op jit(solution)/shard_map/ppermute | solution.py:231
  126.6 0.2 broadcast_select_fusion.3
  126.7 0.1 pad_maximum_fusion.1
  126.8 3.3 %collective-permute-start.23 = (bf16[160,3072]{1,0:T(8,128)(2,1)S(1)}, bf16[160,3072]{1,0:T(8,128)(2,1)S(1)}, u32[]{:S(2)}, u32[]{:S(2)}) collective-permute-start(bf16[160,3072]{1,0:T(8,128)(2,1)S(1)} %pad_maximum_fusion.1), channel_id=1, source_target_pairs={{0,1},{1,0},{2,3},{3,2},{4,5},{5,4},{6,7},{7,6},{8,9},{9,8},{10,11... | collective-permute-start | bytes 2949128 | tf_op jit(solution)/shard_map/ppermute | solution.py:231
  130.1 0.8 convert_add_fusion
  130.9 1.4 %collective-permute-done.23 = bf16[160,3072]{1,0:T(8,128)(2,1)S(1)} collective-permute-done((bf16[160,3072]{1,0:T(8,128)(2,1)S(1)}, bf16[160,3072]{1,0:T(8,128)(2,1)S(1)}, u32[]{:S(2)}, u32[]{:S(2)}) %collective-permute-start.23) | collective-permute-done | bytes 983072 | tf_op jit(solution)/shard_map/ppermute | solution.py:231
  132.3 0.1 broadcast_select_fusion.1
  132.4 1.4 %pad_maximum_fusion = bf16[320,3072]{1,0:T(8,128)(2,1)} fusion(bf16[160,3072]{1,0:T(8,128)(2,1)S(1)} %get-tuple-element.55, bf16[160,3072]{1,0:T(8,128)(2,1)S(1)} %get-tuple-element.54), kind=kLoop, calls=%fused_computation | loop fusion | flops 3932160 | bytes 3932160 | tf_op jit(solution)/shard_map/concatenate | solution.py:271
  (26 shorter events, 0.2 us)
Async XLA Ops:
  0.6 5.1 %collective-permute-start = (f32[128]{0:T(128)}, f32[128]{0:T(128)S(1)}, u32[]{:S(2)}, u32[]{:S(2)}) collective-permute-start(f32[128]{0:T(128)} %param.9), channel_id=1, source_target_pairs={{1,257},{3,259},{5,261},{7,263},{9,265},{11,267},{13,269},{15,271}... | collective-permute-start | bytes 1544 | tf_op jit(solution)/shard_map/ppermute | solution.py:300
  5.7 14.0 %collective-permute-start.5 = (bf16[192,384]{1,0:T(8,128)(2,1)}, bf16[192,384]{1,0:T(8,128)(2,1)S(1)}, u32[]{:S(2)}, u32[]{:S(2)}) collective-permute-start(bf16[192,384]{1,0:T(8,128)(2,1)} %refs_0_), channel_id=1, source_target_pairs={{0,256},{1,257},{2,258},{3,259},{4,260},{5,261},{6,262},{7,263},{8... | collective-permute-start | bytes 442376 | tf_op jit(solution)/shard_map/ppermute | solution.py:231
  9.1 13.8 %collective-permute-start.1 = (bf16[192,384]{1,0:T(8,128)(2,1)}, bf16[192,384]{1,0:T(8,128)(2,1)S(1)}, u32[]{:S(2)}, u32[]{:S(2)}) collective-permute-start(bf16[192,384]{1,0:T(8,128)(2,1)} %refs_0_), channel_id=1, source_target_pairs={{0,32},{1,225},{2,34},{3,227},{4,36},{5,229},{6,38},{7,231},{8,40}... | collective-permute-start | bytes 442376 | tf_op jit(solution)/shard_map/ppermute | solution.py:231
  19.8 7.7 %collective-permute-start.6 = (bf16[192,384]{1,0:T(8,128)(2,1)S(1)}, bf16[192,384]{1,0:T(8,128)(2,1)S(1)}, u32[]{:S(2)}, u32[]{:S(2)}) collective-permute-start(bf16[192,384]{1,0:T(8,128)(2,1)S(1)} %collective-permute-done.5.refs_5_), channel_id=1, source_target_pairs={{0,32},{1,225},{2,34},{3,227},{4,36},{5,229},{6,38},{7,231},{8,40}... | collective-permute-start | bytes 442376 | tf_op jit(solution)/shard_map/ppermute | solution.py:231
  23.9 7.5 %collective-permute-start.2 = (bf16[384,384]{1,0:T(8,128)(2,1)S(1)}, bf16[384,384]{1,0:T(8,128)(2,1)S(1)}, u32[]{:S(2)}, u32[]{:S(2)}) collective-permute-start(bf16[384,384]{1,0:T(8,128)(2,1)S(1)} %pad_maximum_fusion.3), channel_id=1, source_target_pairs={{0,224},{1,33},{2,226},{3,35},{4,228},{5,37},{6,230},{7,39},{8,232... | collective-permute-start | bytes 884744 | tf_op jit(solution)/shard_map/ppermute | solution.py:231
  27.5 8.2 %collective-permute-start.7 = (bf16[384,384]{1,0:T(8,128)(2,1)S(1)}, bf16[384,384]{1,0:T(8,128)(2,1)S(1)}, u32[]{:S(2)}, u32[]{:S(2)}) collective-permute-start(bf16[384,384]{1,0:T(8,128)(2,1)S(1)} %pad_maximum_fusion.4), channel_id=1, source_target_pairs={{0,224},{1,33},{2,226},{3,35},{4,228},{5,37},{6,230},{7,39},{8,232... | collective-permute-start | bytes 884744 | tf_op jit(solution)/shard_map/ppermute | solution.py:231
  31.4 8.7 %collective-permute-start.3 = (bf16[384,384]{1,0:T(8,128)(2,1)S(1)}, bf16[384,384]{1,0:T(8,128)(2,1)S(1)}, u32[]{:S(2)}, u32[]{:S(2)}) collective-permute-start(bf16[384,384]{1,0:T(8,128)(2,1)S(1)} %collective-permute-done.2.refs_2_), channel_id=1, source_target_pairs={{0,32},{1,225},{2,34},{3,227},{4,36},{5,229},{6,38},{7,231},{8,40}... | collective-permute-start | bytes 884744 | tf_op jit(solution)/shard_map/ppermute | solution.py:231
  35.8 8.7 %collective-permute-start.8 = (bf16[384,384]{1,0:T(8,128)(2,1)S(1)}, bf16[384,384]{1,0:T(8,128)(2,1)S(1)}, u32[]{:S(2)}, u32[]{:S(2)}) collective-permute-start(bf16[384,384]{1,0:T(8,128)(2,1)S(1)} %collective-permute-done.7.refs_7_), channel_id=1, source_target_pairs={{0,32},{1,225},{2,34},{3,227},{4,36},{5,229},{6,38},{7,231},{8,40}... | collective-permute-start | bytes 884744 | tf_op jit(solution)/shard_map/ppermute | solution.py:231
  40.0 9.9 %collective-permute-start.4 = (bf16[384,384]{1,0:T(8,128)(2,1)S(1)}, bf16[384,384]{1,0:T(8,128)(2,1)S(1)}, u32[]{:S(2)}, u32[]{:S(2)}) collective-permute-start(bf16[384,384]{1,0:T(8,128)(2,1)S(1)} %collective-permute-done.3.refs_3_), channel_id=1, source_target_pairs={{0,224},{1,33},{2,226},{3,35},{4,228},{5,37},{6,230},{7,39},{8,232... | collective-permute-start | bytes 884744 | tf_op jit(solution)/shard_map/ppermute | solution.py:231
  44.5 7.8 %collective-permute-start.9 = (bf16[384,384]{1,0:T(8,128)(2,1)S(1)}, bf16[384,384]{1,0:T(8,128)(2,1)S(1)}, u32[]{:S(2)}, u32[]{:S(2)}) collective-permute-start(bf16[384,384]{1,0:T(8,128)(2,1)S(1)} %collective-permute-done.8.refs_8_), channel_id=1, source_target_pairs={{0,224},{1,33},{2,226},{3,35},{4,228},{5,37},{6,230},{7,39},{8,232... | collective-permute-start | bytes 884744 | tf_op jit(solution)/shard_map/ppermute | solution.py:231
  46.4 1.5 %copy-start = (bf16[320,3072]{1,0:T(8,128)(2,1)S(1)}, bf16[320,3072]{1,0:T(8,128)(2,1)}, u32[]{:S(2)}) copy-start(bf16[320,3072]{1,0:T(8,128)(2,1)} %inputs.1) | copy-start | bytes 5898244
  47.9 0.7 copy-start.3
  48.6 1.3 copy-start.6
  48.6 3.6 %copy-start.1 = (bf16[192,384]{1,0:T(8,128)(2,1)S(1)}, bf16[192,384]{1,0:T(8,128)(2,1)}, u32[]{:S(2)}) copy-start(bf16[192,384]{1,0:T(8,128)(2,1)} %refs_0_) | copy-start | bytes 442372
  48.6 3.6 %copy-start.2 = (bf16[320,128]{1,0:T(8,128)(2,1)S(1)}, bf16[320,128]{1,0:T(8,128)(2,1)}, u32[]{:S(2)}) copy-start(bf16[320,128]{1,0:T(8,128)(2,1)} %cot.1) | copy-start | bytes 245764
  48.6 3.6 %copy-start.5 = (f32[128]{0:T(128)S(1)}, f32[128]{0:T(128)}, u32[]{:S(2)}) copy-start(f32[128]{0:T(128)} %param.10) | copy-start | bytes 1540
  56.8 8.1 %collective-permute-start.10 = (bf16[160,3072]{1,0:T(8,128)(2,1)S(1)}, bf16[160,3072]{1,0:T(8,128)(2,1)S(1)}, u32[]{:S(2)}, u32[]{:S(2)}) collective-permute-start(bf16[160,3072]{1,0:T(8,128)(2,1)S(1)} %get-tuple-element.36), channel_id=1, source_target_pairs={{0,1},{1,0},{2,3},{3,2},{4,5},{5,4},{6,7},{7,6},{8,9},{9,8},{10,11... | collective-permute-start | bytes 2949128 | tf_op jit(solution)/shard_map/ppermute | solution.py:231
  60.5 2.2 %copy-start.4 = (f32[3072]{0:T(1024)S(1)}, f32[3072]{0:T(1024)}, u32[]{:S(2)}) copy-start(f32[3072]{0:T(1024)} %param.7) | copy-start | bytes 36868
  62.7 4.4 %collective-permute-start.11 = (f32[3072]{0:T(1024)S(1)}, f32[3072]{0:T(1024)S(1)}, u32[]{:S(2)}, u32[]{:S(2)}) collective-permute-start(f32[3072]{0:T(1024)S(1)} %copy-done.4), channel_id=1, source_target_pairs={{1,257},{3,259},{5,261},{7,263},{9,265},{11,267},{13,269},{15,271}... | collective-permute-start | bytes 36872 | tf_op jit(solution)/shard_map/ppermute | solution.py:315
  67.2 11.1 %collective-permute-start.12 = (bf16[80,3072]{1,0:T(8,128)(2,1)S(1)}, bf16[80,3072]{1,0:T(8,128)(2,1)S(1)}, u32[]{:S(2)}, u32[]{:S(2)}) collective-permute-start(bf16[80,3072]{1,0:T(8,128)(2,1)S(1)} %add_convert_fusion.4), channel_id=1, source_target_pairs={{0,2},{1,7},{2,0},{3,5},{4,6},{5,3},{6,4},{7,1},{8,10},{9,15},{10,... | collective-permute-start | bytes 1474568 | tf_op jit(solution)/shard_map/ppermute | solution.py:231
  71.6 10.9 %collective-permute-start.14 = (bf16[768,384]{1,0:T(8,128)(2,1)S(1)}, bf16[768,384]{1,0:T(8,128)(2,1)S(1)}, u32[]{:S(2)}, u32[]{:S(2)}) collective-permute-start(bf16[768,384]{1,0:T(8,128)(2,1)S(1)} %split.21), channel_id=1, source_target_pairs={{0,224},{1,33},{2,226},{3,35},{4,228},{5,37},{6,230},{7,39},{8,232... | collective-permute-start | bytes 1769480 | tf_op jit(solution)/shard_map/ppermute | solution.py:231
  78.4 7.2 %collective-permute-start.13 = (bf16[40,3072]{1,0:T(8,128)(2,1)S(1)}, bf16[40,3072]{1,0:T(8,128)(2,1)S(1)}, u32[]{:S(2)}, u32[]{:S(2)}) collective-permute-start(bf16[40,3072]{1,0:T(8,128)(2,1)S(1)} %slice.34), channel_id=1, source_target_pairs={{0,6},{1,3},{2,4},{3,1},{4,2},{5,7},{6,0},{7,5},{8,14},{9,11},{10,... | collective-permute-start | bytes 737288 | tf_op jit(solution)/shard_map/ppermute | solution.py:231
  82.7 12.0 %collective-permute-start.16 = (bf16[768,384]{1,0:T(8,128)(2,1)S(1)}, bf16[768,384]{1,0:T(8,128)(2,1)S(1)}, u32[]{:S(2)}, u32[]{:S(2)}) collective-permute-start(bf16[768,384]{1,0:T(8,128)(2,1)S(1)} %add_convert_fusion.1), channel_id=1, source_target_pairs={{0,32},{1,225},{2,34},{3,227},{4,36},{5,229},{6,38},{7,231},{8,40}... | collective-permute-start | bytes 1769480 | tf_op jit(solution)/shard_map/ppermute | solution.py:231
  85.7 11.0 %collective-permute-start.15 = (bf16[40,3072]{1,0:T(8,128)(2,1)S(1)}, bf16[40,3072]{1,0:T(8,128)(2,1)S(1)}, u32[]{:S(2)}, u32[]{:S(2)}) collective-permute-start(bf16[40,3072]{1,0:T(8,128)(2,1)S(1)} %add_convert_fusion.9), channel_id=1, source_target_pairs={{0,8},{1,25},{2,10},{3,27},{4,12},{5,29},{6,14},{7,31},{8,0},{9,17... | collective-permute-start | bytes 737288 | tf_op jit(solution)/shard_map/ppermute | solution.py:231
  94.8 13.6 %collective-permute-start.18 = (bf16[768,384]{1,0:T(8,128)(2,1)S(1)}, bf16[768,384]{1,0:T(8,128)(2,1)S(1)}, u32[]{:S(2)}, u32[]{:S(2)}) collective-permute-start(bf16[768,384]{1,0:T(8,128)(2,1)S(1)} %add_convert_fusion), channel_id=1, source_target_pairs={{0,224},{1,33},{2,226},{3,35},{4,228},{5,37},{6,230},{7,39},{8,232... | collective-permute-start | bytes 1769480 | tf_op jit(solution)/shard_map/ppermute | solution.py:231
  96.8 11.1 %collective-permute-start.17 = (bf16[40,3072]{1,0:T(8,128)(2,1)S(1)}, bf16[40,3072]{1,0:T(8,128)(2,1)S(1)}, u32[]{:S(2)}, u32[]{:S(2)}) collective-permute-start(bf16[40,3072]{1,0:T(8,128)(2,1)S(1)} %add_convert_fusion.8.left), channel_id=1, source_target_pairs={{0,24},{1,9},{2,26},{3,11},{4,28},{5,13},{6,30},{7,15},{8,16},{9,1... | collective-permute-start | bytes 737288 | tf_op jit(solution)/shard_map/ppermute | solution.py:231
  108.5 7.2 %collective-permute-start.19 = (bf16[40,3072]{1,0:T(8,128)(2,1)S(1)}, bf16[40,3072]{1,0:T(8,128)(2,1)S(1)}, u32[]{:S(2)}, u32[]{:S(2)}) collective-permute-start(bf16[40,3072]{1,0:T(8,128)(2,1)S(1)} %back.1), channel_id=1, source_target_pairs={{0,6},{1,3},{2,4},{3,1},{4,2},{5,7},{6,0},{7,5},{8,14},{9,11},{10,... | collective-permute-start | bytes 737288 | tf_op jit(solution)/shard_map/ppermute | solution.py:231
  110.4 9.5 %collective-permute-start.21 = (bf16[384,384]{1,0:T(8,128)(2,1)S(1)}, bf16[384,384]{1,0:T(8,128)(2,1)S(1)}, u32[]{:S(2)}, u32[]{:S(2)}) collective-permute-start(bf16[384,384]{1,0:T(8,128)(2,1)S(1)} %add_convert_fusion.7), channel_id=1, source_target_pairs={{0,32},{1,225},{2,34},{3,227},{4,36},{5,229},{6,38},{7,231},{8,40}... | collective-permute-start | bytes 884744 | tf_op jit(solution)/shard_map/ppermute | solution.py:231
  115.8 10.8 %collective-permute-start.20 = (bf16[80,3072]{1,0:T(8,128)(2,1)S(1)}, bf16[80,3072]{1,0:T(8,128)(2,1)S(1)}, u32[]{:S(2)}, u32[]{:S(2)}) collective-permute-start(bf16[80,3072]{1,0:T(8,128)(2,1)S(1)} %pad_maximum_fusion.2), channel_id=1, source_target_pairs={{0,2},{1,7},{2,0},{3,5},{4,6},{5,3},{6,4},{7,1},{8,10},{9,15},{10,... | collective-permute-start | bytes 1474568 | tf_op jit(solution)/shard_map/ppermute | solution.py:231
  120.0 6.8 %collective-permute-start.22 = (bf16[192,384]{1,0:T(8,128)(2,1)S(1)}, bf16[192,384]{1,0:T(8,128)(2,1)S(1)}, u32[]{:S(2)}, u32[]{:S(2)}) collective-permute-start(bf16[192,384]{1,0:T(8,128)(2,1)S(1)} %broadcast_select_fusion.6), channel_id=1, source_target_pairs={{0,256},{1,257},{2,258},{3,259},{4,260},{5,261},{6,262},{7,263},{8... | collective-permute-start | bytes 442376 | tf_op jit(solution)/shard_map/ppermute | solution.py:231
  126.8 5.5 %collective-permute-start.23 = (bf16[160,3072]{1,0:T(8,128)(2,1)S(1)}, bf16[160,3072]{1,0:T(8,128)(2,1)S(1)}, u32[]{:S(2)}, u32[]{:S(2)}) collective-permute-start(bf16[160,3072]{1,0:T(8,128)(2,1)S(1)} %pad_maximum_fusion.1), channel_id=1, source_target_pairs={{0,1},{1,0},{2,3},{3,2},{4,5},{5,4},{6,7},{7,6},{8,9},{9,8},{10,11... | collective-permute-start | bytes 2949128 | tf_op jit(solution)/shard_map/ppermute | solution.py:231
